TPU v7x, 32 devices: a whole 2x2x4 slice. The times are simulated.
32 devices in a mesh: leaf: 16 (over z, y, x), sub: 2 (over core).
Axes of the slice: x: 2, y: 2, z: 4, core: 2. Of those that a mesh axis runs over, the one named last changes fastest.
Arguments:
- density: bfloat16 [128, 256, 32], P('leaf', None, 'sub'), may hold values from -6 to 6
- near_blocks: bfloat16 [128, 6, 256, 256], P('leaf', 'sub'), may hold values from -0.15625 to 0.15625
- near_index: int32 [128, 6], P('leaf', 'sub'), may hold values from 0 to 127, as said below
- col_basis: bfloat16 [128, 256, 64], P('leaf'), may hold values from -0.375 to 0.375
- row_basis: bfloat16 [128, 256, 64], P('leaf'), may hold values from -0.75 to 0.75
- leaf_coupling: bfloat16 [128, 6, 64, 64], P('leaf', 'sub'), may hold values from -0.3125 to 0.3125
- leaf_list: int32 [128, 6], P('leaf', 'sub'), may hold values from 0 to 127, as said below
- leaf_up: bfloat16 [128, 64, 64], P('leaf'), may hold values from -0.25 to 0.25
- leaf_down: bfloat16 [128, 64, 64], P('leaf'), may hold values from -0.75 to 0.75
- node_coupling: bfloat16 [16, 4, 64, 64], P('leaf'), may hold values from -0.375 to 0.375
- node_list: int32 [16, 4], P('leaf'), may hold values from 0 to 15, as said below
- node_up: bfloat16 [16, 64, 64], P('leaf'), may hold values from -0.5 to 0.5
- node_down: bfloat16 [16, 64, 64], P('leaf'), may hold values from -0.75 to 0.75
- upper_coupling: bfloat16 [14, 4, 64, 64], replicated, may hold values from -0.375 to 0.375
- upper_list: int32 [14, 4], replicated, may hold values from 2 to 15, as said below
- upper_up: bfloat16 [12, 64, 64], replicated, may hold values from -0.5 to 0.5
- upper_down: bfloat16 [12, 64, 64], replicated, may hold values from -0.75 to 0.75
Outputs:
- potential: bfloat16 [128, 256, 32], P('leaf', None, 'sub')
Inputs may be any that keep to these rules, and one draw needn't show every extreme that they name: `near_index`: row t holds 6 different leaves, the first being t itself; all lie among the leaves of t's own block of 8 and of the blocks just before and after it; none stands in row t of leaf_list. `leaf_list`: row t holds 6 different leaves other than t, all among the leaves of t's own block of 8 and of the blocks just before and after it. `node_list`: row d holds 4 different clusters other than d; the first is (d + 8) mod 16. `upper_list`: row n - 2 names nodes of node n's level other than n, possibly repeated; the first is the node half that level's size away.
All inputs are finite; a program needn't handle non-finite values.
Results may differ from a plain program's by a relative error of at most 0.029.
Values may be sent and summed in bfloat16 or wider, within the bound.
No kernel may reach another device: no remote copies, remote signals or barrier semaphores. Data moves between devices by JAX's collectives and lax.ppermute only.
A program may use at most 128 MiB of HBM per device.

v0:
```python
import jax
import jax.numpy as jnp
from jax import lax
from jax.sharding import PartitionSpec as P


def extended_2(block, sides, width):
    for axis, dim in sides:
        count = lax.axis_size(axis)
        forward = [(i, i + 1) for i in range(count - 1)]
        backward = [(target, source) for source, target in forward]
        low = lax.ppermute(
            lax.slice_in_dim(block, block.shape[dim] - width, None, axis=dim), axis, forward
        )
        high = lax.ppermute(lax.slice_in_dim(block, 0, width, axis=dim), axis, backward)
        block = jnp.concatenate([low, block, high], axis=dim)
    return block


def upper_tree(raised_coefficients, upper_coupling, upper_list, upper_up, upper_down, node_count):
    levels = node_count.bit_length() - 1
    rank_size = raised_coefficients.shape[1]
    columns = raised_coefficients.shape[2]
    coeffs = {}
    summed = (
        raised_coefficients.astype(jnp.float32)
        .reshape(node_count // 2, 2, rank_size, columns)
        .sum(axis=1)
    )
    coeffs[levels - 1] = summed.astype(jnp.bfloat16)
    for height in range(levels - 2, 0, -1):
        lower_size = 2 ** (height + 1)
        matrices = upper_up[lower_size - 4 : 2 * lower_size - 4]
        shifted = jnp.einsum(
            "nrs,nrc->nsc", matrices, coeffs[height + 1], preferred_element_type=jnp.float32
        )
        coeffs[height] = (
            shifted.reshape(lower_size // 2, 2, rank_size, columns).sum(axis=1).astype(jnp.bfloat16)
        )
    answer = None
    for height in range(1, levels):
        breadth = 2**height
        listed = upper_list[breadth - 2 : 2 * breadth - 2] - breadth
        sources = coeffs[height][listed]
        coupled = jnp.einsum(
            "nfrs,nfsc->nrc",
            upper_coupling[breadth - 2 : 2 * breadth - 2],
            sources,
            preferred_element_type=jnp.float32,
        )
        if height > 1:
            parents = jnp.repeat(answer, 2, axis=0)
            coupled = coupled + jnp.einsum(
                "nrs,nsc->nrc",
                upper_down[breadth - 4 : 2 * breadth - 4],
                parents,
                preferred_element_type=jnp.float32,
            )
        answer = coupled.astype(jnp.bfloat16)
    return answer


def body(
    density,
    near_blocks,
    near_index,
    col_basis,
    row_basis,
    leaf_coupling,
    leaf_list,
    leaf_up,
    leaf_down,
    node_coupling,
    node_list,
    node_up,
    node_down,
    upper_coupling,
    upper_list,
    upper_up,
    upper_down,
):
    leaf_count = density.shape[0]
    half_cols = density.shape[2]
    device = lax.axis_index("leaf")
    core_index = lax.axis_index("sub")
    node_count = lax.axis_size("leaf")
    charge_input = lax.all_gather(density, "sub", axis=2, tiled=True)
    block_entries, couplings = (near_blocks, leaf_coupling)
    near_cols, far_cols = (near_index, leaf_list)
    extended = extended_2(charge_input, (("leaf", 0),), leaf_count)
    offset = device * leaf_count - leaf_count
    leaf_coeff = jnp.einsum(
        "tlr,tlc->trc", col_basis, charge_input, preferred_element_type=jnp.float32
    ).astype(jnp.bfloat16)
    coeff_ext = extended_2(leaf_coeff, (("leaf", 0),), leaf_count)
    selected_nodes = extended[near_cols - offset]
    proximate_portion = jnp.einsum(
        "vpqx,vpxn->vqn", block_entries, selected_nodes, preferred_element_type=jnp.float32
    )
    far_sources = coeff_ext[far_cols - offset]
    far_part = jnp.einsum(
        "tjrs,tjsc->trc", couplings, far_sources, preferred_element_type=jnp.float32
    )
    proximate_field, far_field = (
        lax.psum_scatter(
            proximate_portion.astype(jnp.bfloat16), "sub", scatter_dimension=2, tiled=True
        ).astype(jnp.float32),
        lax.psum_scatter(
            far_part.astype(jnp.bfloat16), "sub", scatter_dimension=2, tiled=True
        ).astype(jnp.float32),
    )
    own_coeff = lax.dynamic_slice_in_dim(leaf_coeff, core_index * half_cols, half_cols, 2)
    node_coeff = jnp.einsum(
        "trs,trc->sc", leaf_up, own_coeff, preferred_element_type=jnp.float32
    ).astype(jnp.bfloat16)
    raised_coefficients = jnp.einsum(
        "rs,rc->sc", node_up[0], node_coeff, preferred_element_type=jnp.float32
    ).astype(jnp.bfloat16)
    all_coeff, all_lifted = (
        lax.all_gather(node_coeff[None], "leaf", axis=0, tiled=True),
        lax.all_gather(raised_coefficients[None], "leaf", axis=0, tiled=True),
    )
    answer = upper_tree(all_lifted, upper_coupling, upper_list, upper_up, upper_down, node_count)
    parent_field = lax.dynamic_index_in_dim(answer, device // 2, 0, keepdims=False)
    node_term = jnp.einsum(
        "frs,fsc->rc", node_coupling[0], all_coeff[node_list[0]], preferred_element_type=jnp.float32
    )
    node_term = node_term + jnp.dot(node_down[0], parent_field, preferred_element_type=jnp.float32)
    node_field = node_term.astype(jnp.bfloat16)
    descended = jnp.einsum("trs,sc->trc", leaf_down, node_field, preferred_element_type=jnp.float32)
    leaf_field = (far_field + descended).astype(jnp.bfloat16)
    farther = jnp.einsum("tlr,trc->tlc", row_basis, leaf_field, preferred_element_type=jnp.float32)
    return (proximate_field + farther).astype(jnp.bfloat16)


def solution(mesh):
    placed = (
        P("leaf", None, "sub"),
        P("leaf", "sub", None, None),
        P("leaf", "sub"),
        P("leaf", None, None),
        P("leaf", None, None),
        P("leaf", "sub", None, None),
        P("leaf", "sub"),
        P("leaf", None, None),
        P("leaf", None, None),
        P("leaf", None, None, None),
        P("leaf", None),
        P("leaf", None, None),
        P("leaf", None, None),
        P(),
        P(),
        P(),
        P(),
    )
    return jax.shard_map(
        body, mesh=mesh, in_specs=placed, out_specs=P("leaf", None, "sub"), check_vma=False
    )
```

profile of v0, /device:TPU:0, one launch (start us, length us, event | category | flops | bytes accessed | tf_op | source)
XLA Modules:
  0.0 144.8 jit_solution(12733212745727232211)
XLA Ops:
  6.5 0.0 copy-start
  6.5 0.0 reduce-scatter.5.cloned.1.call-start
  6.5 2.5 %all_gather.9 = bf16[8,256,32]{1,2,0:T(8,128)(2,1)S(1)} all-gather(bf16[8,256,16]{1,2,0:T(8,128)(2,1)} %param.17), channel_id=1, replica_groups=mesh['leaf'=16,'sub'=2] {'sub'}, dimensions={2}, use_global_device_ids=true | all-gather | bytes 196608 | tf_op jit(solution)/shard_map/all_gather | solution.py:87
  9.1 1.1 convolution_convert_fusion
  10.2 0.0 copy-start.1
  10.2 1.3 collective-permute-start.3
  11.5 6.0 %collective-permute-start.2 = (bf16[8,64,32]{1,2,0:T(8,128)(2,1)S(1)}, bf16[8,64,32]{1,2,0:T(8,128)(2,1)}, u32[]{:S(2)}, u32[]{:S(2)}) collective-permute-start(bf16[8,64,32]{1,2,0:T(8,128)(2,1)S(1)} %convolution_convert_fusion), channel_id=1, source_target_pairs={{0,2},{2,4},{4,6},{6,8},{8,10},{10,12},{12,14},{14,16},{16,18},{18... | collective-permute-start | bytes 98312 | tf_op jit(solution)/shard_map/ppermute | solution.py:12
  17.5 1.3 collective-permute-start.1
  18.8 5.5 %collective-permute-start = (bf16[8,256,32]{1,2,0:T(8,128)(2,1)S(1)}, bf16[8,256,32]{1,2,0:T(8,128)(2,1)}, u32[]{:S(2)}, u32[]{:S(2)}) collective-permute-start(bf16[8,256,32]{1,2,0:T(8,128)(2,1)S(1)} %all_gather.9), channel_id=1, source_target_pairs={{0,2},{2,4},{4,6},{6,8},{8,10},{10,12},{12,14},{14,16},{16,18},{18... | collective-permute-start | bytes 393224 | tf_op jit(solution)/shard_map/ppermute | solution.py:12
  24.3 0.8 compare_select_fusion.2
  25.0 0.7 compare_select_fusion
  25.7 0.8 compare_select_fusion.1
  26.5 0.7 fusion.36
  27.1 0.1 copy.32
  27.2 0.1 reshape.94
  27.3 0.1 copy.31
  27.4 0.1 reshape.86
  27.5 0.7 compare_select_fusion.3
  28.2 0.1 copy.29
  28.3 0.1 reshape.62
  28.4 0.1 copy.28
  28.5 0.1 reshape.54
  28.6 1.1 fusion.12
  29.7 0.8 fusion.14
  30.5 39.4 %all-gather.3 = bf16[16,64,16]{1,2,0:T(8,128)(2,1)S(1)} all-gather(bf16[1,64,16]{1,2,0:T(8,128)(2,1)S(1)} %fusion.14), channel_id=3, replica_groups=mesh['leaf'=16,'sub'=2] {'leaf'}, dimensions={0}, use_global_device_ids=true | all-gather | bytes 34816 | tf_op jit(solution)/shard_map/all_gather | solution.py:121
  69.9 1.0 bitcast_reduce_fusion
  71.0 1.0 bitcast_reduce_fusion.2
  71.9 0.6 gather_fusion.4
  72.5 0.6 gather_fusion.5
  73.1 1.0 fusion.11
  74.1 1.1 convolution_bitcast_fusion.5
  75.3 1.0 fusion.9
  76.3 1.7 %fusion.18 = f32[8,16,64]{2,1,0:T(8,128)} fusion(bf16[8,64,16]{1,2,0:T(8,128)(2,1)S(1)} %bitcast.123, bf16[12,64,64]{2,1,0:T(8,128)(2,1)} %param.33), kind=kOutput, calls=%fused_computation.39 | convolution fusion | flops 1048576 | bytes 180224 | tf_op jit(solution)/shard_map/nrs,nsc->nrc/dot_general | solution.py:53
  78.0 35.8 %all-gather.2 = bf16[16,64,16]{1,2,0:T(8,128)(2,1)S(1)} all-gather(bf16[1,64,16]{1,2,0:T(8,128)(2,1)S(1)} %bitcast.125), channel_id=2, replica_groups=mesh['leaf'=16,'sub'=2] {'leaf'}, dimensions={0}, use_global_device_ids=true | all-gather | bytes 34816 | tf_op jit(solution)/shard_map/all_gather | solution.py:120
  113.8 0.6 gather_fusion.2
  114.4 1.0 convolution_bitcast_fusion.7
  115.3 0.1 copy.30
  115.4 0.1 reshape.78
  115.5 0.0 collective-permute-done.3
  115.5 0.0 copy-done.1
  115.5 0.0 collective-permute-done.2
  115.5 1.0 pad_maximum_fusion.1
  116.5 1.2 gather_fusion.1
  117.7 2.0 %fusion.6 = bf16[8,64,32]{1,2,0:T(8,128)(2,1)} fusion(bf16[8,3,64,32]{2,3,1,0:T(8,128)(2,1)} %bitcast.120, bf16[8,3,64,64]{3,2,1,0:T(8,128)(2,1)} %param.22), kind=kOutput, calls=%fused_computation.18 | convolution fusion | flops 6307840 | bytes 327680 | tf_op jit(solution)/shard_map/tjrs,tjsc->trc/dot_general | solution.py:101
  119.7 0.0 reduce-scatter.5.cloned.1.call-update
  119.7 0.0 reduce-scatter.3.cloned.1.call-start
  119.8 0.0 collective-permute-done.1
  119.8 0.0 collective-permute-done
  119.8 1.7 %pad_maximum_fusion = bf16[24,256,32]{1,2,0:T(8,128)(2,1)} fusion(bf16[8,256,32]{1,2,0:T(8,128)(2,1)} %collective-permute-done.1, bf16[8,256,32]{1,2,0:T(8,128)(2,1)S(1)} %all_gather.9, bf16[8,256,32]{1,2,0:T(8,128)(2,1)} %collective-permute-done), kind=kLoop, calls=%fused_computation.36 | loop fusion | flops 393216 | bytes 786432 | tf_op jit(solution)/shard_map/concatenate | solution.py:16
  121.6 2.3 %gather_fusion = bf16[24,256,32]{1,2,0:T(8,128)(2,1)} fusion(bf16[24,256,32]{1,2,0:T(8,128)(2,1)} %pad_maximum_fusion, s32[1024]{0:T(1024)S(1)} %pad_clamp_fusion.5), kind=kCustom, calls=%fused_computation | custom fusion | bytes 786528 | tf_op jit(solution)/shard_map/gather | solution.py:96
  123.9 0.0 copy-start.3
  123.9 0.0 copy-start.2
  123.9 0.0 copy-done
  123.9 2.7 %fusion.2 = bf16[8,256,32]{1,2,0:T(8,128)(2,1)} fusion(bf16[8,3,256,32]{2,3,1,0:T(8,128)(2,1)} %bitcast.118, bf16[8,3,256,256]{3,2,1,0:T(8,128)(2,1)S(1)} %copy-done), kind=kOutput, calls=%fused_computation.11 | convolution fusion | flops 100728832 | bytes 3670016 | tf_op jit(solution)/shard_map/vpqx,vpxn->vqn/dot_general | solution.py:97
  126.6 0.0 reduce-scatter.3.cloned.1.call-update
  126.6 0.6 gather_fusion.3
  127.2 1.3 convolution_bitcast_fusion.4
  128.5 0.0 copy-done.3
  128.5 0.8 fusion.15
  129.4 0.0 reduce-scatter.5.cloned.1.call-done
  129.4 6.7 %reduce-scatter.3.cloned.1.call-done = bf16[8,256,16]{1,2,0:T(8,128)(2,1)} async-done(((bf16[8,256,32]{1,2,0:T(8,128)(2,1)}), bf16[8,256,16]{1,2,0:T(8,128)(2,1)}) %reduce-scatter.3.cloned.1.call-update) | async-done | bytes 65552 | tf_op jit(solution)/shard_map/reduce_scatter | solution.py:105
  136.0 0.0 copy-done.2
  136.0 1.9 %fusion.3 = bf16[8,256,16]{1,2,0:T(8,128)(2,1)} fusion(bf16[8,256,64]{1,2,0:T(8,128)(2,1)} %param.21, bf16[16,64,1]{1,0,2:T(8,128)(2,1)S(1)} %fusion.15, bf16[8,64,64]{2,1,0:T(8,128)(2,1)S(1)} %copy-done.2, bf16[8,256,16]{1,2,0:T(8,128)(2,1)} %reduce-scatter.3.cloned.1.call-done, bf16[8,64,16]{1,2,0:T(8,128)(2,1)} %reduce-scatter.5.cloned.1.call-done), kind=kOutput, calls=%fused_computation.12 | convolution fusion | flops 5365760 | bytes 477184 | tf_op jit(solution)/shard_map/tlr,trc->tlc/dot_general | solution.py:132
  (9 shorter events, 0.1 us)
Async XLA Ops:
  6.5 117.4 %copy-start = (bf16[8,3,256,256]{3,2,1,0:T(8,128)(2,1)S(1)}, bf16[8,3,256,256]{3,2,1,0:T(8,128)(2,1)}, u32[]{:S(2)}) copy-start(bf16[8,3,256,256]{3,2,1,0:T(8,128)(2,1)} %param.18) | copy-start | bytes 9437188
  6.5 122.8 %reduce-scatter.5.cloned.1.call-start = ((), (), s32[]{:S(2)}) async-start(), calls=%async_computation.3 | async-start | bytes 98304 | tf_op jit(solution)/shard_map/reduce_scatter | solution.py:108
  10.2 105.3 %copy-start.1 = (bf16[8,64,32]{1,2,0:T(8,128)(2,1)}, bf16[8,64,32]{1,2,0:T(8,128)(2,1)S(1)}, u32[]{:S(2)}) copy-start(bf16[8,64,32]{1,2,0:T(8,128)(2,1)S(1)} %convolution_convert_fusion) | copy-start | bytes 98308
  10.2 105.3 %collective-permute-start.3 = (bf16[8,64,32]{1,2,0:T(8,128)(2,1)S(1)}, bf16[8,64,32]{1,2,0:T(8,128)(2,1)}, u32[]{:S(2)}, u32[]{:S(2)}) collective-permute-start(bf16[8,64,32]{1,2,0:T(8,128)(2,1)S(1)} %convolution_convert_fusion), channel_id=1, source_target_pairs={{2,0},{4,2},{6,4},{8,6},{10,8},{12,10},{14,12},{16,14},{18,16},{20... | collective-permute-start | bytes 98312 | tf_op jit(solution)/shard_map/ppermute | solution.py:15
  11.5 104.0 %collective-permute-start.2 = (bf16[8,64,32]{1,2,0:T(8,128)(2,1)S(1)}, bf16[8,64,32]{1,2,0:T(8,128)(2,1)}, u32[]{:S(2)}, u32[]{:S(2)}) collective-permute-start(bf16[8,64,32]{1,2,0:T(8,128)(2,1)S(1)} %convolution_convert_fusion), channel_id=1, source_target_pairs={{0,2},{2,4},{4,6},{6,8},{8,10},{10,12},{12,14},{14,16},{16,18},{18... | collective-permute-start | bytes 98312 | tf_op jit(solution)/shard_map/ppermute | solution.py:12
  17.5 102.3 %collective-permute-start.1 = (bf16[8,256,32]{1,2,0:T(8,128)(2,1)S(1)}, bf16[8,256,32]{1,2,0:T(8,128)(2,1)}, u32[]{:S(2)}, u32[]{:S(2)}) collective-permute-start(bf16[8,256,32]{1,2,0:T(8,128)(2,1)S(1)} %all_gather.9), channel_id=1, source_target_pairs={{2,0},{4,2},{6,4},{8,6},{10,8},{12,10},{14,12},{16,14},{18,16},{20... | collective-permute-start | bytes 393224 | tf_op jit(solution)/shard_map/ppermute | solution.py:15
  18.8 101.0 %collective-permute-start = (bf16[8,256,32]{1,2,0:T(8,128)(2,1)S(1)}, bf16[8,256,32]{1,2,0:T(8,128)(2,1)}, u32[]{:S(2)}, u32[]{:S(2)}) collective-permute-start(bf16[8,256,32]{1,2,0:T(8,128)(2,1)S(1)} %all_gather.9), channel_id=1, source_target_pairs={{0,2},{2,4},{4,6},{6,8},{8,10},{10,12},{12,14},{14,16},{16,18},{18... | collective-permute-start | bytes 393224 | tf_op jit(solution)/shard_map/ppermute | solution.py:12
  119.7 16.3 %reduce-scatter.3.cloned.1.call-start = ((), (), s32[]{:S(2)}) async-start(), calls=%async_computation.2 | async-start | bytes 196608 | tf_op jit(solution)/shard_map/reduce_scatter | solution.py:105
  123.9 4.6 %copy-start.3 = (bf16[1,64,64]{2,1,0:T(8,128)(2,1)S(1)}, bf16[1,64,64]{2,1,0:T(8,128)(2,1)}, u32[]{:S(2)}) copy-start(bf16[1,64,64]{2,1,0:T(8,128)(2,1)} %param.29) | copy-start | bytes 24580
  123.9 12.1 %copy-start.2 = (bf16[8,64,64]{2,1,0:T(8,128)(2,1)S(1)}, bf16[8,64,64]{2,1,0:T(8,128)(2,1)}, u32[]{:S(2)}) copy-start(bf16[8,64,64]{2,1,0:T(8,128)(2,1)} %param.25) | copy-start | bytes 196612
Sparse Core Ops, SparseCore 0:
  119.9 5.2 reduce-scatter.4
  127.3 8.6 reduce-scatter.2
where the time goes:
time: 146 us; the launch traced here: 145 us
  blocking collectives  77.7 us (53%)
  matrix products  19.7 us (13%)
  starting transfers between devices  14.1 us (10%)
  between operations  13.6 us (9%)
  local copies, waits for them, and re-layouts  6.75 us (5%)
  waiting for transfers between devices  6.7 us (5%)
  other arithmetic  6.31 us (4%)
    all_gather x1, blocking collectives, body(): lax.all_gather(raised_coefficients[None], 'leaf', axis=0, tiled=True)  39.4 us
    all_gather x1, blocking collectives, body(): lax.all_gather(node_coeff[None], 'leaf', axis=0, tiled=True)  35.8 us
    ppermute x2, starting transfers between devices, extended_2(): lax.ppermute(lax.slice_in_dim(block, block.shape[dim] - width, None, axis...  11.5 us
    reduce_scatter x1, waiting for transfers between devices, body(): lax.psum_scatter(proximate_portion.astype(jnp.bfloat16), 'sub', scatter_d...  6.65 us
    dot_general x3, matrix products, upper_tree(): jnp.einsum('nfrs,nfsc->nrc', upper_coupling[breadth - 2:2 * breadth - 2],...  3.44 us
  transfers between devices with their start and end apart: 6, of which 1 were waited for; matrix products, arithmetic and copies ran while one was open for 21% of the time, Pallas kernels for 0%

commit v1 on v0

v1 whole, which is shorter than its diff:
```python
import jax
import jax.numpy as jnp
from jax import lax
from jax.experimental import pallas as pl
from jax.experimental.pallas import tpu as pltpu
from jax.sharding import PartitionSpec as P

LAST = (((1,), (1,)), ((), ()))
PLAIN = (((1,), (0,)), ((), ()))


def mm(a, b, dims):
    return lax.dot_general(a, b, dims, preferred_element_type=jnp.float32)


def vmem():
    return pl.BlockSpec(memory_space=pltpu.VMEM)


def smem():
    return pl.BlockSpec(memory_space=pltpu.SMEM)


def anywhere():
    return pl.BlockSpec(memory_space=pl.ANY)


def up_kernel(dens, col, leaf_up, node_up, pack, message):
    leaves, _, points = dens.shape
    rank = col.shape[1]
    halves = points // 128
    node = None
    for t in range(leaves):
        here = dens[t]
        for h in range(halves):
            pack[t * halves + h] = here[:, h * 128 : (h + 1) * 128]
        coeff = mm(here, col[t], LAST).astype(jnp.bfloat16)
        side = t % 2
        pack[leaves * halves + t // 2, :, side * rank : (side + 1) * rank] = coeff
        term = mm(coeff, leaf_up[t], PLAIN)
        node = term if node is None else node + term
    node = node.astype(jnp.bfloat16)
    message[:, :rank] = node
    message[:, rank:] = mm(node, node_up[0], PLAIN).astype(jnp.bfloat16)


def field_kernel(
    lists, lists_other, low, own, high, near, near_other, coup, coup_other,
    near_out, far_out, ext, ext_coeff, blocks, sems,
):
    leaves, entries = near.shape[0], near.shape[1]
    rank = coup.shape[-1]
    points = near.shape[-1]
    halves = points // 128
    copies = []
    for t in range(leaves):
        pair = []
        for s, ref in enumerate((near, near_other)):
            copy = pltpu.make_async_copy(
                ref.at[t], blocks.at[t, pl.ds(s * entries, entries)], sems.at[t, s]
            )
            copy.start()
            pair.append(copy)
        copies.append(pair)
    for b, ref in enumerate((low, own, high)):
        for t in range(leaves):
            for h in range(halves):
                ext[b * leaves + t, :, h * 128 : (h + 1) * 128] = ref[t * halves + h]
            side = t % 2
            ext_coeff[b * leaves + t] = ref[
                leaves * halves + t // 2, :, side * rank : (side + 1) * rank
            ]
    offset = (lax.axis_index("leaf") - 1) * leaves
    for t in range(leaves):
        total = None
        for s, table in enumerate((lists, lists_other)):
            for j in range(entries):
                source = ext_coeff[table[entries + j, t] - offset]
                matrix = (coup, coup_other)[s][t, j]
                term = mm(source, matrix, LAST)
                total = term if total is None else total + term
        far_out[t] = total
    for t in range(leaves):
        for copy in copies[t]:
            copy.wait()
        total = None
        for s, table in enumerate((lists, lists_other)):
            for j in range(entries):
                source = ext[table[j, t] - offset]
                term = mm(source, blocks[t, s * entries + j], LAST)
                total = term if total is None else total + term
        near_out[t] = total


def down_kernel(
    node_list, upper_list, gathered, near, far, row, leaf_down, node_coup, node_down,
    upper_coup, upper_up, upper_down, out, *tree,
):
    nodes, columns, _ = gathered.shape
    rank = row.shape[1]
    leaves = row.shape[0]
    farc = node_coup.shape[1]
    levels = nodes.bit_length() - 1
    me = lax.axis_index("leaf")

    for m in range(nodes // 2):
        left = gathered[(2 * m) ^ me, :, rank:].astype(jnp.float32)
        right = gathered[(2 * m + 1) ^ me, :, rank:].astype(jnp.float32)
        tree[levels - 2][m] = (left + right).astype(jnp.bfloat16)
    for height in range(levels - 2, 0, -1):
        breadth = 2**height
        lower = tree[height]
        for m in range(breadth):
            first = 2 * (breadth + m) - 4
            value = mm(lower[2 * m], upper_up[first], PLAIN)
            value = value + mm(lower[2 * m + 1], upper_up[first + 1], PLAIN)
            tree[height - 1][m] = value.astype(jnp.bfloat16)
    field = None
    for height in range(1, levels):
        breadth = 2**height
        node = (nodes + me) >> (levels - height)
        total = None
        for j in range(farc):
            source = tree[height - 1][upper_list[j, node - 2] - breadth]
            term = mm(source, upper_coup[node - 2, j], LAST)
            total = term if total is None else total + term
        if height > 1:
            total = total + mm(field, upper_down[node - 4], LAST)
        field = total.astype(jnp.bfloat16)
    total = mm(field, node_down[0], LAST)
    for j in range(farc):
        source = gathered[node_list[0, j] ^ me, :, :rank]
        total = total + mm(source, node_coup[0, j], LAST)
    field = total.astype(jnp.bfloat16)
    for t in range(leaves):
        local = (far[t] + mm(field, leaf_down[t], LAST)).astype(jnp.bfloat16)
        out[t] = (near[t] + mm(local, row[t], PLAIN)).astype(jnp.bfloat16)


def body(
    density,
    near_blocks,
    near_index,
    col_basis,
    row_basis,
    leaf_coupling,
    leaf_list,
    leaf_up,
    leaf_down,
    node_coupling,
    node_list,
    node_up,
    node_down,
    upper_coupling,
    upper_list,
    upper_up,
    upper_down,
):
    leaves, points, columns = density.shape
    rank = col_basis.shape[2]
    nodes = lax.axis_size("leaf")
    levels = nodes.bit_length() - 1
    bf16, f32 = jnp.bfloat16, jnp.float32
    swap = [(0, 1), (1, 0)]

    near_other = lax.ppermute(near_blocks, "sub", swap)
    coup_other = lax.ppermute(leaf_coupling, "sub", swap)
    lists = jnp.concatenate([near_index.T, leaf_list.T], axis=0)
    lists_other = lax.ppermute(lists, "sub", swap)

    dens = jnp.swapaxes(density, 1, 2)
    tiles = leaves * (points // 128) + leaves // 2
    pack, message = pl.pallas_call(
        up_kernel,
        out_shape=(
            jax.ShapeDtypeStruct((tiles, columns, 128), bf16),
            jax.ShapeDtypeStruct((columns, 2 * rank), bf16),
        ),
        in_specs=[vmem()] * 4,
        out_specs=(vmem(), vmem()),
        name="up",
    )(dens, jnp.swapaxes(col_basis, 1, 2), leaf_up, node_up)

    low = lax.ppermute(pack, "leaf", [(i, i + 1) for i in range(nodes - 1)])
    high = lax.ppermute(pack, "leaf", [(i + 1, i) for i in range(nodes - 1)])
    gathered = message[None]
    for bit in range(levels):
        step = 1 << bit
        other = lax.ppermute(gathered, "leaf", [(i, i ^ step) for i in range(nodes)])
        gathered = jnp.concatenate([gathered, other], axis=0)

    entries = near_blocks.shape[1]
    near, far = pl.pallas_call(
        field_kernel,
        out_shape=(
            jax.ShapeDtypeStruct((leaves, columns, points), f32),
            jax.ShapeDtypeStruct((leaves, columns, rank), f32),
        ),
        in_specs=[smem()] * 2 + [vmem()] * 3 + [anywhere()] * 2 + [vmem()] * 2,
        out_specs=(vmem(), vmem()),
        scratch_shapes=[
            pltpu.VMEM((3 * leaves, columns, points), bf16),
            pltpu.VMEM((3 * leaves, columns, rank), bf16),
            pltpu.VMEM((leaves, 2 * entries, points, points), bf16),
            pltpu.SemaphoreType.DMA((leaves, 2)),
        ],
        compiler_params=pltpu.CompilerParams(vmem_limit_bytes=24 * 1024 * 1024),
        cost_estimate=pl.CostEstimate(
            flops=2 * leaves * 2 * entries * points * points * 128,
            bytes_accessed=leaves * 2 * entries * points * points * 2,
            transcendentals=0,
        ),
        name="field",
    )(lists, lists_other, low, pack, high, near_blocks, near_other, leaf_coupling, coup_other)

    out = pl.pallas_call(
        down_kernel,
        out_shape=jax.ShapeDtypeStruct((leaves, columns, points), bf16),
        in_specs=[smem()] * 2 + [vmem()] * 10,
        out_specs=vmem(),
        scratch_shapes=[
            pltpu.VMEM((2**height, columns, rank), bf16) for height in range(1, levels)
        ],
        compiler_params=pltpu.CompilerParams(vmem_limit_bytes=24 * 1024 * 1024),
        name="down",
    )(
        node_list, upper_list.T, gathered, near, far, jnp.swapaxes(row_basis, 1, 2), leaf_down,
        node_coupling, node_down, upper_coupling, upper_up, upper_down,
    )
    return jnp.swapaxes(out, 1, 2)


def solution(mesh):
    placed = (
        P("leaf", None, "sub"),
        P("leaf", "sub", None, None),
        P("leaf", "sub"),
        P("leaf", None, None),
        P("leaf", None, None),
        P("leaf", "sub", None, None),
        P("leaf", "sub"),
        P("leaf", None, None),
        P("leaf", None, None),
        P("leaf", None, None, None),
        P("leaf", None),
        P("leaf", None, None),
        P("leaf", None, None),
        P(),
        P(),
        P(),
        P(),
    )
    return jax.shard_map(
        body, mesh=mesh, in_specs=placed, out_specs=P("leaf", None, "sub"), check_vma=False
    )
```

time: 146 us -> 46.3 us (0.32)
  blocking collectives: 77.7 us -> 0 us
  matrix products: 19.7 us -> 0 us
  Pallas kernels: 0 us -> 14 us
  between operations: 13.6 us -> 0.15 us
  other arithmetic: 6.31 us -> 2.78 us
  waiting for transfers between devices: 6.7 us -> 9.04 us
  local copies, waits for them, and re-layouts: 6.75 us -> 4.55 us
    all_gather x3 -> x0, blocking collectives: 77.7 us -> none  [the longest x1 39.4 us: body(): lax.all_gather(raised_coefficients[None], 'leaf', axis=0, tiled=True)]
    dot_general x15 -> x0, matrix products: 19.7 us -> none  [the longest x3 3.44 us: upper_tree(): jnp.einsum('nfrs,nfsc->nrc', upper_coupling[breadth - 2:2 * breadth - 2],...]
    pallas_call x0 -> x3, Pallas kernels: none -> 14 us  [the longest x1 8.59 us: body(): pl.pallas_call(field_kernel, out_shape=(jax.ShapeDtypeStruct((leaves, col...]
    ppermute x4 -> x9, waiting for transfers between devices: 0.01 us -> 9.04 us  [the longest x4 7.88 us: body(): lax.ppermute(gathered, 'leaf', [(i, i ^ step) for i in range(nodes)])]
    reduce_scatter x2 -> x0, waiting for transfers between devices: 6.65 us -> none  [the longest x1 6.65 us: body(): lax.psum_scatter(proximate_portion.astype(jnp.bfloat16), 'sub', scatter_d...]
    gather x6 -> x0, local copies, waits for them, and re-layouts: 5.86 us -> none  [the longest x1 2.33 us: body(): selected_nodes = extended[near_cols - offset]]
    unnamed x8 -> x28, local copies, waits for them, and re-layouts: 0.02 us -> 4.54 us
    select_n x5 -> x0, other arithmetic: 3.56 us -> none  [the longest x3 2.19 us: upper_tree(): sources = coeffs[height][listed]]
  transfers between devices with their start and end apart: 6 -> 9, of which waited for: 1 -> 5; matrix products, arithmetic and copies ran while one was open for 21% -> 8% of each run, Pallas kernels for 0% -> 5%
where the time goes in v1:
time: 46.3 us; the launch traced here: 45.9 us
  starting transfers between devices  15.4 us (33%)
  Pallas kernels  14 us (30%)
  waiting for transfers between devices  9.04 us (20%)
  local copies, waits for them, and re-layouts  4.55 us (10%)
  other arithmetic  2.78 us (6%)
    ppermute x4, starting transfers between devices, body(): lax.ppermute(gathered, 'leaf', [(i, i ^ step) for i in range(nodes)])  8.6 us
    pallas_call x1, Pallas kernels, body(): pl.pallas_call(field_kernel, out_shape=(jax.ShapeDtypeStruct((leaves, col...  8.59 us
    ppermute x4, waiting for transfers between devices, body(): lax.ppermute(gathered, 'leaf', [(i, i ^ step) for i in range(nodes)])  7.88 us
    ppermute x1, starting transfers between devices, body(): low = lax.ppermute(pack, 'leaf', [(i, i + 1) for i in range(nodes - 1)])  5.02 us
    unnamed x28, local copies, waits for them, and re-layouts  4.54 us
    pallas_call x1, Pallas kernels, body(): pl.pallas_call(down_kernel, out_shape=jax.ShapeDtypeStruct((leaves, colum...  3.18 us
    pallas_call x1, Pallas kernels, body(): pl.pallas_call(up_kernel, out_shape=(jax.ShapeDtypeStruct((tiles, columns...  2.23 us
    concatenate x3, other arithmetic, body(): gathered = jnp.concatenate([gathered, other], axis=0)  2.07 us
  transfers between devices with their start and end apart: 9, of which 5 were waited for; matrix products, arithmetic and copies ran while one was open for 8% of the time, Pallas kernels for 5%

profile of v1, /device:TPU:0, one launch (start us, length us, event | category | flops | bytes accessed | tf_op | source)
XLA Modules:
  0.0 45.9 jit_solution(2251385455385010326)
XLA Ops:
  0.0 0.5 collective-permute-start.7
  0.5 2.2 %up.1 = (bf16[20,16,128]{2,1,0:T(8,128)(2,1)}, bf16[16,128]{1,0:T(8,128)(2,1)}) custom-call(bf16[8,16,256]{2,1,0:T(8,128)(2,1)} %bitcast.16, bf16[8,64,256]{2,1,0:T(8,128)(2,1)} %bitcast.11, bf16[8,64,64]{2,1,0:T(8,128)(2,1)} %leaf_up.1, bf16[1,64,64]{2,1,0:T(8,128)(2,1)} %node_up.1), custom_call_target="tpu_custom_call" | custom-call | tf_op jit(solution)/shard_map/up/pallas_call | solution.py:173
  2.7 1.3 %collective-permute-start.6 = (bf16[20,16,128]{2,1,0:T(8,128)(2,1)}, bf16[20,16,128]{2,1,0:T(8,128)(2,1)S(1)}, u32[]{:S(2)}, u32[]{:S(2)}) collective-permute-start(bf16[20,16,128]{2,1,0:T(8,128)(2,1)} %get-tuple-element.10.own), channel_id=1, source_target_pairs={{2,0},{4,2},{6,4},{8,6},{10,8},{12,10},{14,12},{16,14},{18,16},{20... | collective-permute-start | bytes 245768 | tf_op jit(solution)/shard_map/ppermute | solution.py:185
  4.0 5.0 %collective-permute-start.5 = (bf16[20,16,128]{2,1,0:T(8,128)(2,1)}, bf16[20,16,128]{2,1,0:T(8,128)(2,1)S(1)}, u32[]{:S(2)}, u32[]{:S(2)}) collective-permute-start(bf16[20,16,128]{2,1,0:T(8,128)(2,1)} %get-tuple-element.10.own), channel_id=1, source_target_pairs={{0,2},{2,4},{4,6},{6,8},{8,10},{10,12},{12,14},{14,16},{16,18},{18... | collective-permute-start | bytes 245768 | tf_op jit(solution)/shard_map/ppermute | solution.py:184
  9.0 3.0 %collective-permute-start = (bf16[1,16,128]{2,1,0:T(8,128)(2,1)}, bf16[1,16,128]{2,1,0:T(8,128)(2,1)S(1)}, u32[]{:S(2)}, u32[]{:S(2)}) collective-permute-start(bf16[1,16,128]{2,1,0:T(8,128)(2,1)} %bitcast.12), channel_id=1, source_target_pairs={{0,2},{2,0},{4,6},{6,4},{8,10},{10,8},{12,14},{14,12},{16,18},{18,... | collective-permute-start | bytes 12296 | tf_op jit(solution)/shard_map/ppermute | solution.py:189
  12.0 0.0 collective-permute-start.8
  12.0 0.7 %constant_dynamic-update-slice_fusion.4 = bf16[16,16,128]{2,1,0:T(8,128)(2,1)S(1)} fusion(bf16[16,128]{1,0:T(8,128)(2,1)} %get-tuple-element.9), kind=kLoop, calls=%fused_computation.6 | loop fusion | bytes 8192
  12.7 0.7 %pad_add_fusion.lists = s32[6,8]{1,0:T(8,128)S(1)} fusion(s32[3,8]{1,0:T(4,128)} %bitcast.17, s32[3,8]{1,0:T(4,128)} %bitcast.18), kind=kLoop, calls=%fused_computation.8 | loop fusion | flops 48 | bytes 384 | tf_op jit(solution)/shard_map/concatenate | solution.py:168
  13.4 1.3 %collective-permute-done = bf16[1,16,128]{2,1,0:T(8,128)(2,1)S(1)} collective-permute-done((bf16[1,16,128]{2,1,0:T(8,128)(2,1)}, bf16[1,16,128]{2,1,0:T(8,128)(2,1)S(1)}, u32[]{:S(2)}, u32[]{:S(2)}) %collective-permute-start) | collective-permute-done | bytes 4128 | tf_op jit(solution)/shard_map/ppermute | solution.py:189
  14.7 0.7 %pad_maximum_fusion.2 = bf16[2,16,128]{2,1,0:T(8,128)(2,1)S(1)} fusion(bf16[1,16,128]{2,1,0:T(8,128)(2,1)S(1)} %collective-permute-done, bf16[1,16,128]{2,1,0:T(8,128)(2,1)} %bitcast.13), kind=kLoop, calls=%fused_computation.7 | loop fusion | flops 4096 | bytes 16384 | tf_op jit(solution)/shard_map/concatenate | solution.py:190
  15.4 1.5 %collective-permute-start.1 = (bf16[2,16,128]{2,1,0:T(8,128)(2,1)S(1)}, bf16[2,16,128]{2,1,0:T(8,128)(2,1)S(1)}, u32[]{:S(2)}, u32[]{:S(2)}) collective-permute-start(bf16[2,16,128]{2,1,0:T(8,128)(2,1)S(1)} %pad_maximum_fusion.2), channel_id=1, source_target_pairs={{0,4},{2,6},{4,0},{6,2},{8,12},{10,14},{12,8},{14,10},{16,20},{18,... | collective-permute-start | bytes 24584 | tf_op jit(solution)/shard_map/ppermute | solution.py:189
  16.9 2.2 %collective-permute-done.1 = bf16[2,16,128]{2,1,0:T(8,128)(2,1)S(1)} collective-permute-done((bf16[2,16,128]{2,1,0:T(8,128)(2,1)S(1)}, bf16[2,16,128]{2,1,0:T(8,128)(2,1)S(1)}, u32[]{:S(2)}, u32[]{:S(2)}) %collective-permute-start.1) | collective-permute-done | bytes 8224 | tf_op jit(solution)/shard_map/ppermute | solution.py:189
  19.1 0.7 %pad_maximum_fusion.1 = bf16[4,16,128]{2,1,0:T(8,128)(2,1)S(1)} fusion(bf16[2,16,128]{2,1,0:T(8,128)(2,1)S(1)} %collective-permute-done.1, bf16[1,16,128]{2,1,0:T(8,128)(2,1)S(1)} %collective-permute-done, bf16[1,16,128]{2,1,0:T(8,128)(2,1)} %bitcast.14), kind=kLoop, calls=%fused_computation.1 | loop fusion | flops 16384 | bytes 32768 | tf_op jit(solution)/shard_map/concatenate | solution.py:190
  19.8 1.6 %collective-permute-start.2 = (bf16[4,16,128]{2,1,0:T(8,128)(2,1)S(1)}, bf16[4,16,128]{2,1,0:T(8,128)(2,1)S(1)}, u32[]{:S(2)}, u32[]{:S(2)}) collective-permute-start(bf16[4,16,128]{2,1,0:T(8,128)(2,1)S(1)} %pad_maximum_fusion.1), channel_id=1, source_target_pairs={{0,8},{2,10},{4,12},{6,14},{8,0},{10,2},{12,4},{14,6},{16,24},{18,... | collective-permute-start | bytes 49160 | tf_op jit(solution)/shard_map/ppermute | solution.py:189
  21.4 2.2 %collective-permute-done.2 = bf16[4,16,128]{2,1,0:T(8,128)(2,1)S(1)} collective-permute-done((bf16[4,16,128]{2,1,0:T(8,128)(2,1)S(1)}, bf16[4,16,128]{2,1,0:T(8,128)(2,1)S(1)}, u32[]{:S(2)}, u32[]{:S(2)}) %collective-permute-start.2) | collective-permute-done | bytes 16416 | tf_op jit(solution)/shard_map/ppermute | solution.py:189
  23.5 0.7 %pad_maximum_fusion = bf16[8,16,128]{2,1,0:T(8,128)(2,1)S(1)} fusion(bf16[4,16,128]{2,1,0:T(8,128)(2,1)S(1)} %collective-permute-done.2, bf16[2,16,128]{2,1,0:T(8,128)(2,1)S(1)} %collective-permute-done.1, bf16[1,16,128]{2,1,0:T(8,128)(2,1)S(1)} %collective-permute-done, bf16[1,16,128]{2,1,0:T(8,128)(2,1)} %bitcast.15), kind=kLoop, calls=%fused_computation | loop fusion | flops 49152 | bytes 65536 | tf_op jit(solution)/shard_map/concatenate | solution.py:190
  24.2 2.6 %collective-permute-start.3 = (bf16[8,16,128]{2,1,0:T(8,128)(2,1)S(1)}, bf16[8,16,128]{2,1,0:T(8,128)(2,1)S(1)}, u32[]{:S(2)}, u32[]{:S(2)}) collective-permute-start(bf16[8,16,128]{2,1,0:T(8,128)(2,1)S(1)} %pad_maximum_fusion), channel_id=1, source_target_pairs={{0,16},{2,18},{4,20},{6,22},{8,24},{10,26},{12,28},{14,30},{16,0},... | collective-permute-start | bytes 98312 | tf_op jit(solution)/shard_map/ppermute | solution.py:189
  26.8 0.0 copy-start.9
  26.8 0.0 copy-start.10
  26.8 0.0 copy-start.11
  26.8 2.2 %collective-permute-done.3 = bf16[8,16,128]{2,1,0:T(8,128)(2,1)S(1)} collective-permute-done((bf16[8,16,128]{2,1,0:T(8,128)(2,1)S(1)}, bf16[8,16,128]{2,1,0:T(8,128)(2,1)S(1)}, u32[]{:S(2)}, u32[]{:S(2)}) %collective-permute-start.3) | collective-permute-done | bytes 32800 | tf_op jit(solution)/shard_map/ppermute | solution.py:189
  29.0 0.0 collective-permute-start.4
  29.0 0.0 copy-start.8
  29.0 1.2 %collective-permute-done.4.lists_other = s32[6,8]{1,0:T(8,128)S(1)} collective-permute-done((s32[6,8]{1,0:T(8,128)S(1)}, s32[6,8]{1,0:T(8,128)S(1)}, u32[]{:S(2)}, u32[]{:S(2)}) %collective-permute-start.4) | collective-permute-done | bytes 224 | tf_op jit(solution)/shard_map/ppermute | solution.py:169
  30.2 0.0 collective-permute-done.6.high
  30.2 0.0 collective-permute-done.5.low
  30.2 0.0 collective-permute-done.8.coup_other
  30.2 0.0 collective-permute-done.7.near_other
  30.2 0.0 copy-start
  30.2 1.9 %copy-done = bf16[8,3,256,256]{3,2,1,0:T(8,128)(2,1)S(1)} copy-done((bf16[8,3,256,256]{3,2,1,0:T(8,128)(2,1)S(1)}, bf16[8,3,256,256]{3,2,1,0:T(8,128)(2,1)}, u32[]{:S(2)}) %copy-start) | copy-done | bytes 3145752
  32.1 0.0 copy-start.2
  32.1 1.0 %copy-done.2 = bf16[8,3,64,64]{3,2,1,0:T(8,128)(2,1)S(1)} copy-done((bf16[8,3,64,64]{3,2,1,0:T(8,128)(2,1)S(1)}, bf16[8,3,64,64]{3,2,1,0:T(8,128)(2,1)}, u32[]{:S(2)}) %copy-start.2) | copy-done | bytes 196632
  33.1 0.0 copy-start.7
  33.1 0.9 %copy-done.7 = bf16[20,16,128]{2,1,0:T(8,128)(2,1)S(1)} copy-done((bf16[20,16,128]{2,1,0:T(8,128)(2,1)S(1)}, bf16[20,16,128]{2,1,0:T(8,128)(2,1)}, u32[]{:S(2)}) %copy-start.7) | copy-done | bytes 81944
  34.0 0.0 copy-start.1
  34.0 0.0 copy-start.3
  34.0 0.0 copy-start.4
  34.0 0.0 copy-start.5
  34.0 0.0 copy-start.6
  34.0 8.6 %field.1 = (f32[8,16,256]{2,1,0:T(8,128)S(1)}, f32[8,16,64]{2,1,0:T(8,128)S(1)}) custom-call(s32[6,8]{1,0:T(8,128)S(1)} %pad_add_fusion.lists, s32[6,8]{1,0:T(8,128)S(1)} %collective-permute-done.4.lists_other, bf16[20,16,128]{2,1,0:T(8,128)(2,1)S(1)} %collective-permute-done.5.low, bf16[20,16,128]{2,1,0:T(8,128)(2,1)S(1)} %copy-done.7, ...), custom_call_target="tpu_custom_call" | custom-call | flops 805306368 | bytes 6291456 | tf_op jit(solution)/shard_map/field/pallas_call | solution.py:193
  42.6 0.0 copy-done.9
  42.6 0.0 copy-done.10
  42.6 0.0 copy-done.11
  42.6 0.0 copy-done.8
  42.7 0.0 copy-done.1
  42.7 0.0 copy-done.3
  42.7 0.0 copy-done.4
  42.7 0.0 copy-done.5
  42.7 0.0 copy-done.6
  42.7 3.2 %down.1 = bf16[8,16,256]{2,1,0:T(8,128)(2,1)} custom-call(s32[1,4]{1,0:T(1,128)S(1)} %copy-done.11, s32[4,14]{1,0:T(4,128)S(1)} %bitcast.10, bf16[16,16,128]{2,1,0:T(8,128)(2,1)S(1)} %constant_dynamic-update-slice_fusion.gathered, f32[8,16,256]{2,1,0:T(8,128)S(1)} %get-tuple-element.11.near, f32[8,16,64]{2,1,0:T(8,128)S(1)} %get-tuple-element.12.far, ...), custom_call_target="tpu_custom_call" | custom-call | tf_op jit(solution)/shard_map/down/pallas_call | solution.py:216
  (4 shorter events, 0.0 us)
Async XLA Ops:
  0.0 30.2 %collective-permute-start.7 = (bf16[8,3,256,256]{3,2,1,0:T(8,128)(2,1)}, bf16[8,3,256,256]{3,2,1,0:T(8,128)(2,1)S(1)}, u32[]{:S(2)}, u32[]{:S(2)}) collective-permute-start(bf16[8,3,256,256]{3,2,1,0:T(8,128)(2,1)} %near.1), channel_id=1, source_target_pairs={{0,1},{1,0},{2,3},{3,2},{4,5},{5,4},{6,7},{7,6},{8,9},{9,8},{10,11... | collective-permute-start | bytes 9437192 | tf_op jit(solution)/shard_map/ppermute | solution.py:166
  2.7 27.5 %collective-permute-start.6 = (bf16[20,16,128]{2,1,0:T(8,128)(2,1)}, bf16[20,16,128]{2,1,0:T(8,128)(2,1)S(1)}, u32[]{:S(2)}, u32[]{:S(2)}) collective-permute-start(bf16[20,16,128]{2,1,0:T(8,128)(2,1)} %get-tuple-element.10.own), channel_id=1, source_target_pairs={{2,0},{4,2},{6,4},{8,6},{10,8},{12,10},{14,12},{16,14},{18,16},{20... | collective-permute-start | bytes 245768 | tf_op jit(solution)/shard_map/ppermute | solution.py:185
  4.0 26.2 %collective-permute-start.5 = (bf16[20,16,128]{2,1,0:T(8,128)(2,1)}, bf16[20,16,128]{2,1,0:T(8,128)(2,1)S(1)}, u32[]{:S(2)}, u32[]{:S(2)}) collective-permute-start(bf16[20,16,128]{2,1,0:T(8,128)(2,1)} %get-tuple-element.10.own), channel_id=1, source_target_pairs={{0,2},{2,4},{4,6},{6,8},{8,10},{10,12},{12,14},{14,16},{16,18},{18... | collective-permute-start | bytes 245768 | tf_op jit(solution)/shard_map/ppermute | solution.py:184
  9.0 5.7 %collective-permute-start = (bf16[1,16,128]{2,1,0:T(8,128)(2,1)}, bf16[1,16,128]{2,1,0:T(8,128)(2,1)S(1)}, u32[]{:S(2)}, u32[]{:S(2)}) collective-permute-start(bf16[1,16,128]{2,1,0:T(8,128)(2,1)} %bitcast.12), channel_id=1, source_target_pairs={{0,2},{2,0},{4,6},{6,4},{8,10},{10,8},{12,14},{14,12},{16,18},{18,... | collective-permute-start | bytes 12296 | tf_op jit(solution)/shard_map/ppermute | solution.py:189
  12.0 18.2 %collective-permute-start.8 = (bf16[8,3,64,64]{3,2,1,0:T(8,128)(2,1)}, bf16[8,3,64,64]{3,2,1,0:T(8,128)(2,1)S(1)}, u32[]{:S(2)}, u32[]{:S(2)}) collective-permute-start(bf16[8,3,64,64]{3,2,1,0:T(8,128)(2,1)} %coup.1), channel_id=1, source_target_pairs={{0,1},{1,0},{2,3},{3,2},{4,5},{5,4},{6,7},{7,6},{8,9},{9,8},{10,11... | collective-permute-start | bytes 589832 | tf_op jit(solution)/shard_map/ppermute | solution.py:167
  15.4 3.7 %collective-permute-start.1 = (bf16[2,16,128]{2,1,0:T(8,128)(2,1)S(1)}, bf16[2,16,128]{2,1,0:T(8,128)(2,1)S(1)}, u32[]{:S(2)}, u32[]{:S(2)}) collective-permute-start(bf16[2,16,128]{2,1,0:T(8,128)(2,1)S(1)} %pad_maximum_fusion.2), channel_id=1, source_target_pairs={{0,4},{2,6},{4,0},{6,2},{8,12},{10,14},{12,8},{14,10},{16,20},{18,... | collective-permute-start | bytes 24584 | tf_op jit(solution)/shard_map/ppermute | solution.py:189
  19.8 3.7 %collective-permute-start.2 = (bf16[4,16,128]{2,1,0:T(8,128)(2,1)S(1)}, bf16[4,16,128]{2,1,0:T(8,128)(2,1)S(1)}, u32[]{:S(2)}, u32[]{:S(2)}) collective-permute-start(bf16[4,16,128]{2,1,0:T(8,128)(2,1)S(1)} %pad_maximum_fusion.1), channel_id=1, source_target_pairs={{0,8},{2,10},{4,12},{6,14},{8,0},{10,2},{12,4},{14,6},{16,24},{18,... | collective-permute-start | bytes 49160 | tf_op jit(solution)/shard_map/ppermute | solution.py:189
  24.2 4.8 %collective-permute-start.3 = (bf16[8,16,128]{2,1,0:T(8,128)(2,1)S(1)}, bf16[8,16,128]{2,1,0:T(8,128)(2,1)S(1)}, u32[]{:S(2)}, u32[]{:S(2)}) collective-permute-start(bf16[8,16,128]{2,1,0:T(8,128)(2,1)S(1)} %pad_maximum_fusion), channel_id=1, source_target_pairs={{0,16},{2,18},{4,20},{6,22},{8,24},{10,26},{12,28},{14,30},{16,0},... | collective-permute-start | bytes 98312 | tf_op jit(solution)/shard_map/ppermute | solution.py:189
  26.8 15.8 %copy-start.9 = (bf16[1,64,64]{2,1,0:T(8,128)(2,1)S(1)}, bf16[1,64,64]{2,1,0:T(8,128)(2,1)}, u32[]{:S(2)}) copy-start(bf16[1,64,64]{2,1,0:T(8,128)(2,1)} %node_down.1) | copy-start | bytes 24580
  26.8 15.8 %copy-start.10 = (s32[14,4]{0,1:T(4,128)S(1)}, s32[14,4]{0,1:T(4,128)}, u32[]{:S(2)}) copy-start(s32[14,4]{0,1:T(4,128)} %param.31) | copy-start | bytes 676
  26.8 15.8 %copy-start.11 = (s32[1,4]{1,0:T(1,128)S(1)}, s32[1,4]{1,0:T(1,128)}, u32[]{:S(2)}) copy-start(s32[1,4]{1,0:T(1,128)} %node_list.1) | copy-start | bytes 52
  29.0 1.2 %collective-permute-start.4 = (s32[6,8]{1,0:T(8,128)S(1)}, s32[6,8]{1,0:T(8,128)S(1)}, u32[]{:S(2)}, u32[]{:S(2)}) collective-permute-start(s32[6,8]{1,0:T(8,128)S(1)} %pad_add_fusion.lists), channel_id=1, source_target_pairs={{0,1},{1,0},{2,3},{3,2},{4,5},{5,4},{6,7},{7,6},{8,9},{9,8},{10,11... | collective-permute-start | bytes 584 | tf_op jit(solution)/shard_map/ppermute | solution.py:169
  29.0 13.6 %copy-start.8 = (bf16[1,4,64,64]{3,2,1,0:T(8,128)(2,1)S(1)}, bf16[1,4,64,64]{3,2,1,0:T(8,128)(2,1)}, u32[]{:S(2)}) copy-start(bf16[1,4,64,64]{3,2,1,0:T(8,128)(2,1)} %node_coup.1) | copy-start | bytes 98308
  30.2 1.9 %copy-start = (bf16[8,3,256,256]{3,2,1,0:T(8,128)(2,1)S(1)}, bf16[8,3,256,256]{3,2,1,0:T(8,128)(2,1)}, u32[]{:S(2)}) copy-start(bf16[8,3,256,256]{3,2,1,0:T(8,128)(2,1)} %near.1) | copy-start | bytes 9437188
  32.1 1.0 %copy-start.2 = (bf16[8,3,64,64]{3,2,1,0:T(8,128)(2,1)S(1)}, bf16[8,3,64,64]{3,2,1,0:T(8,128)(2,1)}, u32[]{:S(2)}) copy-start(bf16[8,3,64,64]{3,2,1,0:T(8,128)(2,1)} %coup.1) | copy-start | bytes 589828
  33.1 0.9 %copy-start.7 = (bf16[20,16,128]{2,1,0:T(8,128)(2,1)S(1)}, bf16[20,16,128]{2,1,0:T(8,128)(2,1)}, u32[]{:S(2)}) copy-start(bf16[20,16,128]{2,1,0:T(8,128)(2,1)} %get-tuple-element.10.own) | copy-start | bytes 245764
  34.0 8.7 %copy-start.1 = (bf16[14,4,64,64]{3,2,1,0:T(8,128)(2,1)S(1)}, bf16[14,4,64,64]{3,2,1,0:T(8,128)(2,1)}, u32[]{:S(2)}) copy-start(bf16[14,4,64,64]{3,2,1,0:T(8,128)(2,1)} %upper_coup.1) | copy-start | bytes 1376260
  34.0 8.7 %copy-start.3 = (bf16[8,256,64]{1,2,0:T(8,128)(2,1)S(1)}, bf16[8,256,64]{1,2,0:T(8,128)(2,1)}, u32[]{:S(2)}) copy-start(bf16[8,256,64]{1,2,0:T(8,128)(2,1)} %param.21) | copy-start | bytes 786436
  34.0 8.7 %copy-start.4 = (bf16[12,64,64]{2,1,0:T(8,128)(2,1)S(1)}, bf16[12,64,64]{2,1,0:T(8,128)(2,1)}, u32[]{:S(2)}) copy-start(bf16[12,64,64]{2,1,0:T(8,128)(2,1)} %upper_up.1) | copy-start | bytes 294916
  34.0 8.7 %copy-start.5 = (bf16[12,64,64]{2,1,0:T(8,128)(2,1)S(1)}, bf16[12,64,64]{2,1,0:T(8,128)(2,1)}, u32[]{:S(2)}) copy-start(bf16[12,64,64]{2,1,0:T(8,128)(2,1)} %upper_down.1) | copy-start | bytes 294916
  34.0 8.7 %copy-start.6 = (bf16[8,64,64]{2,1,0:T(8,128)(2,1)S(1)}, bf16[8,64,64]{2,1,0:T(8,128)(2,1)}, u32[]{:S(2)}) copy-start(bf16[8,64,64]{2,1,0:T(8,128)(2,1)} %leaf_down.1) | copy-start | bytes 196612

commit v2 on v1

v2 whole, which is shorter than its diff:
```python
import functools

import jax
import jax.numpy as jnp
from jax import lax
from jax.experimental import pallas as pl
from jax.experimental.pallas import tpu as pltpu
from jax.sharding import PartitionSpec as P

LAST = (((1,), (1,)), ((), ()))
PLAIN = (((1,), (0,)), ((), ()))


def mm(a, b, dims):
    return lax.dot_general(a, b, dims, preferred_element_type=jnp.float32)


def vmem():
    return pl.BlockSpec(memory_space=pltpu.VMEM)


def smem():
    return pl.BlockSpec(memory_space=pltpu.SMEM)


def anywhere():
    return pl.BlockSpec(memory_space=pl.ANY)


def up_kernel(dens, col, leaf_up, node_up, coeff_out, message):
    leaves = dens.shape[0]
    rank = col.shape[1]
    node = None
    for t in range(leaves):
        coeff = mm(dens[t], col[t], LAST).astype(jnp.bfloat16)
        coeff_out[t] = coeff
        term = mm(coeff, leaf_up[t], PLAIN)
        node = term if node is None else node + term
    node = node.astype(jnp.bfloat16)
    message[:, :rank] = node
    message[:, rank:] = mm(node, node_up[0], PLAIN).astype(jnp.bfloat16)


def pack_kernel(dens, coeff, near, _, __, pack, near_out, sem):
    copy = pltpu.make_async_copy(near, near_out, sem)
    copy.start()
    leaves, _, points = dens.shape
    rank = coeff.shape[2]
    halves = points // 128
    for t in range(leaves):
        here = dens[t]
        for h in range(halves):
            pack[t * halves + h] = here[:, h * 128 : (h + 1) * 128]
        side = t % 2
        pack[leaves * halves + t // 2, :, side * rank : (side + 1) * rank] = coeff[t]
    copy.wait()


def field_kernel(
    first, lists, lists_other, pair, own, cross, near, near_other, coup, coup_other, _,
    near_out, far_out, ext, ext_coeff,
):
    leaves, entries = near.shape[0], near.shape[1]
    count = near_out.shape[0]
    rank = coup.shape[-1]
    points = near.shape[-1]
    halves = points // 128
    me = lax.axis_index("leaf")
    odd = me & 1
    for slot, ref in ((2 - 2 * odd, pair), (1, own), (2 * odd, cross)):
        for t in range(leaves):
            for h in range(halves):
                ext[slot * leaves + t, :, h * 128 : (h + 1) * 128] = ref[t * halves + h]
            side = t % 2
            ext_coeff[slot * leaves + t] = ref[
                leaves * halves + t // 2, :, side * rank : (side + 1) * rank
            ]
    offset = (me - 1) * leaves
    for k in range(count):
        t = first + k
        total = None
        for table, matrices in ((lists, coup), (lists_other, coup_other)):
            for j in range(entries):
                source = ext_coeff[table[entries + j, t] - offset]
                term = mm(source, matrices[t, j], LAST)
                total = term if total is None else total + term
        far_out[k] = total
        total = None
        for table, blocks in ((lists, near), (lists_other, near_other)):
            for j in range(entries):
                term = mm(ext[table[j, t] - offset], blocks[t, j], LAST)
                total = term if total is None else total + term
        near_out[k] = total


def down_kernel(
    node_list, upper_list, known, other, near, near_late, far, far_late, row, leaf_down, node_coup, node_down,
    upper_coup, upper_up, upper_down, out, *tree,
):
    half_nodes, columns, _ = known.shape
    nodes = 2 * half_nodes
    rank = row.shape[1]
    leaves = row.shape[0]
    gathered, tree = tree[0], tree[1:]
    gathered[:half_nodes] = known[...]
    gathered[half_nodes:] = other[...]
    farc = node_coup.shape[1]
    levels = nodes.bit_length() - 1
    me = lax.axis_index("leaf")

    for m in range(nodes // 2):
        left = gathered[(2 * m) ^ me, :, rank:].astype(jnp.float32)
        right = gathered[(2 * m + 1) ^ me, :, rank:].astype(jnp.float32)
        tree[levels - 2][m] = (left + right).astype(jnp.bfloat16)
    for height in range(levels - 2, 0, -1):
        breadth = 2**height
        lower = tree[height]
        for m in range(breadth):
            first = 2 * (breadth + m) - 4
            value = mm(lower[2 * m], upper_up[first], PLAIN)
            value = value + mm(lower[2 * m + 1], upper_up[first + 1], PLAIN)
            tree[height - 1][m] = value.astype(jnp.bfloat16)
    field = None
    for height in range(1, levels):
        breadth = 2**height
        node = (nodes + me) >> (levels - height)
        total = None
        for j in range(farc):
            source = tree[height - 1][upper_list[j, node - 2] - breadth]
            term = mm(source, upper_coup[node - 2, j], LAST)
            total = term if total is None else total + term
        if height > 1:
            total = total + mm(field, upper_down[node - 4], LAST)
        field = total.astype(jnp.bfloat16)
    total = mm(field, node_down[0], LAST)
    for j in range(farc):
        source = gathered[node_list[0, j] ^ me, :, :rank]
        total = total + mm(source, node_coup[0, j], LAST)
    field = total.astype(jnp.bfloat16)
    half = near.shape[0]
    for t in range(leaves):
        near_here, far_here = (near[t], far[t]) if t < half else (near_late[t - half], far_late[t - half])
        local = (far_here + mm(field, leaf_down[t], LAST)).astype(jnp.bfloat16)
        out[t] = (near_here + mm(local, row[t], PLAIN)).astype(jnp.bfloat16)


def body(
    density,
    near_blocks,
    near_index,
    col_basis,
    row_basis,
    leaf_coupling,
    leaf_list,
    leaf_up,
    leaf_down,
    node_coupling,
    node_list,
    node_up,
    node_down,
    upper_coupling,
    upper_list,
    upper_up,
    upper_down,
):
    leaves, points, columns = density.shape
    rank = col_basis.shape[2]
    nodes = lax.axis_size("leaf")
    levels = nodes.bit_length() - 1
    bf16, f32 = jnp.bfloat16, jnp.float32
    swap = [(0, 1), (1, 0)]

    near_other = lax.ppermute(near_blocks, "sub", swap)
    coup_other = lax.ppermute(leaf_coupling, "sub", swap)
    lists = jnp.concatenate([near_index.T, leaf_list.T], axis=0)
    lists_other = lax.ppermute(lists, "sub", swap)

    dens = jnp.swapaxes(density, 1, 2)
    coeff, message = pl.pallas_call(
        up_kernel,
        out_shape=(
            pltpu.VMEM((leaves, columns, rank), bf16),
            pltpu.VMEM((columns, 2 * rank), bf16),
        ),
        in_specs=[vmem()] * 4,
        out_specs=(vmem(), vmem()),
        name="up",
    )(dens, jnp.swapaxes(col_basis, 1, 2), leaf_up, node_up)
    tiles = leaves * (points // 128) + leaves // 2
    pack, near_here = pl.pallas_call(
        pack_kernel,
        out_shape=(
            pltpu.VMEM((tiles, columns, 128), bf16),
            pltpu.VMEM(near_blocks.shape, bf16),
        ),
        in_specs=[vmem()] * 2 + [anywhere()] * 3,
        out_specs=(vmem(), vmem()),
        scratch_shapes=[pltpu.SemaphoreType.DMA],
        name="pack",
    )(
        dens, coeff, pltpu.with_memory_space_constraint(near_blocks, pltpu.HBM), coup_other,
        lists_other,
    )
    inner = [(i, (i + 1 if i % 2 else i - 1)) for i in range(1, nodes - 1)]
    pair = lax.ppermute(pack, "leaf", [(i, i ^ 1) for i in range(nodes)])
    cross = lax.ppermute(pack, "leaf", inner + [(0, 0), (nodes - 1, nodes - 1)])

    entries = near_blocks.shape[1]
    half = leaves // 2

    def fields(first, after):
        return pl.pallas_call(
            functools.partial(field_kernel, first),
            out_shape=(
                jax.ShapeDtypeStruct((half, columns, points), f32),
                jax.ShapeDtypeStruct((half, columns, rank), f32),
            ),
            in_specs=[smem()] * 2 + [vmem()] * 7 + [anywhere()],
            out_specs=(vmem(), vmem()),
            scratch_shapes=[
                pltpu.VMEM((3 * leaves, columns, points), bf16),
                pltpu.VMEM((3 * leaves, columns, rank), bf16),
            ],
            compiler_params=pltpu.CompilerParams(vmem_limit_bytes=24 * 1024 * 1024),
            cost_estimate=pl.CostEstimate(
                flops=2 * half * 2 * entries * points * points * 256,
                bytes_accessed=half * 2 * entries * points * points * 2,
                transcendentals=0,
            ),
            name="fields",
        )(
            lists, lists_other, pair, pack, cross, near_here, near_other, leaf_coupling,
            coup_other, after,
        )

    known = message[None]
    near = far = near_late = far_late = None
    for bit in range(levels):
        step = 1 << bit
        other = lax.ppermute(known, "leaf", [(i, i ^ step) for i in range(nodes)])
        if bit == 0:
            known, other, pack = lax.optimization_barrier((known, other, pack))
        if bit == levels - 2:
            near, far = fields(0, known)
            known, other, near, far = lax.optimization_barrier((known, other, near, far))
        if bit == levels - 1:
            near_late, far_late = fields(half, known)
        else:
            known = jnp.concatenate([known, other], axis=0)

    out = pl.pallas_call(
        down_kernel,
        out_shape=jax.ShapeDtypeStruct((leaves, columns, points), bf16),
        in_specs=[smem()] * 2 + [vmem()] * 13,
        out_specs=vmem(),
        scratch_shapes=[pltpu.VMEM((nodes, columns, 2 * rank), bf16)]
        + [pltpu.VMEM((2**height, columns, rank), bf16) for height in range(1, levels)],
        compiler_params=pltpu.CompilerParams(vmem_limit_bytes=24 * 1024 * 1024),
        name="down",
    )(
        node_list, upper_list.T, known, other, near, near_late, far, far_late,
        jnp.swapaxes(row_basis, 1, 2), leaf_down, node_coupling, node_down, upper_coupling, upper_up, upper_down,
    )
    return jnp.swapaxes(out, 1, 2)


def solution(mesh):
    placed = (
        P("leaf", None, "sub"),
        P("leaf", "sub", None, None),
        P("leaf", "sub"),
        P("leaf", None, None),
        P("leaf", None, None),
        P("leaf", "sub", None, None),
        P("leaf", "sub"),
        P("leaf", None, None),
        P("leaf", None, None),
        P("leaf", None, None, None),
        P("leaf", None),
        P("leaf", None, None),
        P("leaf", None, None),
        P(),
        P(),
        P(),
        P(),
    )
    return jax.shard_map(
        body, mesh=mesh, in_specs=placed, out_specs=P("leaf", None, "sub"), check_vma=False
    )
```

time: 46.3 us -> 36.8 us (0.79)
  waiting for transfers between devices: 9.04 us -> 3.3 us
  other arithmetic: 2.78 us -> 0.71 us
  starting transfers between devices: 15.4 us -> 14.3 us
    ppermute x6, waiting for transfers between devices: 7.89 us -> 2.13 us  [the longest x4 2.13 us: body(): other = lax.ppermute(known, 'leaf', [(i, i ^ step) for i in range(nodes)])]
    concatenate x3 -> x1, other arithmetic: 2.07 us -> 0.01 us  [body(): known = jnp.concatenate([known, other], axis=0)]
    ppermute x6, starting transfers between devices: 14.9 us -> 13.7 us  [the longest x4 8.69 us: body(): other = lax.ppermute(known, 'leaf', [(i, i ^ step) for i in range(nodes)])]
    unnamed x28 -> x33, local copies, waits for them, and re-layouts: 4.54 us -> 4.13 us
    pallas_call x2 -> x4, Pallas kernels: 10.8 us -> 10.6 us  [the longest x2 6.19 us: fields(): pl.pallas_call(functools.partial(field_kernel, first), out_shape=(jax.Sha...]
  transfers between devices with their start and end apart: 9 -> 9, of which waited for: 5 -> 2; matrix products, arithmetic and copies ran while one was open for 8% -> 2% of each run, Pallas kernels for 5% -> 29%
where the time goes in v2:
time: 36.8 us; the launch traced here: 36.4 us
  starting transfers between devices  14.3 us (39%)
  Pallas kernels  13.7 us (37%)
  local copies, waits for them, and re-layouts  4.14 us (11%)
  waiting for transfers between devices  3.3 us (9%)
  other arithmetic  0.71 us (2%)
    ppermute x4, starting transfers between devices, body(): other = lax.ppermute(known, 'leaf', [(i, i ^ step) for i in range(nodes)])  8.69 us
    pallas_call x2, Pallas kernels, fields(): pl.pallas_call(functools.partial(field_kernel, first), out_shape=(jax.Sha...  6.19 us
    ppermute x1, starting transfers between devices, body(): pair = lax.ppermute(pack, 'leaf', [(i, i ^ 1) for i in range(nodes)])  4.39 us
    unnamed x33, local copies, waits for them, and re-layouts  4.13 us
    pallas_call x1, Pallas kernels, body(): pl.pallas_call(down_kernel, out_shape=jax.ShapeDtypeStruct((leaves, colum...  3.18 us
    pallas_call x1, Pallas kernels, body(): pl.pallas_call(pack_kernel, out_shape=(pltpu.VMEM((tiles, columns, 128),...  2.75 us
    ppermute x4, waiting for transfers between devices, body(): other = lax.ppermute(known, 'leaf', [(i, i ^ step) for i in range(nodes)])  2.13 us
    pallas_call x1, Pallas kernels, body(): pl.pallas_call(up_kernel, out_shape=(pltpu.VMEM((leaves, columns, rank),...  1.63 us
  transfers between devices with their start and end apart: 9, of which 2 were waited for; matrix products, arithmetic and copies ran while one was open for 2% of the time, Pallas kernels for 29%

profile of v2, /device:TPU:0, one launch (start us, length us, event | category | flops | bytes accessed | tf_op | source)
XLA Modules:
  0.0 36.4 jit_solution(13543610095256167827)
XLA Ops:
  0.0 0.5 %collective-permute-start.7 = (bf16[8,3,256,256]{3,2,1,0:T(8,128)(2,1)}, bf16[8,3,256,256]{3,2,1,0:T(8,128)(2,1)}, u32[]{:S(2)}, u32[]{:S(2)}) collective-permute-start(bf16[8,3,256,256]{3,2,1,0:T(8,128)(2,1)} %near.1), channel_id=1, source_target_pairs={{0,1},{1,0},{2,3},{3,2},{4,5},{5,4},{6,7},{7,6},{8,9},{9,8},{10,11... | collective-permute-start | bytes 9437192 | tf_op jit(solution)/shard_map/ppermute | solution.py:173
  0.5 0.1 collective-permute-start.1
  0.5 1.6 %up.1 = (bf16[8,16,64]{2,1,0:T(8,128)(2,1)S(1)}, bf16[16,128]{1,0:T(8,128)(2,1)S(1)}) custom-call(bf16[8,16,256]{2,1,0:T(8,128)(2,1)} %bitcast.13, bf16[8,64,256]{2,1,0:T(8,128)(2,1)} %bitcast.15, bf16[8,64,64]{2,1,0:T(8,128)(2,1)} %leaf_up.1, bf16[1,64,64]{2,1,0:T(8,128)(2,1)} %node_up.1), custom_call_target="tpu_custom_call" | custom-call | tf_op jit(solution)/shard_map/up/pallas_call | solution.py:179
  2.1 0.0 copy-start.11
  2.1 0.6 %copy-done.11 = bf16[8,16,64]{2,1,0:T(8,128)(2,1)} copy-done((bf16[8,16,64]{2,1,0:T(8,128)(2,1)}, bf16[8,16,64]{2,1,0:T(8,128)(2,1)S(1)}, u32[]{:S(2)}) %copy-start.11) | copy-done | bytes 16408
  2.8 2.9 %collective-permute-start = (bf16[1,16,128]{2,1,0:T(8,128)(2,1)S(1)}, bf16[1,16,128]{2,1,0:T(8,128)(2,1)S(1)}, u32[]{:S(2)}, u32[]{:S(2)}) collective-permute-start(bf16[1,16,128]{2,1,0:T(8,128)(2,1)S(1)} %bitcast.9), channel_id=1, source_target_pairs={{0,2},{2,0},{4,6},{6,4},{8,10},{10,8},{12,14},{14,12},{16,18},{18,... | collective-permute-start | bytes 12296 | tf_op jit(solution)/shard_map/ppermute | solution.py:240
  5.7 0.7 %pad_add_fusion.lists = s32[6,8]{1,0:T(8,128)S(1)} fusion(s32[3,8]{1,0:T(4,128)} %bitcast.16, s32[3,8]{1,0:T(4,128)} %bitcast.17), kind=kLoop, calls=%fused_computation.6 | loop fusion | flops 48 | bytes 384 | tf_op jit(solution)/shard_map/concatenate | solution.py:175
  6.4 0.0 collective-permute-start.2
  6.4 1.2 %collective-permute-done.2.__.lists_other = s32[6,8]{1,0:T(8,128)S(1)} collective-permute-done((s32[6,8]{1,0:T(8,128)S(1)}, s32[6,8]{1,0:T(8,128)S(1)}, u32[]{:S(2)}, u32[]{:S(2)}) %collective-permute-start.2) | collective-permute-done | bytes 224 | tf_op jit(solution)/shard_map/ppermute | solution.py:176
  7.6 0.0 copy-start.9
  7.6 0.0 collective-permute-done.1._.coup_other
  7.6 0.0 copy-start
  7.6 0.7 %copy-done = bf16[8,3,64,64]{3,2,1,0:T(8,128)(2,1)} copy-done((bf16[8,3,64,64]{3,2,1,0:T(8,128)(2,1)}, bf16[8,3,64,64]{3,2,1,0:T(8,128)(2,1)S(1)}, u32[]{:S(2)}) %copy-start) | copy-done | bytes 196632
  8.3 0.0 copy-done.9
  8.3 2.8 %pack.1 = (bf16[20,16,128]{2,1,0:T(8,128)(2,1)S(1)}, bf16[8,3,256,256]{3,2,1,0:T(8,128)(2,1)S(1)}) custom-call(bf16[8,16,256]{2,1,0:T(8,128)(2,1)} %bitcast.14, bf16[8,16,64]{2,1,0:T(8,128)(2,1)} %copy-done.11, bf16[8,3,256,256]{3,2,1,0:T(8,128)(2,1)} %near.1, bf16[8,3,64,64]{3,2,1,0:T(8,128)(2,1)} %copy-done, s32[6,8]{1,0:T(8,128)} %copy-done.9), custom_call_target="tpu_custom_call" | custom-call | tf_op jit(solution)/shard_map/pack/pallas_call | solution.py:190
  11.1 0.7 %collective-permute-start.6 = (bf16[20,16,128]{2,1,0:T(8,128)(2,1)S(1)}, bf16[20,16,128]{2,1,0:T(8,128)(2,1)S(1)}, u32[]{:S(2)}, u32[]{:S(2)}) collective-permute-start(bf16[20,16,128]{2,1,0:T(8,128)(2,1)S(1)} %get-tuple-element.25.own), channel_id=1, source_target_pairs={{2,4},{4,2},{6,8},{8,6},{10,12},{12,10},{14,16},{16,14},{18,20},{2... | collective-permute-start | bytes 245768 | tf_op jit(solution)/shard_map/ppermute | solution.py:206
  11.8 4.4 %collective-permute-start.5 = (bf16[20,16,128]{2,1,0:T(8,128)(2,1)S(1)}, bf16[20,16,128]{2,1,0:T(8,128)(2,1)S(1)}, u32[]{:S(2)}, u32[]{:S(2)}) collective-permute-start(bf16[20,16,128]{2,1,0:T(8,128)(2,1)S(1)} %get-tuple-element.25.own), channel_id=1, source_target_pairs={{0,2},{2,0},{4,6},{6,4},{8,10},{10,8},{12,14},{14,12},{16,18},{18,... | collective-permute-start | bytes 245768 | tf_op jit(solution)/shard_map/ppermute | solution.py:205
  16.1 0.0 collective-permute-done
  16.2 1.5 %collective-permute-start.3 = (bf16[2,16,128]{2,1,0:T(8,128)(2,1)S(1)}, bf16[2,16,128]{2,1,0:T(8,128)(2,1)S(1)}, u32[]{:S(2)}, u32[]{:S(2)}) collective-permute-start(bf16[2,16,128]{2,1,0:T(8,128)(2,1)S(1)} %pad_maximum_fusion), channel_id=1, source_target_pairs={{0,4},{2,6},{4,0},{6,2},{8,12},{10,14},{12,8},{14,10},{16,20},{18,... | collective-permute-start | bytes 24584 | tf_op jit(solution)/shard_map/ppermute | solution.py:240
  17.7 2.1 %collective-permute-done.3 = bf16[2,16,128]{2,1,0:T(8,128)(2,1)S(1)} collective-permute-done((bf16[2,16,128]{2,1,0:T(8,128)(2,1)S(1)}, bf16[2,16,128]{2,1,0:T(8,128)(2,1)S(1)}, u32[]{:S(2)}, u32[]{:S(2)}) %collective-permute-start.3) | collective-permute-done | bytes 8224 | tf_op jit(solution)/shard_map/ppermute | solution.py:240
  19.8 1.6 %collective-permute-start.4 = (bf16[4,16,128]{2,1,0:T(8,128)(2,1)S(1)}, bf16[4,16,128]{2,1,0:T(8,128)(2,1)S(1)}, u32[]{:S(2)}, u32[]{:S(2)}) collective-permute-start(bf16[4,16,128]{2,1,0:T(8,128)(2,1)S(1)} %constant_dynamic-update-slice_fusion._), channel_id=1, source_target_pairs={{0,8},{2,10},{4,12},{6,14},{8,0},{10,2},{12,4},{14,6},{16,24},{18,... | collective-permute-start | bytes 49160 | tf_op jit(solution)/shard_map/ppermute | solution.py:240
  21.4 0.0 collective-permute-done.6.cross
  21.4 0.0 collective-permute-done.5.pair
  21.4 0.0 collective-permute-done.7.near_other
  21.4 0.0 copy-start.1
  21.4 1.0 %copy-done.1 = bf16[8,3,64,64]{3,2,1,0:T(8,128)(2,1)S(1)} copy-done((bf16[8,3,64,64]{3,2,1,0:T(8,128)(2,1)S(1)}, bf16[8,3,64,64]{3,2,1,0:T(8,128)(2,1)}, u32[]{:S(2)}) %copy-start.1) | copy-done | bytes 196632
  22.4 0.0 copy-start.2
  22.4 1.0 %copy-done.2 = bf16[8,3,64,64]{3,2,1,0:T(8,128)(2,1)S(1)} copy-done((bf16[8,3,64,64]{3,2,1,0:T(8,128)(2,1)S(1)}, bf16[8,3,64,64]{3,2,1,0:T(8,128)(2,1)}, u32[]{:S(2)}) %copy-start.2) | copy-done | bytes 196632
  23.4 0.0 copy-start.10
  23.4 0.7 %copy-done.10 = s32[6,8]{1,0:T(8,128)S(1)} copy-done((s32[6,8]{1,0:T(8,128)S(1)}, s32[6,8]{1,0:T(8,128)}, u32[]{:S(2)}) %copy-start.10) | copy-done | bytes 216
  24.1 3.1 %fields.2 = (f32[4,16,256]{2,1,0:T(8,128)S(1)}, f32[4,16,64]{2,1,0:T(8,128)S(1)}) custom-call(s32[6,8]{1,0:T(8,128)S(1)} %pad_add_fusion.lists, s32[6,8]{1,0:T(8,128)S(1)} %copy-done.10, bf16[20,16,128]{2,1,0:T(8,128)(2,1)S(1)} %collective-permute-done.5.pair, bf16[20,16,128]{2,1,0:T(8,128)(2,1)S(1)} %get-tuple-element.25.own, ...), custom_call_target="tpu_custom_call" | custom-call | flops 805306368 | bytes 3145728 | tf_op jit(solution)/shard_map/fields/pallas_call | solution.py:212
  27.2 0.0 collective-permute-done.4
  27.2 0.0 copy-start.3
  27.2 0.0 copy-start.4
  27.2 0.0 copy-start.5
  27.2 0.0 copy-start.6
  27.3 0.0 copy-start.7
  27.3 0.0 copy-start.8
  27.3 0.0 copy-start.12
  27.3 0.0 copy-start.13
  27.3 0.0 copy-start.14
  27.3 2.7 %collective-permute-start.8 = (bf16[8,16,128]{2,1,0:T(8,128)(2,1)S(1)}, bf16[8,16,128]{2,1,0:T(8,128)(2,1)S(1)}, u32[]{:S(2)}, u32[]{:S(2)}) collective-permute-start(bf16[8,16,128]{2,1,0:T(8,128)(2,1)S(1)} %constant_dynamic-update-slice_fusion.3._.known), channel_id=1, source_target_pairs={{0,16},{2,18},{4,20},{6,22},{8,24},{10,26},{12,28},{14,30},{16,0},... | collective-permute-start | bytes 98312 | tf_op jit(solution)/shard_map/ppermute | solution.py:240
  30.0 3.1 %fields.3 = (f32[4,16,256]{2,1,0:T(8,128)S(1)}, f32[4,16,64]{2,1,0:T(8,128)S(1)}) custom-call(s32[6,8]{1,0:T(8,128)S(1)} %pad_add_fusion.lists, s32[6,8]{1,0:T(8,128)S(1)} %copy-done.10, bf16[20,16,128]{2,1,0:T(8,128)(2,1)S(1)} %collective-permute-done.5.pair, bf16[20,16,128]{2,1,0:T(8,128)(2,1)S(1)} %get-tuple-element.25.own, ...), custom_call_target="tpu_custom_call" | custom-call | flops 805306368 | bytes 3145728 | tf_op jit(solution)/shard_map/fields/pallas_call | solution.py:212
  33.1 0.0 collective-permute-done.8.other
  33.1 0.0 copy-done.3
  33.1 0.0 copy-done.4
  33.1 0.0 copy-done.5
  33.1 0.0 copy-done.6
  33.1 0.0 copy-done.7
  33.1 0.0 copy-done.8
  33.1 0.0 copy-done.12
  33.2 0.0 copy-done.13
  33.2 0.0 copy-done.14
  33.2 3.2 %down.1 = bf16[8,16,256]{2,1,0:T(8,128)(2,1)} custom-call(s32[1,4]{1,0:T(1,128)S(1)} %copy-done.14, s32[4,14]{1,0:T(4,128)S(1)} %bitcast.12, bf16[8,16,128]{2,1,0:T(8,128)(2,1)S(1)} %constant_dynamic-update-slice_fusion.3._.known, bf16[8,16,128]{2,1,0:T(8,128)(2,1)S(1)} %collective-permute-done.8.other, f32[4,16,256]{2,1,0:T(8,128)S(1)} %get-tuple-element.31.near, ...), custom_call_target="tpu_custom_call" | custom-call | tf_op jit(solution)/shard_map/down/pallas_call | solution.py:251
  (6 shorter events, 0.0 us)
Async XLA Ops:
  0.0 21.4 %collective-permute-start.7 = (bf16[8,3,256,256]{3,2,1,0:T(8,128)(2,1)}, bf16[8,3,256,256]{3,2,1,0:T(8,128)(2,1)}, u32[]{:S(2)}, u32[]{:S(2)}) collective-permute-start(bf16[8,3,256,256]{3,2,1,0:T(8,128)(2,1)} %near.1), channel_id=1, source_target_pairs={{0,1},{1,0},{2,3},{3,2},{4,5},{5,4},{6,7},{7,6},{8,9},{9,8},{10,11... | collective-permute-start | bytes 9437192 | tf_op jit(solution)/shard_map/ppermute | solution.py:173
  0.5 7.1 %collective-permute-start.1 = (bf16[8,3,64,64]{3,2,1,0:T(8,128)(2,1)}, bf16[8,3,64,64]{3,2,1,0:T(8,128)(2,1)S(1)}, u32[]{:S(2)}, u32[]{:S(2)}) collective-permute-start(bf16[8,3,64,64]{3,2,1,0:T(8,128)(2,1)} %coup.3), channel_id=1, source_target_pairs={{0,1},{1,0},{2,3},{3,2},{4,5},{5,4},{6,7},{7,6},{8,9},{9,8},{10,11... | collective-permute-start | bytes 589832 | tf_op jit(solution)/shard_map/ppermute | solution.py:174
  2.1 0.6 %copy-start.11 = (bf16[8,16,64]{2,1,0:T(8,128)(2,1)}, bf16[8,16,64]{2,1,0:T(8,128)(2,1)S(1)}, u32[]{:S(2)}) copy-start(bf16[8,16,64]{2,1,0:T(8,128)(2,1)S(1)} %get-tuple-element.21.coeff) | copy-start | bytes 49156
  2.8 13.4 %collective-permute-start = (bf16[1,16,128]{2,1,0:T(8,128)(2,1)S(1)}, bf16[1,16,128]{2,1,0:T(8,128)(2,1)S(1)}, u32[]{:S(2)}, u32[]{:S(2)}) collective-permute-start(bf16[1,16,128]{2,1,0:T(8,128)(2,1)S(1)} %bitcast.9), channel_id=1, source_target_pairs={{0,2},{2,0},{4,6},{6,4},{8,10},{10,8},{12,14},{14,12},{16,18},{18,... | collective-permute-start | bytes 12296 | tf_op jit(solution)/shard_map/ppermute | solution.py:240
  6.4 1.2 %collective-permute-start.2 = (s32[6,8]{1,0:T(8,128)S(1)}, s32[6,8]{1,0:T(8,128)S(1)}, u32[]{:S(2)}, u32[]{:S(2)}) collective-permute-start(s32[6,8]{1,0:T(8,128)S(1)} %pad_add_fusion.lists), channel_id=1, source_target_pairs={{0,1},{1,0},{2,3},{3,2},{4,5},{5,4},{6,7},{7,6},{8,9},{9,8},{10,11... | collective-permute-start | bytes 584 | tf_op jit(solution)/shard_map/ppermute | solution.py:176
  7.6 0.8 %copy-start.9 = (s32[6,8]{1,0:T(8,128)}, s32[6,8]{1,0:T(8,128)S(1)}, u32[]{:S(2)}) copy-start(s32[6,8]{1,0:T(8,128)S(1)} %collective-permute-done.2.__.lists_other) | copy-start | bytes 580
  7.6 0.7 %copy-start = (bf16[8,3,64,64]{3,2,1,0:T(8,128)(2,1)}, bf16[8,3,64,64]{3,2,1,0:T(8,128)(2,1)S(1)}, u32[]{:S(2)}) copy-start(bf16[8,3,64,64]{3,2,1,0:T(8,128)(2,1)S(1)} %collective-permute-done.1._.coup_other) | copy-start | bytes 589828
  11.1 10.3 %collective-permute-start.6 = (bf16[20,16,128]{2,1,0:T(8,128)(2,1)S(1)}, bf16[20,16,128]{2,1,0:T(8,128)(2,1)S(1)}, u32[]{:S(2)}, u32[]{:S(2)}) collective-permute-start(bf16[20,16,128]{2,1,0:T(8,128)(2,1)S(1)} %get-tuple-element.25.own), channel_id=1, source_target_pairs={{2,4},{4,2},{6,8},{8,6},{10,12},{12,10},{14,16},{16,14},{18,20},{2... | collective-permute-start | bytes 245768 | tf_op jit(solution)/shard_map/ppermute | solution.py:206
  11.8 9.6 %collective-permute-start.5 = (bf16[20,16,128]{2,1,0:T(8,128)(2,1)S(1)}, bf16[20,16,128]{2,1,0:T(8,128)(2,1)S(1)}, u32[]{:S(2)}, u32[]{:S(2)}) collective-permute-start(bf16[20,16,128]{2,1,0:T(8,128)(2,1)S(1)} %get-tuple-element.25.own), channel_id=1, source_target_pairs={{0,2},{2,0},{4,6},{6,4},{8,10},{10,8},{12,14},{14,12},{16,18},{18,... | collective-permute-start | bytes 245768 | tf_op jit(solution)/shard_map/ppermute | solution.py:205
  16.2 3.7 %collective-permute-start.3 = (bf16[2,16,128]{2,1,0:T(8,128)(2,1)S(1)}, bf16[2,16,128]{2,1,0:T(8,128)(2,1)S(1)}, u32[]{:S(2)}, u32[]{:S(2)}) collective-permute-start(bf16[2,16,128]{2,1,0:T(8,128)(2,1)S(1)} %pad_maximum_fusion), channel_id=1, source_target_pairs={{0,4},{2,6},{4,0},{6,2},{8,12},{10,14},{12,8},{14,10},{16,20},{18,... | collective-permute-start | bytes 24584 | tf_op jit(solution)/shard_map/ppermute | solution.py:240
  19.8 7.4 %collective-permute-start.4 = (bf16[4,16,128]{2,1,0:T(8,128)(2,1)S(1)}, bf16[4,16,128]{2,1,0:T(8,128)(2,1)S(1)}, u32[]{:S(2)}, u32[]{:S(2)}) collective-permute-start(bf16[4,16,128]{2,1,0:T(8,128)(2,1)S(1)} %constant_dynamic-update-slice_fusion._), channel_id=1, source_target_pairs={{0,8},{2,10},{4,12},{6,14},{8,0},{10,2},{12,4},{14,6},{16,24},{18,... | collective-permute-start | bytes 49160 | tf_op jit(solution)/shard_map/ppermute | solution.py:240
  21.4 1.0 %copy-start.1 = (bf16[8,3,64,64]{3,2,1,0:T(8,128)(2,1)S(1)}, bf16[8,3,64,64]{3,2,1,0:T(8,128)(2,1)}, u32[]{:S(2)}) copy-start(bf16[8,3,64,64]{3,2,1,0:T(8,128)(2,1)} %copy-done) | copy-start | bytes 589828
  22.4 1.0 %copy-start.2 = (bf16[8,3,64,64]{3,2,1,0:T(8,128)(2,1)S(1)}, bf16[8,3,64,64]{3,2,1,0:T(8,128)(2,1)}, u32[]{:S(2)}) copy-start(bf16[8,3,64,64]{3,2,1,0:T(8,128)(2,1)} %coup.3) | copy-start | bytes 589828
  23.4 0.7 %copy-start.10 = (s32[6,8]{1,0:T(8,128)S(1)}, s32[6,8]{1,0:T(8,128)}, u32[]{:S(2)}) copy-start(s32[6,8]{1,0:T(8,128)} %copy-done.9) | copy-start | bytes 580
  27.2 5.9 %copy-start.3 = (bf16[14,4,64,64]{3,2,1,0:T(8,128)(2,1)S(1)}, bf16[14,4,64,64]{3,2,1,0:T(8,128)(2,1)}, u32[]{:S(2)}) copy-start(bf16[14,4,64,64]{3,2,1,0:T(8,128)(2,1)} %upper_coup.1) | copy-start | bytes 1376260
  27.2 5.9 %copy-start.4 = (bf16[8,256,64]{1,2,0:T(8,128)(2,1)S(1)}, bf16[8,256,64]{1,2,0:T(8,128)(2,1)}, u32[]{:S(2)}) copy-start(bf16[8,256,64]{1,2,0:T(8,128)(2,1)} %param.21) | copy-start | bytes 786436
  27.2 5.9 %copy-start.5 = (bf16[12,64,64]{2,1,0:T(8,128)(2,1)S(1)}, bf16[12,64,64]{2,1,0:T(8,128)(2,1)}, u32[]{:S(2)}) copy-start(bf16[12,64,64]{2,1,0:T(8,128)(2,1)} %upper_up.1) | copy-start | bytes 294916
  27.2 5.9 %copy-start.6 = (bf16[12,64,64]{2,1,0:T(8,128)(2,1)S(1)}, bf16[12,64,64]{2,1,0:T(8,128)(2,1)}, u32[]{:S(2)}) copy-start(bf16[12,64,64]{2,1,0:T(8,128)(2,1)} %upper_down.1) | copy-start | bytes 294916
  27.3 5.9 %copy-start.7 = (bf16[8,64,64]{2,1,0:T(8,128)(2,1)S(1)}, bf16[8,64,64]{2,1,0:T(8,128)(2,1)}, u32[]{:S(2)}) copy-start(bf16[8,64,64]{2,1,0:T(8,128)(2,1)} %leaf_down.1) | copy-start | bytes 196612
  27.3 5.9 %copy-start.8 = (bf16[1,4,64,64]{3,2,1,0:T(8,128)(2,1)S(1)}, bf16[1,4,64,64]{3,2,1,0:T(8,128)(2,1)}, u32[]{:S(2)}) copy-start(bf16[1,4,64,64]{3,2,1,0:T(8,128)(2,1)} %node_coup.1) | copy-start | bytes 98308
  27.3 5.9 %copy-start.12 = (bf16[1,64,64]{2,1,0:T(8,128)(2,1)S(1)}, bf16[1,64,64]{2,1,0:T(8,128)(2,1)}, u32[]{:S(2)}) copy-start(bf16[1,64,64]{2,1,0:T(8,128)(2,1)} %node_down.1) | copy-start | bytes 24580
  27.3 5.9 %copy-start.13 = (s32[14,4]{0,1:T(4,128)S(1)}, s32[14,4]{0,1:T(4,128)}, u32[]{:S(2)}) copy-start(s32[14,4]{0,1:T(4,128)} %param.31) | copy-start | bytes 676
  27.3 5.9 %copy-start.14 = (s32[1,4]{1,0:T(1,128)S(1)}, s32[1,4]{1,0:T(1,128)}, u32[]{:S(2)}) copy-start(s32[1,4]{1,0:T(1,128)} %node_list.1) | copy-start | bytes 52
  27.3 5.8 %collective-permute-start.8 = (bf16[8,16,128]{2,1,0:T(8,128)(2,1)S(1)}, bf16[8,16,128]{2,1,0:T(8,128)(2,1)S(1)}, u32[]{:S(2)}, u32[]{:S(2)}) collective-permute-start(bf16[8,16,128]{2,1,0:T(8,128)(2,1)S(1)} %constant_dynamic-update-slice_fusion.3._.known), channel_id=1, source_target_pairs={{0,16},{2,18},{4,20},{6,22},{8,24},{10,26},{12,28},{14,30},{16,0},... | collective-permute-start | bytes 98312 | tf_op jit(solution)/shard_map/ppermute | solution.py:240

commit v3 on v2

--- a/solution.py
+++ b/solution.py
@@ -13,6 +13,10 @@
 
 def mm(a, b, dims):
     return lax.dot_general(a, b, dims, preferred_element_type=jnp.float32)
+
+
+def pinned(x, space):
+    return pltpu.with_memory_space_constraint(x, space)
 
 
 def vmem():
@@ -41,9 +45,13 @@
     message[:, rank:] = mm(node, node_up[0], PLAIN).astype(jnp.bfloat16)
 
 
-def pack_kernel(dens, coeff, near, _, __, pack, near_out, sem):
-    copy = pltpu.make_async_copy(near, near_out, sem)
-    copy.start()
+def pack_kernel(dens, coeff, coup, near_list, far_list, pack, *rest):
+    copies = [
+        pltpu.make_async_copy(source, target, rest[3].at[k])
+        for k, (source, target) in enumerate(zip((coup, near_list, far_list), rest[:3]))
+    ]
+    for copy in copies:
+        copy.start()
     leaves, _, points = dens.shape
     rank = coeff.shape[2]
     halves = points // 128
@@ -53,18 +61,24 @@
             pack[t * halves + h] = here[:, h * 128 : (h + 1) * 128]
         side = t % 2
         pack[leaves * halves + t // 2, :, side * rank : (side + 1) * rank] = coeff[t]
-    copy.wait()
+    for copy in copies:
+        copy.wait()
 
 
 def field_kernel(
-    first, lists, lists_other, pair, own, cross, near, near_other, coup, coup_other, _,
-    near_out, far_out, ext, ext_coeff,
+    first, near_list, far_list, near_list_other, far_list_other, pair, own, cross,
+    coup, coup_other, near, near_other, near_out, far_out, ext, ext_coeff, blocks, sems,
 ):
     leaves, entries = near.shape[0], near.shape[1]
     count = near_out.shape[0]
     rank = coup.shape[-1]
     points = near.shape[-1]
     halves = points // 128
+    copies = []
+    for k in range(count):
+        copy = pltpu.make_async_copy(near.at[first + k], blocks.at[k], sems.at[k])
+        copy.start()
+        copies.append(copy)
     me = lax.axis_index("leaf")
     odd = me & 1
     for slot, ref in ((2 - 2 * odd, pair), (1, own), (2 * odd, cross)):
@@ -77,19 +91,26 @@
             ]
     offset = (me - 1) * leaves
     for k in range(count):
-        t = first + k
         total = None
-        for table, matrices in ((lists, coup), (lists_other, coup_other)):
+        for table, matrices in ((far_list, coup), (far_list_other, coup_other)):
             for j in range(entries):
-                source = ext_coeff[table[entries + j, t] - offset]
-                term = mm(source, matrices[t, j], LAST)
+                source = ext_coeff[table[j, first + k] - offset]
+                term = mm(source, matrices[first + k, j], LAST)
                 total = term if total is None else total + term
         far_out[k] = total
+    for k in range(count):
         total = None
-        for table, blocks in ((lists, near), (lists_other, near_other)):
-            for j in range(entries):
-                term = mm(ext[table[j, t] - offset], blocks[t, j], LAST)
-                total = term if total is None else total + term
+        for j in range(entries):
+            source = ext[near_list_other[j, first + k] - offset]
+            term = mm(source, near_other[first + k, j], LAST)
+            total = term if total is None else total + term
+        near_out[k] = total
+    for k in range(count):
+        copies[k].wait()
+        total = near_out[k]
+        for j in range(entries):
+            source = ext[near_list[j, first + k] - offset]
+            total = total + mm(source, blocks[k, j], LAST)
         near_out[k] = total
 
 
@@ -172,8 +193,9 @@
 
     near_other = lax.ppermute(near_blocks, "sub", swap)
     coup_other = lax.ppermute(leaf_coupling, "sub", swap)
-    lists = jnp.concatenate([near_index.T, leaf_list.T], axis=0)
-    lists_other = lax.ppermute(lists, "sub", swap)
+    near_list, far_list = near_index.T, leaf_list.T
+    near_list_other = lax.ppermute(near_list, "sub", swap)
+    far_list_other = lax.ppermute(far_list, "sub", swap)
 
     dens = jnp.swapaxes(density, 1, 2)
     coeff, message = pl.pallas_call(
@@ -187,64 +209,75 @@
         name="up",
     )(dens, jnp.swapaxes(col_basis, 1, 2), leaf_up, node_up)
     tiles = leaves * (points // 128) + leaves // 2
-    pack, near_here = pl.pallas_call(
+    hbm, fast = pltpu.HBM, pltpu.VMEM
+    pack, coup_here, near_list, far_list = pl.pallas_call(
         pack_kernel,
         out_shape=(
             pltpu.VMEM((tiles, columns, 128), bf16),
-            pltpu.VMEM(near_blocks.shape, bf16),
+            pltpu.VMEM(leaf_coupling.shape, bf16),
+            pltpu.VMEM(near_list.shape, near_list.dtype),
+            pltpu.VMEM(far_list.shape, far_list.dtype),
         ),
         in_specs=[vmem()] * 2 + [anywhere()] * 3,
-        out_specs=(vmem(), vmem()),
-        scratch_shapes=[pltpu.SemaphoreType.DMA],
+        out_specs=(vmem(),) * 4,
+        scratch_shapes=[pltpu.SemaphoreType.DMA((3,))],
         name="pack",
     )(
-        dens, coeff, pltpu.with_memory_space_constraint(near_blocks, pltpu.HBM), coup_other,
-        lists_other,
+        pinned(dens, hbm), pinned(coeff, fast), pinned(leaf_coupling, hbm),
+        pinned(near_list, hbm), pinned(far_list, hbm),
     )
-    inner = [(i, (i + 1 if i % 2 else i - 1)) for i in range(1, nodes - 1)]
     pair = lax.ppermute(pack, "leaf", [(i, i ^ 1) for i in range(nodes)])
-    cross = lax.ppermute(pack, "leaf", inner + [(0, 0), (nodes - 1, nodes - 1)])
+    others = [(i, (i + 1 if i % 2 else i - 1) % nodes) for i in range(nodes)]
 
     entries = near_blocks.shape[1]
     half = leaves // 2
 
-    def fields(first, after):
+    def fields(first):
+        operands = [near_list, far_list, near_list_other, far_list_other]
+        operands += [pair, pack, cross, coup_here, coup_other]
+        operands = [pinned(x, fast) for x in operands]
+        operands += [pinned(near_blocks, hbm), pinned(near_other, fast)]
         return pl.pallas_call(
             functools.partial(field_kernel, first),
             out_shape=(
-                jax.ShapeDtypeStruct((half, columns, points), f32),
-                jax.ShapeDtypeStruct((half, columns, rank), f32),
+                pltpu.VMEM((half, columns, points), f32),
+                pltpu.VMEM((half, columns, rank), f32),
             ),
-            in_specs=[smem()] * 2 + [vmem()] * 7 + [anywhere()],
+            in_specs=[smem()] * 4 + [vmem()] * 5 + [anywhere(), vmem()],
             out_specs=(vmem(), vmem()),
             scratch_shapes=[
                 pltpu.VMEM((3 * leaves, columns, points), bf16),
                 pltpu.VMEM((3 * leaves, columns, rank), bf16),
+                pltpu.VMEM((half, entries, points, points), bf16),
+                pltpu.SemaphoreType.DMA((half,)),
             ],
-            compiler_params=pltpu.CompilerParams(vmem_limit_bytes=24 * 1024 * 1024),
+            compiler_params=pltpu.CompilerParams(vmem_limit_bytes=16 * 1024 * 1024),
             cost_estimate=pl.CostEstimate(
                 flops=2 * half * 2 * entries * points * points * 256,
                 bytes_accessed=half * 2 * entries * points * points * 2,
                 transcendentals=0,
             ),
             name="fields",
-        )(
-            lists, lists_other, pair, pack, cross, near_here, near_other, leaf_coupling,
-            coup_other, after,
-        )
+        )(*operands)
 
     known = message[None]
-    near = far = near_late = far_late = None
     for bit in range(levels):
         step = 1 << bit
         other = lax.ppermute(known, "leaf", [(i, i ^ step) for i in range(nodes)])
         if bit == 0:
             known, other, pack = lax.optimization_barrier((known, other, pack))
+            cross = lax.ppermute(pack, "leaf", others)
+        if bit == 1:
+            known, other, coup_other, near_list_other, far_list_other = lax.optimization_barrier(
+                (known, other, coup_other, near_list_other, far_list_other)
+            )
         if bit == levels - 2:
-            near, far = fields(0, known)
+            known, cross = lax.optimization_barrier((known, cross))
+            near, far = fields(0)
             known, other, near, far = lax.optimization_barrier((known, other, near, far))
         if bit == levels - 1:
-            near_late, far_late = fields(half, known)
+            known, cross = lax.optimization_barrier((known, cross))
+            near_late, far_late = fields(half)
         else:
             known = jnp.concatenate([known, other], axis=0)
 

time: 36.8 us -> 32.5 us (0.88)
  local copies, waits for them, and re-layouts: 4.14 us -> 0.09 us
  starting transfers between devices: 14.3 us -> 11 us
  waiting for transfers between devices: 3.3 us -> 5.39 us
  Pallas kernels: 13.7 us -> 15.4 us
  other arithmetic: 0.71 us -> 0 us
    ppermute x2 -> x3, waiting for transfers between devices: 1.16 us -> 5.37 us  [the longest x1 4.51 us: body(): cross = lax.ppermute(pack, 'leaf', others)]
    unnamed x33 -> x21, local copies, waits for them, and re-layouts: 4.13 us -> 0.06 us
    ppermute x4, starting transfers between devices: 8.69 us -> 4.84 us  [body(): other = lax.ppermute(known, 'leaf', [(i, i ^ step) for i in range(nodes)])]
    ppermute x2 -> x3, starting transfers between devices: 0.67 us -> 4.11 us  [the longest x1 3.6 us: body(): cross = lax.ppermute(pack, 'leaf', others)]
    ppermute x1, starting transfers between devices: 4.39 us -> 1.41 us  [body(): pair = lax.ppermute(pack, 'leaf', [(i, i ^ 1) for i in range(nodes)])]
    pallas_call x2, Pallas kernels: 6.19 us -> 8.76 us  [fields(): pl.pallas_call(functools.partial(field_kernel, first), out_shape=(pltpu.V...]
    ppermute x4, waiting for transfers between devices: 2.13 us -> 0.01 us  [body(): other = lax.ppermute(known, 'leaf', [(i, i ^ step) for i in range(nodes)])]
    pallas_call x1, Pallas kernels: 2.75 us -> 1.88 us  [body(): pl.pallas_call(pack_kernel, out_shape=(pltpu.VMEM((tiles, columns, 128),...]
  transfers between devices with their start and end apart: 9 -> 10, of which waited for: 2 -> 2; matrix products, arithmetic and copies ran while one was open for 2% -> 0% of each run, Pallas kernels for 29% -> 38%
where the time goes in v3:
time: 32.5 us; the launch traced here: 32.2 us
  Pallas kernels  15.4 us (47%)
  starting transfers between devices  11 us (34%)
  waiting for transfers between devices  5.39 us (17%)
    pallas_call x2, Pallas kernels, fields(): pl.pallas_call(functools.partial(field_kernel, first), out_shape=(pltpu.V...  8.76 us
    ppermute x4, starting transfers between devices, body(): other = lax.ppermute(known, 'leaf', [(i, i ^ step) for i in range(nodes)])  4.84 us
    ppermute x1, waiting for transfers between devices, body(): cross = lax.ppermute(pack, 'leaf', others)  4.51 us
    ppermute x1, starting transfers between devices, body(): cross = lax.ppermute(pack, 'leaf', others)  3.6 us
    pallas_call x1, Pallas kernels, body(): pl.pallas_call(down_kernel, out_shape=jax.ShapeDtypeStruct((leaves, colum...  3.18 us
    pallas_call x1, Pallas kernels, body(): pl.pallas_call(pack_kernel, out_shape=(pltpu.VMEM((tiles, columns, 128),...  1.88 us
    pallas_call x1, Pallas kernels, body(): pl.pallas_call(up_kernel, out_shape=(pltpu.VMEM((leaves, columns, rank),...  1.63 us
    ppermute x1, starting transfers between devices, body(): pair = lax.ppermute(pack, 'leaf', [(i, i ^ 1) for i in range(nodes)])  1.41 us
  transfers between devices with their start and end apart: 10, of which 2 were waited for; matrix products, arithmetic and copies ran while one was open for 0% of the time, Pallas kernels for 38%

profile of v3, /device:TPU:0, one launch (start us, length us, event | category | flops | bytes accessed | tf_op | source)
XLA Modules:
  0.0 32.2 jit_solution(565341018616746970)
XLA Ops:
  0.0 0.5 %collective-permute-start.8 = (bf16[8,3,256,256]{3,2,1,0:T(8,128)(2,1)}, bf16[8,3,256,256]{3,2,1,0:T(8,128)(2,1)}, u32[]{:S(2)}, u32[]{:S(2)}) collective-permute-start(bf16[8,3,256,256]{3,2,1,0:T(8,128)(2,1)} %near.3), channel_id=1, source_target_pairs={{0,1},{1,0},{2,3},{3,2},{4,5},{5,4},{6,7},{7,6},{8,9},{9,8},{10,11... | collective-permute-start | bytes 9437192 | tf_op jit(solution)/shard_map/ppermute | solution.py:194
  0.5 1.6 %up.1 = (bf16[8,16,64]{2,1,0:T(8,128)(2,1)S(1)}, bf16[16,128]{1,0:T(8,128)(2,1)S(1)}) custom-call(bf16[8,16,256]{2,1,0:T(8,128)(2,1)} %bitcast.13, bf16[8,64,256]{2,1,0:T(8,128)(2,1)} %bitcast.12, bf16[8,64,64]{2,1,0:T(8,128)(2,1)} %leaf_up.1, bf16[1,64,64]{2,1,0:T(8,128)(2,1)} %node_up.1), custom_call_target="tpu_custom_call" | custom-call | tf_op jit(solution)/shard_map/up/pallas_call | solution.py:201
  2.1 2.5 %collective-permute-start = (bf16[1,16,128]{2,1,0:T(8,128)(2,1)S(1)}, bf16[1,16,128]{2,1,0:T(8,128)(2,1)S(1)}, u32[]{:S(2)}, u32[]{:S(2)}) collective-permute-start(bf16[1,16,128]{2,1,0:T(8,128)(2,1)S(1)} %bitcast.9), channel_id=1, source_target_pairs={{0,2},{2,0},{4,6},{6,4},{8,10},{10,8},{12,14},{14,12},{16,18},{18,... | collective-permute-start | bytes 12296 | tf_op jit(solution)/shard_map/ppermute | solution.py:266
  4.6 0.2 collective-permute-start.2
  4.8 1.9 %pack.1 = (bf16[20,16,128]{2,1,0:T(8,128)(2,1)S(1)}, bf16[8,3,64,64]{3,2,1,0:T(8,128)(2,1)S(1)}, s32[3,8]{1,0:T(4,128)S(1)}, s32[3,8]{1,0:T(4,128)S(1)}) custom-call(bf16[8,16,256]{2,1,0:T(8,128)(2,1)} %bitcast.14, bf16[8,16,64]{2,1,0:T(8,128)(2,1)S(1)} %get-tuple-element.32.coeff, bf16[8,3,64,64]{3,2,1,0:T(8,128)(2,1)} %coup.1, s32[3,8]{1,0:T(4,128)} %bitcast.15, ...), custom_call_target="tpu_custom_call" | custom-call | tf_op jit(solution)/shard_map/pack/pallas_call | solution.py:213
  6.7 0.0 collective-permute-done
  6.7 1.6 %collective-permute-start.1 = (bf16[2,16,128]{2,1,0:T(8,128)(2,1)S(1)}, bf16[2,16,128]{2,1,0:T(8,128)(2,1)S(1)}, u32[]{:S(2)}, u32[]{:S(2)}) collective-permute-start(bf16[2,16,128]{2,1,0:T(8,128)(2,1)S(1)} %constant_dynamic-update-slice_fusion), channel_id=1, source_target_pairs={{0,4},{2,6},{4,0},{6,2},{8,12},{10,14},{12,8},{14,10},{16,20},{18,... | collective-permute-start | bytes 24584 | tf_op jit(solution)/shard_map/ppermute | solution.py:266
  8.3 0.0 collective-permute-start.3
  8.3 0.5 %collective-permute-start.4 = (s32[3,8]{1,0:T(4,128)}, s32[3,8]{1,0:T(4,128)S(1)}, u32[]{:S(2)}, u32[]{:S(2)}) collective-permute-start(s32[3,8]{1,0:T(4,128)} %bitcast.18), channel_id=1, source_target_pairs={{0,1},{1,0},{2,3},{3,2},{4,5},{5,4},{6,7},{7,6},{8,9},{9,8},{10,11... | collective-permute-start | bytes 296 | tf_op jit(solution)/shard_map/ppermute | solution.py:198
  8.8 0.9 %collective-permute-done.3.near_list_other = s32[3,8]{1,0:T(4,128)S(1)} collective-permute-done((s32[3,8]{1,0:T(4,128)}, s32[3,8]{1,0:T(4,128)S(1)}, u32[]{:S(2)}, u32[]{:S(2)}) %collective-permute-start.3) | collective-permute-done | bytes 128 | tf_op jit(solution)/shard_map/ppermute | solution.py:197
  9.7 1.4 %collective-permute-start.7 = (bf16[20,16,128]{2,1,0:T(8,128)(2,1)S(1)}, bf16[20,16,128]{2,1,0:T(8,128)(2,1)S(1)}, u32[]{:S(2)}, u32[]{:S(2)}) collective-permute-start(bf16[20,16,128]{2,1,0:T(8,128)(2,1)S(1)} %get-tuple-element.38.own), channel_id=1, source_target_pairs={{0,2},{2,0},{4,6},{6,4},{8,10},{10,8},{12,14},{14,12},{16,18},{18,... | collective-permute-start | bytes 245768 | tf_op jit(solution)/shard_map/ppermute | solution.py:229
  11.1 0.0 collective-permute-done.4.far_list_other
  11.1 3.6 %collective-permute-start.5 = (bf16[20,16,128]{2,1,0:T(8,128)(2,1)S(1)}, bf16[20,16,128]{2,1,0:T(8,128)(2,1)S(1)}, u32[]{:S(2)}, u32[]{:S(2)}) collective-permute-start(bf16[20,16,128]{2,1,0:T(8,128)(2,1)S(1)} %get-tuple-element.38.own), channel_id=1, source_target_pairs={{0,30},{2,4},{4,2},{6,8},{8,6},{10,12},{12,10},{14,16},{16,14},{18... | collective-permute-start | bytes 245768 | tf_op jit(solution)/shard_map/ppermute | solution.py:269
  14.7 0.0 collective-permute-done.1
  14.7 0.0 collective-permute-done.2.coup_other
  14.7 0.1 collective-permute-start.6
  14.8 4.5 %collective-permute-done.5.cross = bf16[20,16,128]{2,1,0:T(8,128)(2,1)S(1)} collective-permute-done((bf16[20,16,128]{2,1,0:T(8,128)(2,1)S(1)}, bf16[20,16,128]{2,1,0:T(8,128)(2,1)S(1)}, u32[]{:S(2)}, u32[]{:S(2)}) %collective-permute-start.5) | collective-permute-done | bytes 81952 | tf_op jit(solution)/shard_map/ppermute | solution.py:269
  19.3 0.0 collective-permute-done.7.pair
  19.3 0.0 collective-permute-done.8.near_other
  19.3 4.3 %fields.2 = (f32[4,16,256]{2,1,0:T(8,128)S(1)}, f32[4,16,64]{2,1,0:T(8,128)S(1)}) custom-call(s32[3,8]{1,0:T(4,128)S(1)} %get-tuple-element.40.near_list, s32[3,8]{1,0:T(4,128)S(1)} %get-tuple-element.41.far_list, s32[3,8]{1,0:T(4,128)S(1)} %collective-permute-done.3.near_list_other, s32[3,8]{1,0:T(4,128)S(1)} %collective-permute-done.4.far_list_other, ...), custom_call_target="tpu_custom_call" | custom-call | flops 805306368 | bytes 3145728 | tf_op jit(solution)/shard_map/fields/pallas_call | solution.py:240
  23.7 0.0 collective-permute-done.6
  23.7 0.0 copy-start
  23.7 0.0 copy-start.1
  23.7 0.0 copy-start.2
  23.7 0.0 copy-start.3
  23.7 0.0 copy-start.4
  23.8 0.0 copy-start.5
  23.8 0.0 copy-start.6
  23.8 0.0 copy-start.7
  23.8 0.0 copy-start.8
  23.8 0.7 %collective-permute-start.9 = (bf16[8,16,128]{2,1,0:T(8,128)(2,1)S(1)}, bf16[8,16,128]{2,1,0:T(8,128)(2,1)S(1)}, u32[]{:S(2)}, u32[]{:S(2)}) collective-permute-start(bf16[8,16,128]{2,1,0:T(8,128)(2,1)S(1)} %constant_dynamic-update-slice_fusion.4.known), channel_id=1, source_target_pairs={{0,16},{2,18},{4,20},{6,22},{8,24},{10,26},{12,28},{14,30},{16,0},... | collective-permute-start | bytes 98312 | tf_op jit(solution)/shard_map/ppermute | solution.py:266
  24.5 4.4 %fields.3 = (f32[4,16,256]{2,1,0:T(8,128)S(1)}, f32[4,16,64]{2,1,0:T(8,128)S(1)}) custom-call(s32[3,8]{1,0:T(4,128)S(1)} %get-tuple-element.40.near_list, s32[3,8]{1,0:T(4,128)S(1)} %get-tuple-element.41.far_list, s32[3,8]{1,0:T(4,128)S(1)} %collective-permute-done.3.near_list_other, s32[3,8]{1,0:T(4,128)S(1)} %collective-permute-done.4.far_list_other, ...), custom_call_target="tpu_custom_call" | custom-call | flops 805306368 | bytes 3145728 | tf_op jit(solution)/shard_map/fields/pallas_call | solution.py:240
  28.9 0.0 collective-permute-done.9.other
  28.9 0.0 copy-done
  28.9 0.0 copy-done.1
  28.9 0.0 copy-done.2
  29.0 0.0 copy-done.3
  29.0 0.0 copy-done.4
  29.0 0.0 copy-done.5
  29.0 0.0 copy-done.6
  29.0 0.0 copy-done.7
  29.0 0.0 copy-done.8
  29.0 3.2 %down.1 = bf16[8,16,256]{2,1,0:T(8,128)(2,1)} custom-call(s32[1,4]{1,0:T(1,128)S(1)} %copy-done.8, s32[4,14]{1,0:T(4,128)S(1)} %bitcast.11, bf16[8,16,128]{2,1,0:T(8,128)(2,1)S(1)} %constant_dynamic-update-slice_fusion.4.known, bf16[8,16,128]{2,1,0:T(8,128)(2,1)S(1)} %collective-permute-done.9.other, f32[4,16,256]{2,1,0:T(8,128)S(1)} %get-tuple-element.52.near, ...), custom_call_target="tpu_custom_call" | custom-call | tf_op jit(solution)/shard_map/down/pallas_call | solution.py:284
  (6 shorter events, 0.0 us)
Async XLA Ops:
  0.0 19.3 %collective-permute-start.8 = (bf16[8,3,256,256]{3,2,1,0:T(8,128)(2,1)}, bf16[8,3,256,256]{3,2,1,0:T(8,128)(2,1)}, u32[]{:S(2)}, u32[]{:S(2)}) collective-permute-start(bf16[8,3,256,256]{3,2,1,0:T(8,128)(2,1)} %near.3), channel_id=1, source_target_pairs={{0,1},{1,0},{2,3},{3,2},{4,5},{5,4},{6,7},{7,6},{8,9},{9,8},{10,11... | collective-permute-start | bytes 9437192 | tf_op jit(solution)/shard_map/ppermute | solution.py:194
  2.1 4.6 %collective-permute-start = (bf16[1,16,128]{2,1,0:T(8,128)(2,1)S(1)}, bf16[1,16,128]{2,1,0:T(8,128)(2,1)S(1)}, u32[]{:S(2)}, u32[]{:S(2)}) collective-permute-start(bf16[1,16,128]{2,1,0:T(8,128)(2,1)S(1)} %bitcast.9), channel_id=1, source_target_pairs={{0,2},{2,0},{4,6},{6,4},{8,10},{10,8},{12,14},{14,12},{16,18},{18,... | collective-permute-start | bytes 12296 | tf_op jit(solution)/shard_map/ppermute | solution.py:266
  4.6 10.1 %collective-permute-start.2 = (bf16[8,3,64,64]{3,2,1,0:T(8,128)(2,1)}, bf16[8,3,64,64]{3,2,1,0:T(8,128)(2,1)S(1)}, u32[]{:S(2)}, u32[]{:S(2)}) collective-permute-start(bf16[8,3,64,64]{3,2,1,0:T(8,128)(2,1)} %coup.1), channel_id=1, source_target_pairs={{0,1},{1,0},{2,3},{3,2},{4,5},{5,4},{6,7},{7,6},{8,9},{9,8},{10,11... | collective-permute-start | bytes 589832 | tf_op jit(solution)/shard_map/ppermute | solution.py:195
  6.7 8.0 %collective-permute-start.1 = (bf16[2,16,128]{2,1,0:T(8,128)(2,1)S(1)}, bf16[2,16,128]{2,1,0:T(8,128)(2,1)S(1)}, u32[]{:S(2)}, u32[]{:S(2)}) collective-permute-start(bf16[2,16,128]{2,1,0:T(8,128)(2,1)S(1)} %constant_dynamic-update-slice_fusion), channel_id=1, source_target_pairs={{0,4},{2,6},{4,0},{6,2},{8,12},{10,14},{12,8},{14,10},{16,20},{18,... | collective-permute-start | bytes 24584 | tf_op jit(solution)/shard_map/ppermute | solution.py:266
  8.3 1.4 %collective-permute-start.3 = (s32[3,8]{1,0:T(4,128)}, s32[3,8]{1,0:T(4,128)S(1)}, u32[]{:S(2)}, u32[]{:S(2)}) collective-permute-start(s32[3,8]{1,0:T(4,128)} %bitcast.16), channel_id=1, source_target_pairs={{0,1},{1,0},{2,3},{3,2},{4,5},{5,4},{6,7},{7,6},{8,9},{9,8},{10,11... | collective-permute-start | bytes 296 | tf_op jit(solution)/shard_map/ppermute | solution.py:197
  8.3 2.8 %collective-permute-start.4 = (s32[3,8]{1,0:T(4,128)}, s32[3,8]{1,0:T(4,128)S(1)}, u32[]{:S(2)}, u32[]{:S(2)}) collective-permute-start(s32[3,8]{1,0:T(4,128)} %bitcast.18), channel_id=1, source_target_pairs={{0,1},{1,0},{2,3},{3,2},{4,5},{5,4},{6,7},{7,6},{8,9},{9,8},{10,11... | collective-permute-start | bytes 296 | tf_op jit(solution)/shard_map/ppermute | solution.py:198
  9.7 9.6 %collective-permute-start.7 = (bf16[20,16,128]{2,1,0:T(8,128)(2,1)S(1)}, bf16[20,16,128]{2,1,0:T(8,128)(2,1)S(1)}, u32[]{:S(2)}, u32[]{:S(2)}) collective-permute-start(bf16[20,16,128]{2,1,0:T(8,128)(2,1)S(1)} %get-tuple-element.38.own), channel_id=1, source_target_pairs={{0,2},{2,0},{4,6},{6,4},{8,10},{10,8},{12,14},{14,12},{16,18},{18,... | collective-permute-start | bytes 245768 | tf_op jit(solution)/shard_map/ppermute | solution.py:229
  11.1 8.2 %collective-permute-start.5 = (bf16[20,16,128]{2,1,0:T(8,128)(2,1)S(1)}, bf16[20,16,128]{2,1,0:T(8,128)(2,1)S(1)}, u32[]{:S(2)}, u32[]{:S(2)}) collective-permute-start(bf16[20,16,128]{2,1,0:T(8,128)(2,1)S(1)} %get-tuple-element.38.own), channel_id=1, source_target_pairs={{0,30},{2,4},{4,2},{6,8},{8,6},{10,12},{12,10},{14,16},{16,14},{18... | collective-permute-start | bytes 245768 | tf_op jit(solution)/shard_map/ppermute | solution.py:269
  14.7 9.0 %collective-permute-start.6 = (bf16[4,16,128]{2,1,0:T(8,128)(2,1)S(1)}, bf16[4,16,128]{2,1,0:T(8,128)(2,1)S(1)}, u32[]{:S(2)}, u32[]{:S(2)}) collective-permute-start(bf16[4,16,128]{2,1,0:T(8,128)(2,1)S(1)} %constant_dynamic-update-slice_fusion.2), channel_id=1, source_target_pairs={{0,8},{2,10},{4,12},{6,14},{8,0},{10,2},{12,4},{14,6},{16,24},{18,... | collective-permute-start | bytes 49160 | tf_op jit(solution)/shard_map/ppermute | solution.py:266
  23.7 5.2 %copy-start = (bf16[14,4,64,64]{3,2,1,0:T(8,128)(2,1)S(1)}, bf16[14,4,64,64]{3,2,1,0:T(8,128)(2,1)}, u32[]{:S(2)}) copy-start(bf16[14,4,64,64]{3,2,1,0:T(8,128)(2,1)} %upper_coup.1) | copy-start | bytes 1376260
  23.7 5.2 %copy-start.1 = (bf16[8,256,64]{1,2,0:T(8,128)(2,1)S(1)}, bf16[8,256,64]{1,2,0:T(8,128)(2,1)}, u32[]{:S(2)}) copy-start(bf16[8,256,64]{1,2,0:T(8,128)(2,1)} %param.21) | copy-start | bytes 786436
  23.7 5.2 %copy-start.2 = (bf16[12,64,64]{2,1,0:T(8,128)(2,1)S(1)}, bf16[12,64,64]{2,1,0:T(8,128)(2,1)}, u32[]{:S(2)}) copy-start(bf16[12,64,64]{2,1,0:T(8,128)(2,1)} %upper_up.1) | copy-start | bytes 294916
  23.7 5.2 %copy-start.3 = (bf16[12,64,64]{2,1,0:T(8,128)(2,1)S(1)}, bf16[12,64,64]{2,1,0:T(8,128)(2,1)}, u32[]{:S(2)}) copy-start(bf16[12,64,64]{2,1,0:T(8,128)(2,1)} %upper_down.1) | copy-start | bytes 294916
  23.7 5.2 %copy-start.4 = (bf16[8,64,64]{2,1,0:T(8,128)(2,1)S(1)}, bf16[8,64,64]{2,1,0:T(8,128)(2,1)}, u32[]{:S(2)}) copy-start(bf16[8,64,64]{2,1,0:T(8,128)(2,1)} %leaf_down.1) | copy-start | bytes 196612
  23.8 5.2 %copy-start.5 = (bf16[1,4,64,64]{3,2,1,0:T(8,128)(2,1)S(1)}, bf16[1,4,64,64]{3,2,1,0:T(8,128)(2,1)}, u32[]{:S(2)}) copy-start(bf16[1,4,64,64]{3,2,1,0:T(8,128)(2,1)} %node_coup.1) | copy-start | bytes 98308
  23.8 5.2 %copy-start.6 = (bf16[1,64,64]{2,1,0:T(8,128)(2,1)S(1)}, bf16[1,64,64]{2,1,0:T(8,128)(2,1)}, u32[]{:S(2)}) copy-start(bf16[1,64,64]{2,1,0:T(8,128)(2,1)} %node_down.1) | copy-start | bytes 24580
  23.8 5.2 %copy-start.7 = (s32[14,4]{0,1:T(4,128)S(1)}, s32[14,4]{0,1:T(4,128)}, u32[]{:S(2)}) copy-start(s32[14,4]{0,1:T(4,128)} %param.31) | copy-start | bytes 676
  23.8 5.2 %copy-start.8 = (s32[1,4]{1,0:T(1,128)S(1)}, s32[1,4]{1,0:T(1,128)}, u32[]{:S(2)}) copy-start(s32[1,4]{1,0:T(1,128)} %node_list.1) | copy-start | bytes 52
  23.8 5.1 %collective-permute-start.9 = (bf16[8,16,128]{2,1,0:T(8,128)(2,1)S(1)}, bf16[8,16,128]{2,1,0:T(8,128)(2,1)S(1)}, u32[]{:S(2)}, u32[]{:S(2)}) collective-permute-start(bf16[8,16,128]{2,1,0:T(8,128)(2,1)S(1)} %constant_dynamic-update-slice_fusion.4.known), channel_id=1, source_target_pairs={{0,16},{2,18},{4,20},{6,22},{8,24},{10,26},{12,28},{14,30},{16,0},... | collective-permute-start | bytes 98312 | tf_op jit(solution)/shard_map/ppermute | solution.py:266

commit v4 on v2

v4 whole, which is shorter than its diff:
```python
import jax
import jax.numpy as jnp
from jax import lax
from jax.experimental import pallas as pl
from jax.experimental.pallas import tpu as pltpu
from jax.sharding import PartitionSpec as P

LAST = (((1,), (1,)), ((), ()))
PLAIN = (((1,), (0,)), ((), ()))


def mm(a, b, dims):
    return lax.dot_general(a, b, dims, preferred_element_type=jnp.float32)


def vmem():
    return pl.BlockSpec(memory_space=pltpu.VMEM)


def smem():
    return pl.BlockSpec(memory_space=pltpu.SMEM)


def up_kernel(dens, col, leaf_up, node_up, coeff_out, message):
    leaves = dens.shape[0]
    rank = col.shape[1]
    node = None
    for t in range(leaves):
        coeff = mm(dens[t], col[t], LAST).astype(jnp.bfloat16)
        coeff_out[t] = coeff
        term = mm(coeff, leaf_up[t], PLAIN)
        node = term if node is None else node + term
    node = node.astype(jnp.bfloat16)
    message[:, :rank] = node
    message[:, rank:] = mm(node, node_up[0], PLAIN).astype(jnp.bfloat16)


def pack_rows(pack, t, leaves, long, short):
    halves = long.shape[1] // 128
    rank = short.shape[1]
    for h in range(halves):
        pack[t * halves + h] = long[:, h * 128 : (h + 1) * 128]
    side = t % 2
    pack[leaves * halves + t // 2, :, side * rank : (side + 1) * rank] = short


def unpack_long(pack, t, halves):
    return jnp.concatenate([pack[t * halves + h] for h in range(halves)], axis=1)


def unpack_short(pack, t, leaves, halves, rank):
    side = t % 2
    return pack[leaves * halves + t // 2, :, side * rank : (side + 1) * rank]


def pack_kernel(dens, coeff, pack):
    leaves = dens.shape[0]
    for t in range(leaves):
        pack_rows(pack, t, leaves, dens[t], coeff[t])


def stage_kernel(*refs):
    count = len(refs) // 2
    sems = refs[-1]
    copies = [
        pltpu.make_async_copy(source, target, sems.at[k])
        for k, (source, target) in enumerate(zip(refs[:count], refs[count:-1]))
    ]
    for copy in copies:
        copy.start()
    for copy in copies:
        copy.wait()


def field_kernel(
    near_list, far_list, pair, own, cross, pair_other, own_other, cross_other, coup, near,
    near_out, far_out, send, ext, ext_coeff,
):
    leaves, entries = near.shape[0], near.shape[1]
    columns = own.shape[1]
    rank = coup.shape[-1]
    halves = near.shape[-1] // 128
    me = lax.axis_index("leaf")
    odd = me & 1
    for slot, pair_of_cores in (
        (2 - 2 * odd, (pair, pair_other)),
        (1, (own, own_other)),
        (2 * odd, (cross, cross_other)),
    ):
        for c, ref in enumerate(pair_of_cores):
            rows = slice(c * columns, (c + 1) * columns)
            for t in range(leaves):
                ext[slot * leaves + t, rows] = unpack_long(ref, t, halves)
                ext_coeff[slot * leaves + t, rows] = unpack_short(ref, t, leaves, halves, rank)
    offset = (me - 1) * leaves
    for t in range(leaves):
        total = None
        for j in range(entries):
            term = mm(ext[near_list[j, t] - offset], near[t, j], LAST)
            total = term if total is None else total + term
        far = None
        for j in range(entries):
            term = mm(ext_coeff[far_list[j, t] - offset], coup[t, j], LAST)
            far = term if far is None else far + term
        near_out[t] = total[:columns]
        far_out[t] = far[:columns]
        pack_rows(
            send, t, leaves, total[columns:].astype(jnp.bfloat16), far[columns:].astype(jnp.bfloat16)
        )


def down_kernel(
    node_list, upper_list, known, other, near, far, received, row, leaf_down, node_coup, node_down,
    upper_coup, upper_up, upper_down, out, *tree,
):
    half_nodes, columns, _ = known.shape
    nodes = 2 * half_nodes
    rank = row.shape[1]
    leaves = row.shape[0]
    gathered, tree = tree[0], tree[1:]
    gathered[:half_nodes] = known[...]
    gathered[half_nodes:] = other[...]
    farc = node_coup.shape[1]
    levels = nodes.bit_length() - 1
    me = lax.axis_index("leaf")

    for m in range(nodes // 2):
        left = gathered[(2 * m) ^ me, :, rank:].astype(jnp.float32)
        right = gathered[(2 * m + 1) ^ me, :, rank:].astype(jnp.float32)
        tree[levels - 2][m] = (left + right).astype(jnp.bfloat16)
    for height in range(levels - 2, 0, -1):
        breadth = 2**height
        lower = tree[height]
        for m in range(breadth):
            first = 2 * (breadth + m) - 4
            value = mm(lower[2 * m], upper_up[first], PLAIN)
            value = value + mm(lower[2 * m + 1], upper_up[first + 1], PLAIN)
            tree[height - 1][m] = value.astype(jnp.bfloat16)
    field = None
    for height in range(1, levels):
        breadth = 2**height
        node = (nodes + me) >> (levels - height)
        total = None
        for j in range(farc):
            source = tree[height - 1][upper_list[j, node - 2] - breadth]
            term = mm(source, upper_coup[node - 2, j], LAST)
            total = term if total is None else total + term
        if height > 1:
            total = total + mm(field, upper_down[node - 4], LAST)
        field = total.astype(jnp.bfloat16)
    total = mm(field, node_down[0], LAST)
    for j in range(farc):
        source = gathered[node_list[0, j] ^ me, :, :rank]
        total = total + mm(source, node_coup[0, j], LAST)
    field = total.astype(jnp.bfloat16)
    halves = near.shape[2] // 128
    for t in range(leaves):
        local = far[t] + unpack_short(received, t, leaves, halves, rank).astype(jnp.float32)
        local = (local + mm(field, leaf_down[t], LAST)).astype(jnp.bfloat16)
        close = near[t] + unpack_long(received, t, halves).astype(jnp.float32)
        out[t] = (close + mm(local, row[t], PLAIN)).astype(jnp.bfloat16)


def body(
    density,
    near_blocks,
    near_index,
    col_basis,
    row_basis,
    leaf_coupling,
    leaf_list,
    leaf_up,
    leaf_down,
    node_coupling,
    node_list,
    node_up,
    node_down,
    upper_coupling,
    upper_list,
    upper_up,
    upper_down,
):
    leaves, points, columns = density.shape
    rank = col_basis.shape[2]
    nodes = lax.axis_size("leaf")
    levels = nodes.bit_length() - 1
    bf16, f32 = jnp.bfloat16, jnp.float32
    swap = [(0, 1), (1, 0)]

    dens = jnp.swapaxes(density, 1, 2)
    coeff, message = pl.pallas_call(
        up_kernel,
        out_shape=(
            pltpu.VMEM((leaves, columns, rank), bf16),
            pltpu.VMEM((columns, 2 * rank), bf16),
        ),
        in_specs=[vmem()] * 4,
        out_specs=(vmem(), vmem()),
        name="up",
    )(dens, jnp.swapaxes(col_basis, 1, 2), leaf_up, node_up)
    tiles = leaves * (points // 128) + leaves // 2
    pack = pl.pallas_call(
        pack_kernel,
        out_shape=pltpu.VMEM((tiles, columns, 128), bf16),
        in_specs=[vmem()] * 2,
        out_specs=vmem(),
        name="pack",
    )(dens, coeff)
    staged = [near_index.T, leaf_list.T, leaf_coupling, near_blocks]
    staged = pl.pallas_call(
        stage_kernel,
        out_shape=[pltpu.VMEM(x.shape, x.dtype) for x in staged],
        in_specs=[pl.BlockSpec(memory_space=pl.ANY)] * 4,
        out_specs=[vmem()] * 4,
        scratch_shapes=[pltpu.SemaphoreType.DMA((4,))],
        name="stage",
    )(*[pltpu.with_memory_space_constraint(x, pltpu.HBM) for x in staged])
    pair = lax.ppermute(pack, "leaf", [(i, i ^ 1) for i in range(nodes)])
    others = [(i, (i + 1 if i % 2 else i - 1) % nodes) for i in range(nodes)]

    cross = lax.ppermute(pack, "leaf", others)
    own_other = lax.ppermute(pack, "sub", swap)

    entries = near_blocks.shape[1]

    def fields(*packs):
        return pl.pallas_call(
            field_kernel,
            out_shape=(
                pltpu.VMEM((leaves, columns, points), f32),
                pltpu.VMEM((leaves, columns, rank), f32),
                pltpu.VMEM((tiles, columns, 128), bf16),
            ),
            in_specs=[smem()] * 2 + [vmem()] * 8,
            out_specs=(vmem(),) * 3,
            scratch_shapes=[
                pltpu.VMEM((3 * leaves, 2 * columns, points), bf16),
                pltpu.VMEM((3 * leaves, 2 * columns, rank), bf16),
            ],
            compiler_params=pltpu.CompilerParams(vmem_limit_bytes=16 * 1024 * 1024),
            cost_estimate=pl.CostEstimate(
                flops=2 * leaves * entries * points * points * 256,
                bytes_accessed=leaves * entries * points * points * 2,
                transcendentals=0,
            ),
            name="fields",
        )(staged[0], staged[1], *packs, staged[2], staged[3])

    known = message[None]
    for bit in range(levels):
        step = 1 << bit
        other = lax.ppermute(known, "leaf", [(i, i ^ step) for i in range(nodes)])
        if bit == 0:
            known, other, pack = lax.optimization_barrier((known, other, pack))
        if bit == 1:
            known, other, pair, cross, own_other, staged = lax.optimization_barrier(
                (known, other, pair, cross, own_other, staged)
            )
            pair_other = lax.ppermute(pair, "sub", swap)
            cross_other = lax.ppermute(cross, "sub", swap)
        if bit == levels - 2:
            near, far, send = fields(pair, pack, cross, pair_other, own_other, cross_other)
            known, other, near, far, send = lax.optimization_barrier(
                (known, other, near, far, send)
            )
        if bit < levels - 1:
            known = jnp.concatenate([known, other], axis=0)
    received = lax.ppermute(send, "sub", swap)

    out = pl.pallas_call(
        down_kernel,
        out_shape=jax.ShapeDtypeStruct((leaves, columns, points), bf16),
        in_specs=[smem()] * 2 + [vmem()] * 12,
        out_specs=vmem(),
        scratch_shapes=[pltpu.VMEM((nodes, columns, 2 * rank), bf16)]
        + [pltpu.VMEM((2**height, columns, rank), bf16) for height in range(1, levels)],
        compiler_params=pltpu.CompilerParams(vmem_limit_bytes=24 * 1024 * 1024),
        name="down",
    )(
        node_list, upper_list.T, known, other, near, far, received,
        jnp.swapaxes(row_basis, 1, 2), leaf_down, node_coupling, node_down, upper_coupling, upper_up, upper_down,
    )
    return jnp.swapaxes(out, 1, 2)


def solution(mesh):
    placed = (
        P("leaf", None, "sub"),
        P("leaf", "sub", None, None),
        P("leaf", "sub"),
        P("leaf", None, None),
        P("leaf", None, None),
        P("leaf", "sub", None, None),
        P("leaf", "sub"),
        P("leaf", None, None),
        P("leaf", None, None),
        P("leaf", None, None, None),
        P("leaf", None),
        P("leaf", None, None),
        P("leaf", None, None),
        P(),
        P(),
        P(),
        P(),
    )
    return jax.shard_map(
        body, mesh=mesh, in_specs=placed, out_specs=P("leaf", None, "sub"), check_vma=False
    )
```

time: 36.8 us -> 32.6 us (0.89)
  waiting for transfers between devices: 3.3 us -> 8.59 us
  starting transfers between devices: 14.3 us -> 9.61 us
  Pallas kernels: 13.7 us -> 10.7 us
  local copies, waits for them, and re-layouts: 4.14 us -> 3.28 us
  other arithmetic: 0.71 us -> 0 us
    ppermute x4, waiting for transfers between devices: 2.13 us -> 8.58 us  [body(): other = lax.ppermute(known, 'leaf', [(i, i ^ step) for i in range(nodes)])]
    ppermute x4, starting transfers between devices: 8.69 us -> 3.01 us  [body(): other = lax.ppermute(known, 'leaf', [(i, i ^ step) for i in range(nodes)])]
    ppermute x4 -> x5, starting transfers between devices: 1.18 us -> 6.59 us  [the longest x1 6.02 us: body(): cross = lax.ppermute(pack, 'leaf', others)]
    ppermute x1, starting transfers between devices: 4.39 us -> 0.01 us  [body(): pair = lax.ppermute(pack, 'leaf', [(i, i ^ 1) for i in range(nodes)])]
    pallas_call x3, Pallas kernels: 8.94 us -> 5.88 us  [the longest x1 2.24 us: fields(): pl.pallas_call(field_kernel, out_shape=(pltpu.VMEM((leaves, columns, poin...]
    unnamed x33 -> x23, local copies, waits for them, and re-layouts: 4.13 us -> 1.97 us
    concatenate x2 -> x3, local copies, waits for them, and re-layouts: 0.02 us -> 1.3 us  [body(): known = jnp.concatenate([known, other], axis=0)]
    ppermute x4 -> x5, waiting for transfers between devices: 1.17 us -> 0.01 us  [the longest x1 0.01 us: body(): cross = lax.ppermute(pack, 'leaf', others)]
  transfers between devices with their start and end apart: 9 -> 10, of which waited for: 2 -> 3; matrix products, arithmetic and copies ran while one was open for 2% -> 8% of each run, Pallas kernels for 29% -> 18%
where the time goes in v4:
time: 32.6 us; the launch traced here: 32.3 us
  Pallas kernels  10.7 us (33%)
  starting transfers between devices  9.61 us (29%)
  waiting for transfers between devices  8.59 us (26%)
  local copies, waits for them, and re-layouts  3.28 us (10%)
    ppermute x4, waiting for transfers between devices, body(): other = lax.ppermute(known, 'leaf', [(i, i ^ step) for i in range(nodes)])  8.58 us
    ppermute x1, starting transfers between devices, body(): cross = lax.ppermute(pack, 'leaf', others)  6.02 us
    pallas_call x1, Pallas kernels, body(): pl.pallas_call(down_kernel, out_shape=jax.ShapeDtypeStruct((leaves, colum...  3.18 us
    ppermute x4, starting transfers between devices, body(): other = lax.ppermute(known, 'leaf', [(i, i ^ step) for i in range(nodes)])  3.01 us
    pallas_call x1, Pallas kernels, fields(): pl.pallas_call(field_kernel, out_shape=(pltpu.VMEM((leaves, columns, poin...  2.24 us
    pallas_call x1, Pallas kernels, body(): pl.pallas_call(stage_kernel, out_shape=[pltpu.VMEM(x.shape, x.dtype) for...  2.1 us
    unnamed x23, local copies, waits for them, and re-layouts  1.97 us
    pallas_call x1, Pallas kernels, body(): pl.pallas_call(up_kernel, out_shape=(pltpu.VMEM((leaves, columns, rank),...  1.63 us
  transfers between devices with their start and end apart: 10, of which 3 were waited for; matrix products, arithmetic and copies ran while one was open for 8% of the time, Pallas kernels for 18%

profile of v4, /device:TPU:0, one launch (start us, length us, event | category | flops | bytes accessed | tf_op | source)
XLA Modules:
  0.0 32.3 jit_solution(3931664999145229634)
XLA Ops:
  0.0 1.6 %up.1 = (bf16[8,16,64]{2,1,0:T(8,128)(2,1)S(1)}, bf16[16,128]{1,0:T(8,128)(2,1)S(1)}) custom-call(bf16[8,16,256]{2,1,0:T(8,128)(2,1)} %bitcast.13, bf16[8,64,256]{2,1,0:T(8,128)(2,1)} %bitcast.12, bf16[8,64,64]{2,1,0:T(8,128)(2,1)} %leaf_up.1, bf16[1,64,64]{2,1,0:T(8,128)(2,1)} %node_up.1), custom_call_target="tpu_custom_call" | custom-call | tf_op jit(solution)/shard_map/up/pallas_call | solution.py:191
  1.6 0.0 copy-start.6
  1.6 0.6 %copy-done.6 = bf16[8,16,64]{2,1,0:T(8,128)(2,1)} copy-done((bf16[8,16,64]{2,1,0:T(8,128)(2,1)}, bf16[8,16,64]{2,1,0:T(8,128)(2,1)S(1)}, u32[]{:S(2)}) %copy-start.6) | copy-done | bytes 16408
  2.3 2.9 %collective-permute-start = (bf16[1,16,128]{2,1,0:T(8,128)(2,1)S(1)}, bf16[1,16,128]{2,1,0:T(8,128)(2,1)S(1)}, u32[]{:S(2)}, u32[]{:S(2)}) collective-permute-start(bf16[1,16,128]{2,1,0:T(8,128)(2,1)S(1)} %bitcast.9), channel_id=1, source_target_pairs={{0,2},{2,0},{4,6},{6,4},{8,10},{10,8},{12,14},{14,12},{16,18},{18,... | collective-permute-start | bytes 12296 | tf_op jit(solution)/shard_map/ppermute | solution.py:252
  5.2 1.5 %pack.1.own = bf16[20,16,128]{2,1,0:T(8,128)(2,1)} custom-call(bf16[8,16,256]{2,1,0:T(8,128)(2,1)} %bitcast.14, bf16[8,16,64]{2,1,0:T(8,128)(2,1)} %copy-done.6), custom_call_target="tpu_custom_call" | custom-call | tf_op jit(solution)/shard_map/pack/pallas_call | solution.py:202
  6.7 0.0 collective-permute-start.2
  6.7 6.0 %collective-permute-start.3 = (bf16[20,16,128]{2,1,0:T(8,128)(2,1)}, bf16[20,16,128]{2,1,0:T(8,128)(2,1)}, u32[]{:S(2)}, u32[]{:S(2)}) collective-permute-start(bf16[20,16,128]{2,1,0:T(8,128)(2,1)} %pack.1.own), channel_id=1, source_target_pairs={{0,30},{2,4},{4,2},{6,8},{8,6},{10,12},{12,10},{14,16},{16,14},{18... | collective-permute-start | bytes 245768 | tf_op jit(solution)/shard_map/ppermute | solution.py:221
  12.8 0.0 collective-permute-start.4
  12.8 0.0 collective-permute-done
  12.8 0.6 %constant_dynamic-update-slice_fusion.1 = bf16[2,16,128]{2,1,0:T(8,128)(2,1)} fusion(bf16[1,16,128]{2,1,0:T(8,128)(2,1)S(1)} %bitcast.10), kind=kLoop, calls=%fused_computation.1 | loop fusion | bytes 8192
  13.4 0.6 %constant_dynamic-update-slice_fusion = bf16[2,16,128]{2,1,0:T(8,128)(2,1)} fusion(bf16[2,16,128]{2,1,0:T(8,128)(2,1)} %constant_dynamic-update-slice_fusion.1, bf16[1,16,128]{2,1,0:T(8,128)(2,1)S(1)} %collective-permute-done), kind=kLoop, calls=%fused_computation | loop fusion | bytes 8192 | tf_op jit(solution)/shard_map/concatenate | solution.py:267
  13.9 0.0 collective-permute-start.1
  14.0 0.0 copy-start.8
  14.0 0.0 copy-start.9
  14.0 2.1 %stage.1 = (s32[3,8]{1,0:T(4,128)S(1)}, s32[3,8]{1,0:T(4,128)S(1)}, bf16[8,3,64,64]{3,2,1,0:T(8,128)(2,1)S(1)}, bf16[8,3,256,256]{3,2,1,0:T(8,128)(2,1)S(1)}) custom-call(s32[3,8]{1,0:T(4,128)} %bitcast.15, s32[3,8]{1,0:T(4,128)} %bitcast.16, bf16[8,3,64,64]{3,2,1,0:T(8,128)(2,1)} %refs_2_.1, bf16[8,3,256,256]{3,2,1,0:T(8,128)(2,1)} %refs_3_.1), custom_call_target="tpu_custom_call" | custom-call | tf_op jit(solution)/shard_map/stage/pallas_call | solution.py:210
  16.1 0.0 copy-start
  16.1 0.0 copy-start.1
  16.1 0.0 copy-start.2
  16.1 0.0 copy-start.3
  16.1 0.0 copy-start.4
  16.1 0.0 copy-start.5
  16.1 0.0 copy-start.7
  16.2 1.8 %collective-permute-done.1 = bf16[2,16,128]{2,1,0:T(8,128)(2,1)} collective-permute-done((bf16[2,16,128]{2,1,0:T(8,128)(2,1)}, bf16[2,16,128]{2,1,0:T(8,128)(2,1)}, u32[]{:S(2)}, u32[]{:S(2)}) %collective-permute-start.1) | collective-permute-done | bytes 8224 | tf_op jit(solution)/shard_map/ppermute | solution.py:252
  17.9 0.0 collective-permute-done.2.pair
  17.9 0.0 collective-permute-done.3.cross
  17.9 0.0 collective-permute-done.4.own_other
  17.9 0.1 collective-permute-start.6
  18.0 0.5 %collective-permute-start.7 = (bf16[20,16,128]{2,1,0:T(8,128)(2,1)}, bf16[20,16,128]{2,1,0:T(8,128)(2,1)S(1)}, u32[]{:S(2)}, u32[]{:S(2)}) collective-permute-start(bf16[20,16,128]{2,1,0:T(8,128)(2,1)} %collective-permute-done.3.cross), channel_id=1, source_target_pairs={{0,1},{1,0},{2,3},{3,2},{4,5},{5,4},{6,7},{7,6},{8,9},{9,8},{10,11... | collective-permute-start | bytes 245768 | tf_op jit(solution)/shard_map/ppermute | solution.py:260
  18.5 0.7 %constant_dynamic-update-slice_fusion.3 = bf16[4,16,128]{2,1,0:T(8,128)(2,1)S(1)} fusion(bf16[2,16,128]{2,1,0:T(8,128)(2,1)} %constant_dynamic-update-slice_fusion), kind=kLoop, calls=%fused_computation.3 | loop fusion | bytes 16384
  19.2 0.7 %constant_dynamic-update-slice_fusion.2 = bf16[4,16,128]{2,1,0:T(8,128)(2,1)S(1)} fusion(bf16[4,16,128]{2,1,0:T(8,128)(2,1)S(1)} %constant_dynamic-update-slice_fusion.3, bf16[2,16,128]{2,1,0:T(8,128)(2,1)} %collective-permute-done.1), kind=kLoop, calls=%fused_computation.2 | loop fusion | bytes 16384 | tf_op jit(solution)/shard_map/concatenate | solution.py:267
  19.9 0.0 collective-permute-start.5
  19.9 0.0 collective-permute-done.6.pair_other
  19.9 0.0 collective-permute-done.7.cross_other
  19.9 2.2 %fields.1 = (f32[8,16,256]{2,1,0:T(8,128)S(1)}, f32[8,16,64]{2,1,0:T(8,128)S(1)}, bf16[20,16,128]{2,1,0:T(8,128)(2,1)S(1)}) custom-call(s32[3,8]{1,0:T(4,128)S(1)} %get-tuple-element.41.near_list, s32[3,8]{1,0:T(4,128)S(1)} %get-tuple-element.42.far_list, bf16[20,16,128]{2,1,0:T(8,128)(2,1)} %collective-permute-done.2.pair, bf16[20,16,128]{2,1,0:T(8,128)(2,1)} %pack.1.own, ...), custom_call_target="tpu_custom_call" | custom-call | flops 805306368 | bytes 3145728 | tf_op jit(solution)/shard_map/fields/pallas_call | solution.py:227
  22.2 1.5 %collective-permute-done.5 = bf16[4,16,128]{2,1,0:T(8,128)(2,1)S(1)} collective-permute-done((bf16[4,16,128]{2,1,0:T(8,128)(2,1)S(1)}, bf16[4,16,128]{2,1,0:T(8,128)(2,1)S(1)}, u32[]{:S(2)}, u32[]{:S(2)}) %collective-permute-start.5) | collective-permute-done | bytes 16416 | tf_op jit(solution)/shard_map/ppermute | solution.py:252
  23.6 0.0 collective-permute-start.9
  23.7 0.1 collective-permute-start.8
  23.7 5.3 %collective-permute-done.8.other = bf16[8,16,128]{2,1,0:T(8,128)(2,1)S(1)} collective-permute-done((bf16[8,16,128]{2,1,0:T(8,128)(2,1)S(1)}, bf16[8,16,128]{2,1,0:T(8,128)(2,1)S(1)}, u32[]{:S(2)}, u32[]{:S(2)}) %collective-permute-start.8) | collective-permute-done | bytes 32800 | tf_op jit(solution)/shard_map/ppermute | solution.py:252
  29.1 0.0 collective-permute-done.9.received
  29.1 0.0 copy-done.8
  29.1 0.0 copy-done.9
  29.1 0.0 copy-done
  29.1 0.0 copy-done.1
  29.1 0.0 copy-done.2
  29.1 0.0 copy-done.3
  29.1 0.0 copy-done.4
  29.1 0.0 copy-done.5
  29.1 0.0 copy-done.7
  29.1 3.2 %down.1 = bf16[8,16,256]{2,1,0:T(8,128)(2,1)} custom-call(s32[1,4]{1,0:T(1,128)S(1)} %copy-done.9, s32[4,14]{1,0:T(4,128)S(1)} %bitcast.11, bf16[8,16,128]{2,1,0:T(8,128)(2,1)S(1)} %constant_dynamic-update-slice_fusion.4.known, bf16[8,16,128]{2,1,0:T(8,128)(2,1)S(1)} %collective-permute-done.8.other, f32[8,16,256]{2,1,0:T(8,128)S(1)} %get-tuple-element.54.near, ...), custom_call_target="tpu_custom_call" | custom-call | tf_op jit(solution)/shard_map/down/pallas_call | solution.py:270
  (2 shorter events, 0.0 us)
Async XLA Ops:
  1.6 0.6 %copy-start.6 = (bf16[8,16,64]{2,1,0:T(8,128)(2,1)}, bf16[8,16,64]{2,1,0:T(8,128)(2,1)S(1)}, u32[]{:S(2)}) copy-start(bf16[8,16,64]{2,1,0:T(8,128)(2,1)S(1)} %get-tuple-element.32.coeff) | copy-start | bytes 49156
  2.3 10.5 %collective-permute-start = (bf16[1,16,128]{2,1,0:T(8,128)(2,1)S(1)}, bf16[1,16,128]{2,1,0:T(8,128)(2,1)S(1)}, u32[]{:S(2)}, u32[]{:S(2)}) collective-permute-start(bf16[1,16,128]{2,1,0:T(8,128)(2,1)S(1)} %bitcast.9), channel_id=1, source_target_pairs={{0,2},{2,0},{4,6},{6,4},{8,10},{10,8},{12,14},{14,12},{16,18},{18,... | collective-permute-start | bytes 12296 | tf_op jit(solution)/shard_map/ppermute | solution.py:252
  6.7 11.2 %collective-permute-start.2 = (bf16[20,16,128]{2,1,0:T(8,128)(2,1)}, bf16[20,16,128]{2,1,0:T(8,128)(2,1)}, u32[]{:S(2)}, u32[]{:S(2)}) collective-permute-start(bf16[20,16,128]{2,1,0:T(8,128)(2,1)} %pack.1.own), channel_id=1, source_target_pairs={{0,2},{2,0},{4,6},{6,4},{8,10},{10,8},{12,14},{14,12},{16,18},{18,... | collective-permute-start | bytes 245768 | tf_op jit(solution)/shard_map/ppermute | solution.py:218
  6.7 11.2 %collective-permute-start.3 = (bf16[20,16,128]{2,1,0:T(8,128)(2,1)}, bf16[20,16,128]{2,1,0:T(8,128)(2,1)}, u32[]{:S(2)}, u32[]{:S(2)}) collective-permute-start(bf16[20,16,128]{2,1,0:T(8,128)(2,1)} %pack.1.own), channel_id=1, source_target_pairs={{0,30},{2,4},{4,2},{6,8},{8,6},{10,12},{12,10},{14,16},{16,14},{18... | collective-permute-start | bytes 245768 | tf_op jit(solution)/shard_map/ppermute | solution.py:221
  12.8 5.2 %collective-permute-start.4 = (bf16[20,16,128]{2,1,0:T(8,128)(2,1)}, bf16[20,16,128]{2,1,0:T(8,128)(2,1)}, u32[]{:S(2)}, u32[]{:S(2)}) collective-permute-start(bf16[20,16,128]{2,1,0:T(8,128)(2,1)} %pack.1.own), channel_id=1, source_target_pairs={{0,1},{1,0},{2,3},{3,2},{4,5},{5,4},{6,7},{7,6},{8,9},{9,8},{10,11... | collective-permute-start | bytes 245768 | tf_op jit(solution)/shard_map/ppermute | solution.py:222
  13.9 4.0 %collective-permute-start.1 = (bf16[2,16,128]{2,1,0:T(8,128)(2,1)}, bf16[2,16,128]{2,1,0:T(8,128)(2,1)}, u32[]{:S(2)}, u32[]{:S(2)}) collective-permute-start(bf16[2,16,128]{2,1,0:T(8,128)(2,1)} %constant_dynamic-update-slice_fusion), channel_id=1, source_target_pairs={{0,4},{2,6},{4,0},{6,2},{8,12},{10,14},{12,8},{14,10},{16,20},{18,... | collective-permute-start | bytes 24584 | tf_op jit(solution)/shard_map/ppermute | solution.py:252
  14.0 15.1 %copy-start.8 = (s32[14,4]{0,1:T(4,128)S(1)}, s32[14,4]{0,1:T(4,128)}, u32[]{:S(2)}) copy-start(s32[14,4]{0,1:T(4,128)} %param.31) | copy-start | bytes 676
  14.0 15.1 %copy-start.9 = (s32[1,4]{1,0:T(1,128)S(1)}, s32[1,4]{1,0:T(1,128)}, u32[]{:S(2)}) copy-start(s32[1,4]{1,0:T(1,128)} %node_list.1) | copy-start | bytes 52
  16.1 13.0 %copy-start = (bf16[14,4,64,64]{3,2,1,0:T(8,128)(2,1)S(1)}, bf16[14,4,64,64]{3,2,1,0:T(8,128)(2,1)}, u32[]{:S(2)}) copy-start(bf16[14,4,64,64]{3,2,1,0:T(8,128)(2,1)} %upper_coup.1) | copy-start | bytes 1376260
  16.1 13.0 %copy-start.1 = (bf16[8,256,64]{1,2,0:T(8,128)(2,1)S(1)}, bf16[8,256,64]{1,2,0:T(8,128)(2,1)}, u32[]{:S(2)}) copy-start(bf16[8,256,64]{1,2,0:T(8,128)(2,1)} %param.21) | copy-start | bytes 786436
  16.1 13.0 %copy-start.2 = (bf16[12,64,64]{2,1,0:T(8,128)(2,1)S(1)}, bf16[12,64,64]{2,1,0:T(8,128)(2,1)}, u32[]{:S(2)}) copy-start(bf16[12,64,64]{2,1,0:T(8,128)(2,1)} %upper_up.1) | copy-start | bytes 294916
  16.1 13.0 %copy-start.3 = (bf16[12,64,64]{2,1,0:T(8,128)(2,1)S(1)}, bf16[12,64,64]{2,1,0:T(8,128)(2,1)}, u32[]{:S(2)}) copy-start(bf16[12,64,64]{2,1,0:T(8,128)(2,1)} %upper_down.1) | copy-start | bytes 294916
  16.1 13.0 %copy-start.4 = (bf16[8,64,64]{2,1,0:T(8,128)(2,1)S(1)}, bf16[8,64,64]{2,1,0:T(8,128)(2,1)}, u32[]{:S(2)}) copy-start(bf16[8,64,64]{2,1,0:T(8,128)(2,1)} %leaf_down.1) | copy-start | bytes 196612
  16.1 13.0 %copy-start.5 = (bf16[1,4,64,64]{3,2,1,0:T(8,128)(2,1)S(1)}, bf16[1,4,64,64]{3,2,1,0:T(8,128)(2,1)}, u32[]{:S(2)}) copy-start(bf16[1,4,64,64]{3,2,1,0:T(8,128)(2,1)} %node_coup.1) | copy-start | bytes 98308
  16.1 13.0 %copy-start.7 = (bf16[1,64,64]{2,1,0:T(8,128)(2,1)S(1)}, bf16[1,64,64]{2,1,0:T(8,128)(2,1)}, u32[]{:S(2)}) copy-start(bf16[1,64,64]{2,1,0:T(8,128)(2,1)} %node_down.1) | copy-start | bytes 24580
  17.9 2.0 %collective-permute-start.6 = (bf16[20,16,128]{2,1,0:T(8,128)(2,1)}, bf16[20,16,128]{2,1,0:T(8,128)(2,1)S(1)}, u32[]{:S(2)}, u32[]{:S(2)}) collective-permute-start(bf16[20,16,128]{2,1,0:T(8,128)(2,1)} %collective-permute-done.2.pair), channel_id=1, source_target_pairs={{0,1},{1,0},{2,3},{3,2},{4,5},{5,4},{6,7},{7,6},{8,9},{9,8},{10,11... | collective-permute-start | bytes 245768 | tf_op jit(solution)/shard_map/ppermute | solution.py:259
  18.0 1.9 %collective-permute-start.7 = (bf16[20,16,128]{2,1,0:T(8,128)(2,1)}, bf16[20,16,128]{2,1,0:T(8,128)(2,1)S(1)}, u32[]{:S(2)}, u32[]{:S(2)}) collective-permute-start(bf16[20,16,128]{2,1,0:T(8,128)(2,1)} %collective-permute-done.3.cross), channel_id=1, source_target_pairs={{0,1},{1,0},{2,3},{3,2},{4,5},{5,4},{6,7},{7,6},{8,9},{9,8},{10,11... | collective-permute-start | bytes 245768 | tf_op jit(solution)/shard_map/ppermute | solution.py:260
  19.9 3.7 %collective-permute-start.5 = (bf16[4,16,128]{2,1,0:T(8,128)(2,1)S(1)}, bf16[4,16,128]{2,1,0:T(8,128)(2,1)S(1)}, u32[]{:S(2)}, u32[]{:S(2)}) collective-permute-start(bf16[4,16,128]{2,1,0:T(8,128)(2,1)S(1)} %constant_dynamic-update-slice_fusion.2), channel_id=1, source_target_pairs={{0,8},{2,10},{4,12},{6,14},{8,0},{10,2},{12,4},{14,6},{16,24},{18,... | collective-permute-start | bytes 49160 | tf_op jit(solution)/shard_map/ppermute | solution.py:252
  23.6 5.4 %collective-permute-start.9 = (bf16[20,16,128]{2,1,0:T(8,128)(2,1)S(1)}, bf16[20,16,128]{2,1,0:T(8,128)(2,1)S(1)}, u32[]{:S(2)}, u32[]{:S(2)}) collective-permute-start(bf16[20,16,128]{2,1,0:T(8,128)(2,1)S(1)} %get-tuple-element.56), channel_id=1, source_target_pairs={{0,1},{1,0},{2,3},{3,2},{4,5},{5,4},{6,7},{7,6},{8,9},{9,8},{10,11... | collective-permute-start | bytes 245768 | tf_op jit(solution)/shard_map/ppermute | solution.py:268
  23.7 5.4 %collective-permute-start.8 = (bf16[8,16,128]{2,1,0:T(8,128)(2,1)S(1)}, bf16[8,16,128]{2,1,0:T(8,128)(2,1)S(1)}, u32[]{:S(2)}, u32[]{:S(2)}) collective-permute-start(bf16[8,16,128]{2,1,0:T(8,128)(2,1)S(1)} %constant_dynamic-update-slice_fusion.4.known), channel_id=1, source_target_pairs={{0,16},{2,18},{4,20},{6,22},{8,24},{10,26},{12,28},{14,30},{16,0},... | collective-permute-start | bytes 98312 | tf_op jit(solution)/shard_map/ppermute | solution.py:252

commit v5 on v4

--- a/solution.py
+++ b/solution.py
@@ -13,6 +13,14 @@
     return lax.dot_general(a, b, dims, preferred_element_type=jnp.float32)
 
 
+def pinned(x, space):
+    return pltpu.with_memory_space_constraint(x, space)
+
+
+def limit(mebibytes):
+    return pltpu.CompilerParams(vmem_limit_bytes=mebibytes * 1024 * 1024)
+
+
 def vmem():
     return pl.BlockSpec(memory_space=pltpu.VMEM)
 
@@ -21,8 +29,9 @@
     return pl.BlockSpec(memory_space=pltpu.SMEM)
 
 
-def up_kernel(dens, col, leaf_up, node_up, coeff_out, message):
+def up_kernel(dens, col, leaf_up, node_up, coeff_out, message, dens_out):
     leaves = dens.shape[0]
+    dens_out[...] = dens[...]
     rank = col.shape[1]
     node = None
     for t in range(leaves):
@@ -188,24 +197,27 @@
     swap = [(0, 1), (1, 0)]
 
     dens = jnp.swapaxes(density, 1, 2)
-    coeff, message = pl.pallas_call(
+    coeff, message, dens_here = pl.pallas_call(
         up_kernel,
         out_shape=(
             pltpu.VMEM((leaves, columns, rank), bf16),
             pltpu.VMEM((columns, 2 * rank), bf16),
+            pltpu.VMEM(dens.shape, bf16),
         ),
         in_specs=[vmem()] * 4,
-        out_specs=(vmem(), vmem()),
+        out_specs=(vmem(),) * 3,
+        compiler_params=limit(4),
         name="up",
-    )(dens, jnp.swapaxes(col_basis, 1, 2), leaf_up, node_up)
+    )(*[pinned(x, pltpu.HBM) for x in (dens, jnp.swapaxes(col_basis, 1, 2), leaf_up, node_up)])
     tiles = leaves * (points // 128) + leaves // 2
     pack = pl.pallas_call(
         pack_kernel,
         out_shape=pltpu.VMEM((tiles, columns, 128), bf16),
         in_specs=[vmem()] * 2,
         out_specs=vmem(),
+        compiler_params=limit(4),
         name="pack",
-    )(dens, coeff)
+    )(pinned(dens_here, pltpu.VMEM), pinned(coeff, pltpu.VMEM))
     staged = [near_index.T, leaf_list.T, leaf_coupling, near_blocks]
     staged = pl.pallas_call(
         stage_kernel,
@@ -213,12 +225,19 @@
         in_specs=[pl.BlockSpec(memory_space=pl.ANY)] * 4,
         out_specs=[vmem()] * 4,
         scratch_shapes=[pltpu.SemaphoreType.DMA((4,))],
+        compiler_params=limit(4),
         name="stage",
-    )(*[pltpu.with_memory_space_constraint(x, pltpu.HBM) for x in staged])
+    )(*[pinned(x, pltpu.HBM) for x in staged])
     pair = lax.ppermute(pack, "leaf", [(i, i ^ 1) for i in range(nodes)])
-    others = [(i, (i + 1 if i % 2 else i - 1) % nodes) for i in range(nodes)]
-
-    cross = lax.ppermute(pack, "leaf", others)
+    cores = lax.axis_size("sub")
+    others = [
+        (i * cores + c, (i + 1 if i % 2 else i - 1) * cores + c)
+        for i in range(1, nodes - 1)
+        for c in range(cores)
+    ]
+    others += [(i * cores + c, i * cores + 1 - c) for i in (0, nodes - 1) for c in range(cores)]
+
+    cross = lax.ppermute(pack, ("leaf", "sub"), others)
     own_other = lax.ppermute(pack, "sub", swap)
 
     entries = near_blocks.shape[1]
@@ -237,7 +256,7 @@
                 pltpu.VMEM((3 * leaves, 2 * columns, points), bf16),
                 pltpu.VMEM((3 * leaves, 2 * columns, rank), bf16),
             ],
-            compiler_params=pltpu.CompilerParams(vmem_limit_bytes=16 * 1024 * 1024),
+            compiler_params=limit(8),
             cost_estimate=pl.CostEstimate(
                 flops=2 * leaves * entries * points * points * 256,
                 bytes_accessed=leaves * entries * points * points * 2,
@@ -274,7 +293,7 @@
         out_specs=vmem(),
         scratch_shapes=[pltpu.VMEM((nodes, columns, 2 * rank), bf16)]
         + [pltpu.VMEM((2**height, columns, rank), bf16) for height in range(1, levels)],
-        compiler_params=pltpu.CompilerParams(vmem_limit_bytes=24 * 1024 * 1024),
+        compiler_params=limit(8),
         name="down",
     )(
         node_list, upper_list.T, known, other, near, far, received,

time: 32.6 us -> 24.1 us (0.74)
  waiting for transfers between devices: 8.59 us -> 2.96 us
  local copies, waits for them, and re-layouts: 3.28 us -> 0.08 us
  starting transfers between devices: 9.61 us -> 11.9 us
  Pallas kernels: 10.7 us -> 8.87 us
    ppermute x4, starting transfers between devices: 3.01 us -> 10.6 us  [body(): other = lax.ppermute(known, 'leaf', [(i, i ^ step) for i in range(nodes)])]
    ppermute x1, starting transfers between devices: 6.02 us -> 0.07 us  [body(): cross = lax.ppermute(pack, ('leaf', 'sub'), others)]
    ppermute x4, waiting for transfers between devices: 8.58 us -> 2.94 us  [body(): other = lax.ppermute(known, 'leaf', [(i, i ^ step) for i in range(nodes)])]
    unnamed x23 -> x21, local copies, waits for them, and re-layouts: 1.97 us -> 0.05 us
    pallas_call x1, Pallas kernels: 1.54 us -> 0.08 us  [body(): pl.pallas_call(pack_kernel, out_shape=pltpu.VMEM((tiles, columns, 128), b...]
    concatenate x3, local copies, waits for them, and re-layouts: 1.3 us -> 0.02 us  [body(): known = jnp.concatenate([known, other], axis=0)]
    ppermute x1, starting transfers between devices: 0.01 us -> 0.5 us  [body(): own_other = lax.ppermute(pack, 'sub', swap)]
    pallas_call x1, Pallas kernels: 2.24 us -> 1.81 us  [fields(): pl.pallas_call(field_kernel, out_shape=(pltpu.VMEM((leaves, columns, poin...]
  transfers between devices with their start and end apart: 10 -> 10, of which waited for: 3 -> 2; matrix products, arithmetic and copies ran while one was open for 8% -> 0% of each run, Pallas kernels for 18% -> 17%
where the time goes in v5:
time: 24.1 us; the launch traced here: 24 us
  starting transfers between devices  11.9 us (49%)
  Pallas kernels  8.87 us (37%)
  waiting for transfers between devices  2.96 us (12%)
    ppermute x4, starting transfers between devices, body(): other = lax.ppermute(known, 'leaf', [(i, i ^ step) for i in range(nodes)])  10.6 us
    pallas_call x1, Pallas kernels, body(): pl.pallas_call(down_kernel, out_shape=jax.ShapeDtypeStruct((leaves, colum...  3.18 us
    ppermute x4, waiting for transfers between devices, body(): other = lax.ppermute(known, 'leaf', [(i, i ^ step) for i in range(nodes)])  2.94 us
    pallas_call x1, Pallas kernels, body(): pl.pallas_call(stage_kernel, out_shape=[pltpu.VMEM(x.shape, x.dtype) for...  2.17 us
    pallas_call x1, Pallas kernels, fields(): pl.pallas_call(field_kernel, out_shape=(pltpu.VMEM((leaves, columns, poin...  1.81 us
    pallas_call x1, Pallas kernels, body(): pl.pallas_call(up_kernel, out_shape=(pltpu.VMEM((leaves, columns, rank),...  1.63 us
    ppermute x1, starting transfers between devices, body(): own_other = lax.ppermute(pack, 'sub', swap)  0.5 us
  transfers between devices with their start and end apart: 10, of which 2 were waited for; matrix products, arithmetic and copies ran while one was open for 0% of the time, Pallas kernels for 17%

profile of v5, /device:TPU:0, one launch (start us, length us, event | category | flops | bytes accessed | tf_op | source)
XLA Modules:
  0.0 24.0 jit_solution(7819358474629275025)
XLA Ops:
  0.0 1.6 %up.1 = (bf16[8,16,64]{2,1,0:T(8,128)(2,1)S(1)}, bf16[16,128]{1,0:T(8,128)(2,1)S(1)}, bf16[8,16,256]{2,1,0:T(8,128)(2,1)S(1)}) custom-call(bf16[8,16,256]{2,1,0:T(8,128)(2,1)} %bitcast.13, bf16[8,64,256]{2,1,0:T(8,128)(2,1)} %bitcast.12, bf16[8,64,64]{2,1,0:T(8,128)(2,1)} %leaf_up.1, bf16[1,64,64]{2,1,0:T(8,128)(2,1)} %node_up.1), custom_call_target="tpu_custom_call" | custom-call | tf_op jit(solution)/shard_map/up/pallas_call | solution.py:200
  1.6 3.0 %collective-permute-start = (bf16[1,16,128]{2,1,0:T(8,128)(2,1)S(1)}, bf16[1,16,128]{2,1,0:T(8,128)(2,1)S(1)}, u32[]{:S(2)}, u32[]{:S(2)}) collective-permute-start(bf16[1,16,128]{2,1,0:T(8,128)(2,1)S(1)} %bitcast.9), channel_id=1, source_target_pairs={{0,2},{2,0},{4,6},{6,4},{8,10},{10,8},{12,14},{14,12},{16,18},{18,... | collective-permute-start | bytes 12296 | tf_op jit(solution)/shard_map/ppermute | solution.py:271
  4.6 0.1 pack.1.own
  4.7 0.0 collective-permute-start.2
  4.7 0.1 collective-permute-start.3
  4.8 0.5 %collective-permute-start.4 = (bf16[20,16,128]{2,1,0:T(8,128)(2,1)S(1)}, bf16[20,16,128]{2,1,0:T(8,128)(2,1)S(1)}, u32[]{:S(2)}, u32[]{:S(2)}) collective-permute-start(bf16[20,16,128]{2,1,0:T(8,128)(2,1)S(1)} %pack.1.own), channel_id=1, source_target_pairs={{0,1},{1,0},{2,3},{3,2},{4,5},{5,4},{6,7},{7,6},{8,9},{9,8},{10,11... | collective-permute-start | bytes 245768 | tf_op jit(solution)/shard_map/ppermute | solution.py:241
  5.3 0.9 %collective-permute-done = bf16[1,16,128]{2,1,0:T(8,128)(2,1)S(1)} collective-permute-done((bf16[1,16,128]{2,1,0:T(8,128)(2,1)S(1)}, bf16[1,16,128]{2,1,0:T(8,128)(2,1)S(1)}, u32[]{:S(2)}, u32[]{:S(2)}) %collective-permute-start) | collective-permute-done | bytes 4128 | tf_op jit(solution)/shard_map/ppermute | solution.py:271
  6.2 2.1 %collective-permute-start.1 = (bf16[2,16,128]{2,1,0:T(8,128)(2,1)S(1)}, bf16[2,16,128]{2,1,0:T(8,128)(2,1)S(1)}, u32[]{:S(2)}, u32[]{:S(2)}) collective-permute-start(bf16[2,16,128]{2,1,0:T(8,128)(2,1)S(1)} %constant_dynamic-update-slice_fusion), channel_id=1, source_target_pairs={{0,4},{2,6},{4,0},{6,2},{8,12},{10,14},{12,8},{14,10},{16,20},{18,... | collective-permute-start | bytes 24584 | tf_op jit(solution)/shard_map/ppermute | solution.py:271
  8.2 0.0 copy-start
  8.3 0.0 copy-start.1
  8.3 0.0 copy-start.2
  8.3 0.0 copy-start.3
  8.3 0.0 copy-start.4
  8.3 0.0 copy-start.5
  8.3 0.0 copy-start.6
  8.3 0.0 copy-start.7
  8.3 0.0 copy-start.8
  8.3 2.2 %stage.1 = (s32[3,8]{1,0:T(4,128)S(1)}, s32[3,8]{1,0:T(4,128)S(1)}, bf16[8,3,64,64]{3,2,1,0:T(8,128)(2,1)S(1)}, bf16[8,3,256,256]{3,2,1,0:T(8,128)(2,1)S(1)}) custom-call(s32[3,8]{1,0:T(4,128)} %bitcast.14, s32[3,8]{1,0:T(4,128)} %bitcast.15, bf16[8,3,64,64]{3,2,1,0:T(8,128)(2,1)} %refs_2_.1, bf16[8,3,256,256]{3,2,1,0:T(8,128)(2,1)} %refs_3_.1), custom_call_target="tpu_custom_call" | custom-call | tf_op jit(solution)/shard_map/stage/pallas_call | solution.py:222
  10.5 0.0 collective-permute-done.1
  10.5 0.0 collective-permute-done.2.pair
  10.5 0.0 collective-permute-done.3.cross
  10.5 0.0 collective-permute-done.4.own_other
  10.5 0.3 %collective-permute-start.6 = (bf16[20,16,128]{2,1,0:T(8,128)(2,1)S(1)}, bf16[20,16,128]{2,1,0:T(8,128)(2,1)S(1)}, u32[]{:S(2)}, u32[]{:S(2)}) collective-permute-start(bf16[20,16,128]{2,1,0:T(8,128)(2,1)S(1)} %collective-permute-done.2.pair), channel_id=1, source_target_pairs={{0,1},{1,0},{2,3},{3,2},{4,5},{5,4},{6,7},{7,6},{8,9},{9,8},{10,11... | collective-permute-start | bytes 245768 | tf_op jit(solution)/shard_map/ppermute | solution.py:278
  10.8 0.3 %collective-permute-start.7 = (bf16[20,16,128]{2,1,0:T(8,128)(2,1)S(1)}, bf16[20,16,128]{2,1,0:T(8,128)(2,1)S(1)}, u32[]{:S(2)}, u32[]{:S(2)}) collective-permute-start(bf16[20,16,128]{2,1,0:T(8,128)(2,1)S(1)} %collective-permute-done.3.cross), channel_id=1, source_target_pairs={{0,1},{1,0},{2,3},{3,2},{4,5},{5,4},{6,7},{7,6},{8,9},{9,8},{10,11... | collective-permute-start | bytes 245768 | tf_op jit(solution)/shard_map/ppermute | solution.py:279
  11.1 2.7 %collective-permute-start.5 = (bf16[4,16,128]{2,1,0:T(8,128)(2,1)S(1)}, bf16[4,16,128]{2,1,0:T(8,128)(2,1)S(1)}, u32[]{:S(2)}, u32[]{:S(2)}) collective-permute-start(bf16[4,16,128]{2,1,0:T(8,128)(2,1)S(1)} %constant_dynamic-update-slice_fusion.2), channel_id=1, source_target_pairs={{0,8},{2,10},{4,12},{6,14},{8,0},{10,2},{12,4},{14,6},{16,24},{18,... | collective-permute-start | bytes 49160 | tf_op jit(solution)/shard_map/ppermute | solution.py:271
  13.9 0.0 collective-permute-done.6.pair_other
  13.9 0.0 collective-permute-done.7.cross_other
  13.9 1.8 %fields.1 = (f32[8,16,256]{2,1,0:T(8,128)S(1)}, f32[8,16,64]{2,1,0:T(8,128)S(1)}, bf16[20,16,128]{2,1,0:T(8,128)(2,1)S(1)}) custom-call(s32[3,8]{1,0:T(4,128)S(1)} %get-tuple-element.43.near_list, s32[3,8]{1,0:T(4,128)S(1)} %get-tuple-element.44.far_list, bf16[20,16,128]{2,1,0:T(8,128)(2,1)S(1)} %collective-permute-done.2.pair, ...), custom_call_target="tpu_custom_call" | custom-call | flops 805306368 | bytes 3145728 | tf_op jit(solution)/shard_map/fields/pallas_call | solution.py:246
  15.7 0.0 collective-permute-done.5
  15.7 0.1 collective-permute-start.9
  15.8 2.9 %collective-permute-start.8 = (bf16[8,16,128]{2,1,0:T(8,128)(2,1)S(1)}, bf16[8,16,128]{2,1,0:T(8,128)(2,1)S(1)}, u32[]{:S(2)}, u32[]{:S(2)}) collective-permute-start(bf16[8,16,128]{2,1,0:T(8,128)(2,1)S(1)} %constant_dynamic-update-slice_fusion.4.known), channel_id=1, source_target_pairs={{0,16},{2,18},{4,20},{6,22},{8,24},{10,26},{12,28},{14,30},{16,0},... | collective-permute-start | bytes 98312 | tf_op jit(solution)/shard_map/ppermute | solution.py:271
  18.7 2.0 %collective-permute-done.8.other = bf16[8,16,128]{2,1,0:T(8,128)(2,1)S(1)} collective-permute-done((bf16[8,16,128]{2,1,0:T(8,128)(2,1)S(1)}, bf16[8,16,128]{2,1,0:T(8,128)(2,1)S(1)}, u32[]{:S(2)}, u32[]{:S(2)}) %collective-permute-start.8) | collective-permute-done | bytes 32800 | tf_op jit(solution)/shard_map/ppermute | solution.py:271
  20.7 0.0 collective-permute-done.9.received
  20.7 0.0 copy-done
  20.7 0.0 copy-done.1
  20.7 0.0 copy-done.2
  20.7 0.0 copy-done.3
  20.7 0.0 copy-done.4
  20.7 0.0 copy-done.5
  20.7 0.0 copy-done.6
  20.8 0.0 copy-done.7
  20.8 0.0 copy-done.8
  20.8 3.2 %down.1 = bf16[8,16,256]{2,1,0:T(8,128)(2,1)} custom-call(s32[1,4]{1,0:T(1,128)S(1)} %copy-done.8, s32[4,14]{1,0:T(4,128)S(1)} %bitcast.11, bf16[8,16,128]{2,1,0:T(8,128)(2,1)S(1)} %constant_dynamic-update-slice_fusion.4.known, bf16[8,16,128]{2,1,0:T(8,128)(2,1)S(1)} %collective-permute-done.8.other, f32[8,16,256]{2,1,0:T(8,128)S(1)} %get-tuple-element.56.near, ...), custom_call_target="tpu_custom_call" | custom-call | tf_op jit(solution)/shard_map/down/pallas_call | solution.py:289
  (6 shorter events, 0.0 us)
Async XLA Ops:
  1.6 4.5 %collective-permute-start = (bf16[1,16,128]{2,1,0:T(8,128)(2,1)S(1)}, bf16[1,16,128]{2,1,0:T(8,128)(2,1)S(1)}, u32[]{:S(2)}, u32[]{:S(2)}) collective-permute-start(bf16[1,16,128]{2,1,0:T(8,128)(2,1)S(1)} %bitcast.9), channel_id=1, source_target_pairs={{0,2},{2,0},{4,6},{6,4},{8,10},{10,8},{12,14},{14,12},{16,18},{18,... | collective-permute-start | bytes 12296 | tf_op jit(solution)/shard_map/ppermute | solution.py:271
  4.7 5.8 %collective-permute-start.2 = (bf16[20,16,128]{2,1,0:T(8,128)(2,1)S(1)}, bf16[20,16,128]{2,1,0:T(8,128)(2,1)S(1)}, u32[]{:S(2)}, u32[]{:S(2)}) collective-permute-start(bf16[20,16,128]{2,1,0:T(8,128)(2,1)S(1)} %pack.1.own), channel_id=1, source_target_pairs={{0,2},{2,0},{4,6},{6,4},{8,10},{10,8},{12,14},{14,12},{16,18},{18,... | collective-permute-start | bytes 245768 | tf_op jit(solution)/shard_map/ppermute | solution.py:231
  4.7 5.8 %collective-permute-start.3 = (bf16[20,16,128]{2,1,0:T(8,128)(2,1)S(1)}, bf16[20,16,128]{2,1,0:T(8,128)(2,1)S(1)}, u32[]{:S(2)}, u32[]{:S(2)}) collective-permute-start(bf16[20,16,128]{2,1,0:T(8,128)(2,1)S(1)} %pack.1.own), channel_id=1, source_target_pairs={{2,4},{3,5},{4,2},{5,3},{6,8},{7,9},{8,6},{9,7},{10,12},{11,13},{1... | collective-permute-start | bytes 245768 | tf_op jit(solution)/shard_map/ppermute | solution.py:240
  4.8 5.8 %collective-permute-start.4 = (bf16[20,16,128]{2,1,0:T(8,128)(2,1)S(1)}, bf16[20,16,128]{2,1,0:T(8,128)(2,1)S(1)}, u32[]{:S(2)}, u32[]{:S(2)}) collective-permute-start(bf16[20,16,128]{2,1,0:T(8,128)(2,1)S(1)} %pack.1.own), channel_id=1, source_target_pairs={{0,1},{1,0},{2,3},{3,2},{4,5},{5,4},{6,7},{7,6},{8,9},{9,8},{10,11... | collective-permute-start | bytes 245768 | tf_op jit(solution)/shard_map/ppermute | solution.py:241
  6.2 4.3 %collective-permute-start.1 = (bf16[2,16,128]{2,1,0:T(8,128)(2,1)S(1)}, bf16[2,16,128]{2,1,0:T(8,128)(2,1)S(1)}, u32[]{:S(2)}, u32[]{:S(2)}) collective-permute-start(bf16[2,16,128]{2,1,0:T(8,128)(2,1)S(1)} %constant_dynamic-update-slice_fusion), channel_id=1, source_target_pairs={{0,4},{2,6},{4,0},{6,2},{8,12},{10,14},{12,8},{14,10},{16,20},{18,... | collective-permute-start | bytes 24584 | tf_op jit(solution)/shard_map/ppermute | solution.py:271
  8.2 12.4 %copy-start = (bf16[14,4,64,64]{3,2,1,0:T(8,128)(2,1)S(1)}, bf16[14,4,64,64]{3,2,1,0:T(8,128)(2,1)}, u32[]{:S(2)}) copy-start(bf16[14,4,64,64]{3,2,1,0:T(8,128)(2,1)} %upper_coup.1) | copy-start | bytes 1376260
  8.3 12.4 %copy-start.1 = (bf16[8,256,64]{1,2,0:T(8,128)(2,1)S(1)}, bf16[8,256,64]{1,2,0:T(8,128)(2,1)}, u32[]{:S(2)}) copy-start(bf16[8,256,64]{1,2,0:T(8,128)(2,1)} %param.21) | copy-start | bytes 786436
  8.3 12.5 %copy-start.2 = (bf16[12,64,64]{2,1,0:T(8,128)(2,1)S(1)}, bf16[12,64,64]{2,1,0:T(8,128)(2,1)}, u32[]{:S(2)}) copy-start(bf16[12,64,64]{2,1,0:T(8,128)(2,1)} %upper_up.1) | copy-start | bytes 294916
  8.3 12.5 %copy-start.3 = (bf16[12,64,64]{2,1,0:T(8,128)(2,1)S(1)}, bf16[12,64,64]{2,1,0:T(8,128)(2,1)}, u32[]{:S(2)}) copy-start(bf16[12,64,64]{2,1,0:T(8,128)(2,1)} %upper_down.1) | copy-start | bytes 294916
  8.3 12.5 %copy-start.4 = (bf16[8,64,64]{2,1,0:T(8,128)(2,1)S(1)}, bf16[8,64,64]{2,1,0:T(8,128)(2,1)}, u32[]{:S(2)}) copy-start(bf16[8,64,64]{2,1,0:T(8,128)(2,1)} %leaf_down.1) | copy-start | bytes 196612
  8.3 12.5 %copy-start.5 = (bf16[1,4,64,64]{3,2,1,0:T(8,128)(2,1)S(1)}, bf16[1,4,64,64]{3,2,1,0:T(8,128)(2,1)}, u32[]{:S(2)}) copy-start(bf16[1,4,64,64]{3,2,1,0:T(8,128)(2,1)} %node_coup.1) | copy-start | bytes 98308
  8.3 12.5 %copy-start.6 = (bf16[1,64,64]{2,1,0:T(8,128)(2,1)S(1)}, bf16[1,64,64]{2,1,0:T(8,128)(2,1)}, u32[]{:S(2)}) copy-start(bf16[1,64,64]{2,1,0:T(8,128)(2,1)} %node_down.1) | copy-start | bytes 24580
  8.3 12.5 %copy-start.7 = (s32[14,4]{0,1:T(4,128)S(1)}, s32[14,4]{0,1:T(4,128)}, u32[]{:S(2)}) copy-start(s32[14,4]{0,1:T(4,128)} %param.31) | copy-start | bytes 676
  8.3 12.5 %copy-start.8 = (s32[1,4]{1,0:T(1,128)S(1)}, s32[1,4]{1,0:T(1,128)}, u32[]{:S(2)}) copy-start(s32[1,4]{1,0:T(1,128)} %node_list.1) | copy-start | bytes 52
  10.5 3.3 %collective-permute-start.6 = (bf16[20,16,128]{2,1,0:T(8,128)(2,1)S(1)}, bf16[20,16,128]{2,1,0:T(8,128)(2,1)S(1)}, u32[]{:S(2)}, u32[]{:S(2)}) collective-permute-start(bf16[20,16,128]{2,1,0:T(8,128)(2,1)S(1)} %collective-permute-done.2.pair), channel_id=1, source_target_pairs={{0,1},{1,0},{2,3},{3,2},{4,5},{5,4},{6,7},{7,6},{8,9},{9,8},{10,11... | collective-permute-start | bytes 245768 | tf_op jit(solution)/shard_map/ppermute | solution.py:278
  10.8 3.0 %collective-permute-start.7 = (bf16[20,16,128]{2,1,0:T(8,128)(2,1)S(1)}, bf16[20,16,128]{2,1,0:T(8,128)(2,1)S(1)}, u32[]{:S(2)}, u32[]{:S(2)}) collective-permute-start(bf16[20,16,128]{2,1,0:T(8,128)(2,1)S(1)} %collective-permute-done.3.cross), channel_id=1, source_target_pairs={{0,1},{1,0},{2,3},{3,2},{4,5},{5,4},{6,7},{7,6},{8,9},{9,8},{10,11... | collective-permute-start | bytes 245768 | tf_op jit(solution)/shard_map/ppermute | solution.py:279
  11.1 4.6 %collective-permute-start.5 = (bf16[4,16,128]{2,1,0:T(8,128)(2,1)S(1)}, bf16[4,16,128]{2,1,0:T(8,128)(2,1)S(1)}, u32[]{:S(2)}, u32[]{:S(2)}) collective-permute-start(bf16[4,16,128]{2,1,0:T(8,128)(2,1)S(1)} %constant_dynamic-update-slice_fusion.2), channel_id=1, source_target_pairs={{0,8},{2,10},{4,12},{6,14},{8,0},{10,2},{12,4},{14,6},{16,24},{18,... | collective-permute-start | bytes 49160 | tf_op jit(solution)/shard_map/ppermute | solution.py:271
  15.7 5.0 %collective-permute-start.9 = (bf16[20,16,128]{2,1,0:T(8,128)(2,1)S(1)}, bf16[20,16,128]{2,1,0:T(8,128)(2,1)S(1)}, u32[]{:S(2)}, u32[]{:S(2)}) collective-permute-start(bf16[20,16,128]{2,1,0:T(8,128)(2,1)S(1)} %get-tuple-element.58), channel_id=1, source_target_pairs={{0,1},{1,0},{2,3},{3,2},{4,5},{5,4},{6,7},{7,6},{8,9},{9,8},{10,11... | collective-permute-start | bytes 245768 | tf_op jit(solution)/shard_map/ppermute | solution.py:287
  15.8 4.9 %collective-permute-start.8 = (bf16[8,16,128]{2,1,0:T(8,128)(2,1)S(1)}, bf16[8,16,128]{2,1,0:T(8,128)(2,1)S(1)}, u32[]{:S(2)}, u32[]{:S(2)}) collective-permute-start(bf16[8,16,128]{2,1,0:T(8,128)(2,1)S(1)} %constant_dynamic-update-slice_fusion.4.known), channel_id=1, source_target_pairs={{0,16},{2,18},{4,20},{6,22},{8,24},{10,26},{12,28},{14,30},{16,0},... | collective-permute-start | bytes 98312 | tf_op jit(solution)/shard_map/ppermute | solution.py:271

commit v6 on v5

--- a/solution.py
+++ b/solution.py
@@ -118,56 +118,60 @@
         )
 
 
-def down_kernel(
-    node_list, upper_list, known, other, near, far, received, row, leaf_down, node_coup, node_down,
-    upper_coup, upper_up, upper_down, out, *tree,
+def weights_kernel(
+    node_list, upper_list, node_coup, node_down, upper_coup, upper_up, upper_down, leaf_down, row,
+    to_field, to_points, named, *tree,
 ):
-    half_nodes, columns, _ = known.shape
-    nodes = 2 * half_nodes
-    rank = row.shape[1]
-    leaves = row.shape[0]
-    gathered, tree = tree[0], tree[1:]
-    gathered[:half_nodes] = known[...]
-    gathered[half_nodes:] = other[...]
+    nodes, rank = to_field.shape[0], to_field.shape[1]
     farc = node_coup.shape[1]
     levels = nodes.bit_length() - 1
     me = lax.axis_index("leaf")
-
-    for m in range(nodes // 2):
-        left = gathered[(2 * m) ^ me, :, rank:].astype(jnp.float32)
-        right = gathered[(2 * m + 1) ^ me, :, rank:].astype(jnp.float32)
-        tree[levels - 2][m] = (left + right).astype(jnp.bfloat16)
-    for height in range(levels - 2, 0, -1):
-        breadth = 2**height
-        lower = tree[height]
-        for m in range(breadth):
-            first = 2 * (breadth + m) - 4
-            value = mm(lower[2 * m], upper_up[first], PLAIN)
-            value = value + mm(lower[2 * m + 1], upper_up[first + 1], PLAIN)
-            tree[height - 1][m] = value.astype(jnp.bfloat16)
-    field = None
+    for t in range(leaf_down.shape[0]):
+        to_points[t] = mm(leaf_down[t], row[t], (((0,), (0,)), ((), ()))).astype(jnp.bfloat16)
+    named[...] = jnp.zeros_like(named)
+    for j in range(farc):
+        place = node_list[0, j] ^ me
+        named[place] = named[place] + node_coup[0, j].astype(jnp.float32)
     for height in range(1, levels):
         breadth = 2**height
         node = (nodes + me) >> (levels - height)
-        total = None
+        level = tree[height - 1]
+        level[...] = jnp.zeros_like(level)
         for j in range(farc):
-            source = tree[height - 1][upper_list[j, node - 2] - breadth]
-            term = mm(source, upper_coup[node - 2, j], LAST)
-            total = term if total is None else total + term
+            place = upper_list[j, node - 2] - breadth
+            level[place] = level[place] + upper_coup[node - 2, j].astype(jnp.float32)
         if height > 1:
-            total = total + mm(field, upper_down[node - 4], LAST)
-        field = total.astype(jnp.bfloat16)
-    total = mm(field, node_down[0], LAST)
-    for j in range(farc):
-        source = gathered[node_list[0, j] ^ me, :, :rank]
-        total = total + mm(source, node_coup[0, j], LAST)
-    field = total.astype(jnp.bfloat16)
+            for parent in range(breadth // 2):
+                above = tree[height - 2][parent].astype(jnp.bfloat16)
+                above = mm(upper_down[node - 4], above, PLAIN).astype(jnp.bfloat16)
+                for m in (2 * parent, 2 * parent + 1):
+                    level[m] = level[m] + mm(above, upper_up[breadth + m - 4], LAST)
+    for parent in range(nodes // 2):
+        lifted = mm(node_down[0], tree[levels - 2][parent].astype(jnp.bfloat16), PLAIN)
+        lifted = lifted.astype(jnp.bfloat16)
+        for n in (2 * parent, 2 * parent + 1):
+            to_field[n ^ me, :, rank:] = lifted
+    for place in range(nodes):
+        to_field[place, :, :rank] = named[place].astype(jnp.bfloat16)
+
+
+def base_kernel(near, far, received, row, base):
+    leaves, rank = row.shape[0], row.shape[1]
     halves = near.shape[2] // 128
     for t in range(leaves):
         local = far[t] + unpack_short(received, t, leaves, halves, rank).astype(jnp.float32)
-        local = (local + mm(field, leaf_down[t], LAST)).astype(jnp.bfloat16)
         close = near[t] + unpack_long(received, t, halves).astype(jnp.float32)
-        out[t] = (close + mm(local, row[t], PLAIN)).astype(jnp.bfloat16)
+        base[t] = close + mm(local.astype(jnp.bfloat16), row[t], PLAIN)
+
+
+def down_kernel(known, other, to_field, to_points, base, out):
+    half = known.shape[0]
+    messages = [known[p] for p in range(half)] + [other[p] for p in range(half)]
+    matrices = [to_field[p] for p in range(2 * half)]
+    field = mm(jnp.concatenate(messages, axis=1), jnp.concatenate(matrices, axis=1), LAST)
+    field = field.astype(jnp.bfloat16)
+    for t in range(out.shape[0]):
+        out[t] = (base[t] + mm(field, to_points[t], PLAIN)).astype(jnp.bfloat16)
 
 
 def body(
@@ -207,6 +211,9 @@
         in_specs=[vmem()] * 4,
         out_specs=(vmem(),) * 3,
         compiler_params=limit(4),
+        cost_estimate=pl.CostEstimate(
+            flops=2_000_000_000, bytes_accessed=5_000_000, transcendentals=0
+        ),
         name="up",
     )(*[pinned(x, pltpu.HBM) for x in (dens, jnp.swapaxes(col_basis, 1, 2), leaf_up, node_up)])
     tiles = leaves * (points // 128) + leaves // 2
@@ -216,19 +223,12 @@
         in_specs=[vmem()] * 2,
         out_specs=vmem(),
         compiler_params=limit(4),
+        cost_estimate=pl.CostEstimate(
+            flops=2_000_000_000, bytes_accessed=5_000_000, transcendentals=0
+        ),
         name="pack",
     )(pinned(dens_here, pltpu.VMEM), pinned(coeff, pltpu.VMEM))
-    staged = [near_index.T, leaf_list.T, leaf_coupling, near_blocks]
-    staged = pl.pallas_call(
-        stage_kernel,
-        out_shape=[pltpu.VMEM(x.shape, x.dtype) for x in staged],
-        in_specs=[pl.BlockSpec(memory_space=pl.ANY)] * 4,
-        out_specs=[vmem()] * 4,
-        scratch_shapes=[pltpu.SemaphoreType.DMA((4,))],
-        compiler_params=limit(4),
-        name="stage",
-    )(*[pinned(x, pltpu.HBM) for x in staged])
-    pair = lax.ppermute(pack, "leaf", [(i, i ^ 1) for i in range(nodes)])
+    staged = (near_index.T, leaf_list.T, leaf_coupling, near_blocks)
     cores = lax.axis_size("sub")
     others = [
         (i * cores + c, (i + 1 if i % 2 else i - 1) * cores + c)
@@ -238,7 +238,6 @@
     others += [(i * cores + c, i * cores + 1 - c) for i in (0, nodes - 1) for c in range(cores)]
 
     cross = lax.ppermute(pack, ("leaf", "sub"), others)
-    own_other = lax.ppermute(pack, "sub", swap)
 
     entries = near_blocks.shape[1]
 
@@ -265,15 +264,38 @@
             name="fields",
         )(staged[0], staged[1], *packs, staged[2], staged[3])
 
+    row = jnp.swapaxes(row_basis, 1, 2)
+    weights = pl.pallas_call(
+        weights_kernel,
+        out_shape=(
+            pltpu.VMEM((nodes, rank, 2 * rank), bf16),
+            pltpu.VMEM((leaves, rank, points), bf16),
+        ),
+        in_specs=[smem()] * 2 + [vmem()] * 7,
+        out_specs=(vmem(),) * 2,
+        scratch_shapes=[pltpu.VMEM((nodes, rank, rank), f32)]
+        + [pltpu.VMEM((2**height, rank, rank), f32) for height in range(1, levels)],
+        compiler_params=limit(16),
+        cost_estimate=pl.CostEstimate(
+            flops=2_000_000_000, bytes_accessed=3_000_000, transcendentals=0
+        ),
+        name="weights",
+    )(
+        node_list, upper_list.T, node_coupling, node_down, upper_coupling, upper_up, upper_down,
+        leaf_down, row,
+    )
+
     known = message[None]
     for bit in range(levels):
         step = 1 << bit
         other = lax.ppermute(known, "leaf", [(i, i ^ step) for i in range(nodes)])
         if bit == 0:
             known, other, pack = lax.optimization_barrier((known, other, pack))
+            pair = lax.ppermute(pack, "leaf", [(i, i ^ 1) for i in range(nodes)])
+            own_other = lax.ppermute(pack, "sub", swap)
         if bit == 1:
-            known, other, pair, cross, own_other, staged = lax.optimization_barrier(
-                (known, other, pair, cross, own_other, staged)
+            known, other, pair, cross, own_other, weights = lax.optimization_barrier(
+                (known, other, pair, cross, own_other, weights)
             )
             pair_other = lax.ppermute(pair, "sub", swap)
             cross_other = lax.ppermute(cross, "sub", swap)
@@ -285,20 +307,26 @@
         if bit < levels - 1:
             known = jnp.concatenate([known, other], axis=0)
     received = lax.ppermute(send, "sub", swap)
-
+    base = pl.pallas_call(
+        base_kernel,
+        out_shape=pltpu.VMEM((leaves, columns, points), f32),
+        in_specs=[vmem()] * 4,
+        out_specs=vmem(),
+        compiler_params=limit(4),
+        cost_estimate=pl.CostEstimate(
+            flops=1_000_000_000, bytes_accessed=1_000_000, transcendentals=0
+        ),
+        name="base",
+    )(near, far, received, row)
+    other, base = lax.optimization_barrier((other, base))
     out = pl.pallas_call(
         down_kernel,
         out_shape=jax.ShapeDtypeStruct((leaves, columns, points), bf16),
-        in_specs=[smem()] * 2 + [vmem()] * 12,
+        in_specs=[vmem()] * 5,
         out_specs=vmem(),
-        scratch_shapes=[pltpu.VMEM((nodes, columns, 2 * rank), bf16)]
-        + [pltpu.VMEM((2**height, columns, rank), bf16) for height in range(1, levels)],
         compiler_params=limit(8),
         name="down",
-    )(
-        node_list, upper_list.T, known, other, near, far, received,
-        jnp.swapaxes(row_basis, 1, 2), leaf_down, node_coupling, node_down, upper_coupling, upper_up, upper_down,
-    )
+    )(known, other, *weights, base)
     return jnp.swapaxes(out, 1, 2)
 
 

time: 24.1 us -> 22.3 us (0.925)
  Pallas kernels: 8.87 us -> 6.64 us
  waiting for transfers between devices: 2.96 us -> 3.87 us
  starting transfers between devices: 11.9 us -> 11.4 us
    pallas_call x1, Pallas kernels: 3.18 us -> 1.03 us  [body(): pl.pallas_call(down_kernel, out_shape=jax.ShapeDtypeStruct((leaves, colum...]
    ppermute x1, starting transfers between devices: 0.02 us -> 2.02 us  [body(): pair = lax.ppermute(pack, 'leaf', [(i, i ^ 1) for i in range(nodes)])]
    ppermute x4, starting transfers between devices: 10.6 us -> 8.76 us  [body(): other = lax.ppermute(known, 'leaf', [(i, i ^ step) for i in range(nodes)])]
    ppermute x4, waiting for transfers between devices: 2.94 us -> 3.85 us  [body(): other = lax.ppermute(known, 'leaf', [(i, i ^ step) for i in range(nodes)])]
    ppermute x1, starting transfers between devices: 0.5 us -> 0.01 us  [body(): own_other = lax.ppermute(pack, 'sub', swap)]
    pallas_call x1 -> x2, Pallas kernels: 2.17 us -> 2.09 us  [the longest x1 1.88 us: body(): pl.pallas_call(weights_kernel, out_shape=(pltpu.VMEM((nodes, rank, 2 * ra...]
  transfers between devices with their start and end apart: 10 -> 10, of which waited for: 2 -> 4; matrix products, arithmetic and copies ran while one was open for 0% -> 0% of each run, Pallas kernels for 17% -> 18%
where the time goes in v6:
time: 22.3 us; the launch traced here: 22.2 us
  starting transfers between devices  11.4 us (51%)
  Pallas kernels  6.64 us (30%)
  waiting for transfers between devices  3.87 us (17%)
    ppermute x4, starting transfers between devices, body(): other = lax.ppermute(known, 'leaf', [(i, i ^ step) for i in range(nodes)])  8.76 us
    ppermute x4, waiting for transfers between devices, body(): other = lax.ppermute(known, 'leaf', [(i, i ^ step) for i in range(nodes)])  3.85 us
    ppermute x1, starting transfers between devices, body(): pair = lax.ppermute(pack, 'leaf', [(i, i ^ 1) for i in range(nodes)])  2.02 us
    pallas_call x1, Pallas kernels, body(): pl.pallas_call(weights_kernel, out_shape=(pltpu.VMEM((nodes, rank, 2 * ra...  1.88 us
    pallas_call x1, Pallas kernels, fields(): pl.pallas_call(field_kernel, out_shape=(pltpu.VMEM((leaves, columns, poin...  1.81 us
    pallas_call x1, Pallas kernels, body(): pl.pallas_call(up_kernel, out_shape=(pltpu.VMEM((leaves, columns, rank),...  1.63 us
    pallas_call x1, Pallas kernels, body(): pl.pallas_call(down_kernel, out_shape=jax.ShapeDtypeStruct((leaves, colum...  1.03 us
  transfers between devices with their start and end apart: 10, of which 4 were waited for; matrix products, arithmetic and copies ran while one was open for 0% of the time, Pallas kernels for 18%

profile of v6, /device:TPU:0, one launch (start us, length us, event | category | flops | bytes accessed | tf_op | source)
XLA Modules:
  0.0 22.2 jit_solution(6071564584523912801)
XLA Ops:
  0.0 1.6 %up.1 = (bf16[8,16,64]{2,1,0:T(8,128)(2,1)S(1)}, bf16[16,128]{1,0:T(8,128)(2,1)S(1)}, bf16[8,16,256]{2,1,0:T(8,128)(2,1)S(1)}) custom-call(bf16[8,16,256]{2,1,0:T(8,128)(2,1)} %bitcast.16, bf16[8,64,256]{2,1,0:T(8,128)(2,1)} %bitcast.15, bf16[8,64,64]{2,1,0:T(8,128)(2,1)} %leaf_up.1, bf16[1,64,64]{2,1,0:T(8,128)(2,1)} %node_up.1), custom_call_target="tpu_custom_call" | custom-call | flops 2000000000 | bytes 5000000 | tf_op jit(solution)/shard_map/up/pallas_call | solution.py:204
  1.6 3.0 %collective-permute-start = (bf16[1,16,128]{2,1,0:T(8,128)(2,1)S(1)}, bf16[1,16,128]{2,1,0:T(8,128)(2,1)S(1)}, u32[]{:S(2)}, u32[]{:S(2)}) collective-permute-start(bf16[1,16,128]{2,1,0:T(8,128)(2,1)S(1)} %bitcast.8), channel_id=1, source_target_pairs={{0,2},{2,0},{4,6},{6,4},{8,10},{10,8},{12,14},{14,12},{16,18},{18,... | collective-permute-start | bytes 12296 | tf_op jit(solution)/shard_map/ppermute | solution.py:291
  4.6 0.0 copy-start.4
  4.6 0.0 copy-start.5
  4.6 0.0 copy-start.6
  4.6 0.0 copy-start.7
  4.6 0.0 copy-start.8
  4.6 0.0 copy-start.9
  4.6 0.0 copy-start.10
  4.6 0.0 copy-start.11
  4.6 0.0 copy-start.12
  4.7 0.1 pack.1.own
  4.7 0.0 collective-permute-start.3
  4.8 1.4 %collective-permute-done = bf16[1,16,128]{2,1,0:T(8,128)(2,1)S(1)} collective-permute-done((bf16[1,16,128]{2,1,0:T(8,128)(2,1)S(1)}, bf16[1,16,128]{2,1,0:T(8,128)(2,1)S(1)}, u32[]{:S(2)}, u32[]{:S(2)}) %collective-permute-start) | collective-permute-done | bytes 4128 | tf_op jit(solution)/shard_map/ppermute | solution.py:291
  6.2 2.0 %collective-permute-start.2 = (bf16[20,16,128]{2,1,0:T(8,128)(2,1)S(1)}, bf16[20,16,128]{2,1,0:T(8,128)(2,1)S(1)}, u32[]{:S(2)}, u32[]{:S(2)}) collective-permute-start(bf16[20,16,128]{2,1,0:T(8,128)(2,1)S(1)} %pack.1.own), channel_id=1, source_target_pairs={{0,2},{2,0},{4,6},{6,4},{8,10},{10,8},{12,14},{14,12},{16,18},{18,... | collective-permute-start | bytes 245768 | tf_op jit(solution)/shard_map/ppermute | solution.py:294
  8.2 0.0 collective-permute-start.4
  8.2 1.6 %collective-permute-start.1 = (bf16[2,16,128]{2,1,0:T(8,128)(2,1)S(1)}, bf16[2,16,128]{2,1,0:T(8,128)(2,1)S(1)}, u32[]{:S(2)}, u32[]{:S(2)}) collective-permute-start(bf16[2,16,128]{2,1,0:T(8,128)(2,1)S(1)} %constant_dynamic-update-slice_fusion), channel_id=1, source_target_pairs={{0,4},{2,6},{4,0},{6,2},{8,12},{10,14},{12,8},{14,10},{16,20},{18,... | collective-permute-start | bytes 24584 | tf_op jit(solution)/shard_map/ppermute | solution.py:291
  9.8 0.0 copy-done.4
  9.8 0.0 copy-done.5
  9.8 0.0 copy-done.6
  9.8 0.0 copy-done.7
  9.8 0.0 copy-done.8
  9.8 0.0 copy-done.9
  9.8 0.0 copy-done.10
  9.8 0.0 copy-done.11
  9.8 0.0 copy-done.12
  9.9 0.0 copy-start
  9.9 0.0 copy-start.1
  9.9 0.0 copy-start.2
  9.9 0.0 copy-start.3
  9.9 1.9 %weights.1 = (bf16[16,64,128]{2,1,0:T(8,128)(2,1)S(1)}, bf16[8,64,256]{2,1,0:T(8,128)(2,1)S(1)}) custom-call(s32[1,4]{1,0:T(1,128)S(1)} %copy-done.12, s32[4,14]{1,0:T(4,128)S(1)} %bitcast.14, bf16[1,4,64,64]{3,2,1,0:T(8,128)(2,1)S(1)} %copy-done.9, bf16[1,64,64]{2,1,0:T(8,128)(2,1)S(1)} %copy-done.10, bf16[14,4,64,64]{3,2,1,0:T(8,128)(2,1)S(1)} %copy-done.4, ...), custom_call_target="tpu_custom_call" | custom-call | flops 2000000000 | bytes 3000000 | tf_op jit(solution)/shard_map/weights/pallas_call | solution.py:268
  11.8 0.1 collective-permute-done.1
  11.9 0.0 collective-permute-done.3.cross
  11.9 0.0 collective-permute-done.2.pair
  11.9 0.0 collective-permute-done.4.own_other
  11.9 0.1 collective-permute-start.6
  12.1 0.4 %collective-permute-start.7 = (bf16[20,16,128]{2,1,0:T(8,128)(2,1)S(1)}, bf16[20,16,128]{2,1,0:T(8,128)(2,1)S(1)}, u32[]{:S(2)}, u32[]{:S(2)}) collective-permute-start(bf16[20,16,128]{2,1,0:T(8,128)(2,1)S(1)} %collective-permute-done.3.cross), channel_id=1, source_target_pairs={{0,1},{1,0},{2,3},{3,2},{4,5},{5,4},{6,7},{7,6},{8,9},{9,8},{10,11... | collective-permute-start | bytes 245768 | tf_op jit(solution)/shard_map/ppermute | solution.py:301
  12.5 1.6 %collective-permute-start.5 = (bf16[4,16,128]{2,1,0:T(8,128)(2,1)S(1)}, bf16[4,16,128]{2,1,0:T(8,128)(2,1)S(1)}, u32[]{:S(2)}, u32[]{:S(2)}) collective-permute-start(bf16[4,16,128]{2,1,0:T(8,128)(2,1)S(1)} %constant_dynamic-update-slice_fusion.2), channel_id=1, source_target_pairs={{0,8},{2,10},{4,12},{6,14},{8,0},{10,2},{12,4},{14,6},{16,24},{18,... | collective-permute-start | bytes 49160 | tf_op jit(solution)/shard_map/ppermute | solution.py:291
  14.1 0.0 collective-permute-done.6.pair_other
  14.1 0.0 collective-permute-done.7.cross_other
  14.1 0.0 copy-done
  14.1 0.0 copy-done.1
  14.1 0.0 copy-done.2
  14.1 0.0 copy-done.3
  14.1 1.8 %fields.1 = (f32[8,16,256]{2,1,0:T(8,128)S(1)}, f32[8,16,64]{2,1,0:T(8,128)S(1)}, bf16[20,16,128]{2,1,0:T(8,128)(2,1)S(1)}) custom-call(s32[3,8]{1,0:T(4,128)S(1)} %bitcast.10, s32[3,8]{1,0:T(4,128)S(1)} %bitcast.11, bf16[20,16,128]{2,1,0:T(8,128)(2,1)S(1)} %collective-permute-done.2.pair, bf16[20,16,128]{2,1,0:T(8,128)(2,1)S(1)} %pack.1.own, ...), custom_call_target="tpu_custom_call" | custom-call | flops 805306368 | bytes 3145728 | tf_op jit(solution)/shard_map/fields/pallas_call | solution.py:245
  16.0 0.3 %collective-permute-done.5 = bf16[4,16,128]{2,1,0:T(8,128)(2,1)S(1)} collective-permute-done((bf16[4,16,128]{2,1,0:T(8,128)(2,1)S(1)}, bf16[4,16,128]{2,1,0:T(8,128)(2,1)S(1)}, u32[]{:S(2)}, u32[]{:S(2)}) %collective-permute-start.5) | collective-permute-done | bytes 16416 | tf_op jit(solution)/shard_map/ppermute | solution.py:291
  16.3 0.0 collective-permute-start.9
  16.3 2.7 %collective-permute-start.8 = (bf16[8,16,128]{2,1,0:T(8,128)(2,1)S(1)}, bf16[8,16,128]{2,1,0:T(8,128)(2,1)S(1)}, u32[]{:S(2)}, u32[]{:S(2)}) collective-permute-start(bf16[8,16,128]{2,1,0:T(8,128)(2,1)S(1)} %constant_dynamic-update-slice_fusion.4.known), channel_id=1, source_target_pairs={{0,16},{2,18},{4,20},{6,22},{8,24},{10,26},{12,28},{14,30},{16,0},... | collective-permute-start | bytes 98312 | tf_op jit(solution)/shard_map/ppermute | solution.py:291
  18.9 0.0 collective-permute-done.9.received
  18.9 0.2 base.1
  19.1 2.0 %collective-permute-done.8.other = bf16[8,16,128]{2,1,0:T(8,128)(2,1)S(1)} collective-permute-done((bf16[8,16,128]{2,1,0:T(8,128)(2,1)S(1)}, bf16[8,16,128]{2,1,0:T(8,128)(2,1)S(1)}, u32[]{:S(2)}, u32[]{:S(2)}) %collective-permute-start.8) | collective-permute-done | bytes 32800 | tf_op jit(solution)/shard_map/ppermute | solution.py:291
  21.1 1.0 %down.1 = bf16[8,16,256]{2,1,0:T(8,128)(2,1)} custom-call(bf16[8,16,128]{2,1,0:T(8,128)(2,1)S(1)} %constant_dynamic-update-slice_fusion.4.known, bf16[8,16,128]{2,1,0:T(8,128)(2,1)S(1)} %collective-permute-done.8.other, bf16[16,64,128]{2,1,0:T(8,128)(2,1)S(1)} %get-tuple-element.52.to_field, bf16[8,64,256]{2,1,0:T(8,128)(2,1)S(1)} %get-tuple-element.53.to_points, ...), custom_call_target="tpu_custom_call" | custom-call | tf_op jit(solution)/shard_map/down/pallas_call | solution.py:322
  (6 shorter events, 0.0 us)
Async XLA Ops:
  1.6 4.5 %collective-permute-start = (bf16[1,16,128]{2,1,0:T(8,128)(2,1)S(1)}, bf16[1,16,128]{2,1,0:T(8,128)(2,1)S(1)}, u32[]{:S(2)}, u32[]{:S(2)}) collective-permute-start(bf16[1,16,128]{2,1,0:T(8,128)(2,1)S(1)} %bitcast.8), channel_id=1, source_target_pairs={{0,2},{2,0},{4,6},{6,4},{8,10},{10,8},{12,14},{14,12},{16,18},{18,... | collective-permute-start | bytes 12296 | tf_op jit(solution)/shard_map/ppermute | solution.py:291
  4.6 5.2 %copy-start.4 = (bf16[14,4,64,64]{3,2,1,0:T(8,128)(2,1)S(1)}, bf16[14,4,64,64]{3,2,1,0:T(8,128)(2,1)}, u32[]{:S(2)}) copy-start(bf16[14,4,64,64]{3,2,1,0:T(8,128)(2,1)} %upper_coup.1) | copy-start | bytes 1376260
  4.6 5.2 %copy-start.5 = (bf16[8,256,64]{1,2,0:T(8,128)(2,1)S(1)}, bf16[8,256,64]{1,2,0:T(8,128)(2,1)}, u32[]{:S(2)}) copy-start(bf16[8,256,64]{1,2,0:T(8,128)(2,1)} %param.21) | copy-start | bytes 786436
  4.6 5.2 %copy-start.6 = (bf16[12,64,64]{2,1,0:T(8,128)(2,1)S(1)}, bf16[12,64,64]{2,1,0:T(8,128)(2,1)}, u32[]{:S(2)}) copy-start(bf16[12,64,64]{2,1,0:T(8,128)(2,1)} %upper_up.1) | copy-start | bytes 294916
  4.6 5.2 %copy-start.7 = (bf16[12,64,64]{2,1,0:T(8,128)(2,1)S(1)}, bf16[12,64,64]{2,1,0:T(8,128)(2,1)}, u32[]{:S(2)}) copy-start(bf16[12,64,64]{2,1,0:T(8,128)(2,1)} %upper_down.1) | copy-start | bytes 294916
  4.6 5.2 %copy-start.8 = (bf16[8,64,64]{2,1,0:T(8,128)(2,1)S(1)}, bf16[8,64,64]{2,1,0:T(8,128)(2,1)}, u32[]{:S(2)}) copy-start(bf16[8,64,64]{2,1,0:T(8,128)(2,1)} %leaf_down.1) | copy-start | bytes 196612
  4.6 5.2 %copy-start.9 = (bf16[1,4,64,64]{3,2,1,0:T(8,128)(2,1)S(1)}, bf16[1,4,64,64]{3,2,1,0:T(8,128)(2,1)}, u32[]{:S(2)}) copy-start(bf16[1,4,64,64]{3,2,1,0:T(8,128)(2,1)} %node_coup.1) | copy-start | bytes 98308
  4.6 5.2 %copy-start.10 = (bf16[1,64,64]{2,1,0:T(8,128)(2,1)S(1)}, bf16[1,64,64]{2,1,0:T(8,128)(2,1)}, u32[]{:S(2)}) copy-start(bf16[1,64,64]{2,1,0:T(8,128)(2,1)} %node_down.1) | copy-start | bytes 24580
  4.6 5.2 %copy-start.11 = (s32[14,4]{0,1:T(4,128)S(1)}, s32[14,4]{0,1:T(4,128)}, u32[]{:S(2)}) copy-start(s32[14,4]{0,1:T(4,128)} %param.31) | copy-start | bytes 676
  4.6 5.2 %copy-start.12 = (s32[1,4]{1,0:T(1,128)S(1)}, s32[1,4]{1,0:T(1,128)}, u32[]{:S(2)}) copy-start(s32[1,4]{1,0:T(1,128)} %node_list.1) | copy-start | bytes 52
  4.7 7.2 %collective-permute-start.3 = (bf16[20,16,128]{2,1,0:T(8,128)(2,1)S(1)}, bf16[20,16,128]{2,1,0:T(8,128)(2,1)S(1)}, u32[]{:S(2)}, u32[]{:S(2)}) collective-permute-start(bf16[20,16,128]{2,1,0:T(8,128)(2,1)S(1)} %pack.1.own), channel_id=1, source_target_pairs={{2,4},{3,5},{4,2},{5,3},{6,8},{7,9},{8,6},{9,7},{10,12},{11,13},{1... | collective-permute-start | bytes 245768 | tf_op jit(solution)/shard_map/ppermute | solution.py:240
  6.2 5.8 %collective-permute-start.2 = (bf16[20,16,128]{2,1,0:T(8,128)(2,1)S(1)}, bf16[20,16,128]{2,1,0:T(8,128)(2,1)S(1)}, u32[]{:S(2)}, u32[]{:S(2)}) collective-permute-start(bf16[20,16,128]{2,1,0:T(8,128)(2,1)S(1)} %pack.1.own), channel_id=1, source_target_pairs={{0,2},{2,0},{4,6},{6,4},{8,10},{10,8},{12,14},{14,12},{16,18},{18,... | collective-permute-start | bytes 245768 | tf_op jit(solution)/shard_map/ppermute | solution.py:294
  8.2 3.7 %collective-permute-start.4 = (bf16[20,16,128]{2,1,0:T(8,128)(2,1)S(1)}, bf16[20,16,128]{2,1,0:T(8,128)(2,1)S(1)}, u32[]{:S(2)}, u32[]{:S(2)}) collective-permute-start(bf16[20,16,128]{2,1,0:T(8,128)(2,1)S(1)} %pack.1.own), channel_id=1, source_target_pairs={{0,1},{1,0},{2,3},{3,2},{4,5},{5,4},{6,7},{7,6},{8,9},{9,8},{10,11... | collective-permute-start | bytes 245768 | tf_op jit(solution)/shard_map/ppermute | solution.py:295
  8.2 3.7 %collective-permute-start.1 = (bf16[2,16,128]{2,1,0:T(8,128)(2,1)S(1)}, bf16[2,16,128]{2,1,0:T(8,128)(2,1)S(1)}, u32[]{:S(2)}, u32[]{:S(2)}) collective-permute-start(bf16[2,16,128]{2,1,0:T(8,128)(2,1)S(1)} %constant_dynamic-update-slice_fusion), channel_id=1, source_target_pairs={{0,4},{2,6},{4,0},{6,2},{8,12},{10,14},{12,8},{14,10},{16,20},{18,... | collective-permute-start | bytes 24584 | tf_op jit(solution)/shard_map/ppermute | solution.py:291
  9.9 4.3 %copy-start = (bf16[8,3,256,256]{3,2,1,0:T(8,128)(2,1)S(1)}, bf16[8,3,256,256]{3,2,1,0:T(8,128)(2,1)}, u32[]{:S(2)}) copy-start(bf16[8,3,256,256]{3,2,1,0:T(8,128)(2,1)} %near.1) | copy-start | bytes 9437188
  9.9 4.2 %copy-start.1 = (bf16[8,3,64,64]{3,2,1,0:T(8,128)(2,1)S(1)}, bf16[8,3,64,64]{3,2,1,0:T(8,128)(2,1)}, u32[]{:S(2)}) copy-start(bf16[8,3,64,64]{3,2,1,0:T(8,128)(2,1)} %coup.1) | copy-start | bytes 589828
  9.9 4.2 %copy-start.2 = (s32[8,3]{0,1:T(4,128)S(1)}, s32[8,3]{0,1:T(4,128)}, u32[]{:S(2)}) copy-start(s32[8,3]{0,1:T(4,128)} %param.19) | copy-start | bytes 292
  9.9 4.2 %copy-start.3 = (s32[8,3]{0,1:T(4,128)S(1)}, s32[8,3]{0,1:T(4,128)}, u32[]{:S(2)}) copy-start(s32[8,3]{0,1:T(4,128)} %param.23) | copy-start | bytes 292
  11.9 2.2 %collective-permute-start.6 = (bf16[20,16,128]{2,1,0:T(8,128)(2,1)S(1)}, bf16[20,16,128]{2,1,0:T(8,128)(2,1)S(1)}, u32[]{:S(2)}, u32[]{:S(2)}) collective-permute-start(bf16[20,16,128]{2,1,0:T(8,128)(2,1)S(1)} %collective-permute-done.2.pair), channel_id=1, source_target_pairs={{0,1},{1,0},{2,3},{3,2},{4,5},{5,4},{6,7},{7,6},{8,9},{9,8},{10,11... | collective-permute-start | bytes 245768 | tf_op jit(solution)/shard_map/ppermute | solution.py:300
  12.1 2.0 %collective-permute-start.7 = (bf16[20,16,128]{2,1,0:T(8,128)(2,1)S(1)}, bf16[20,16,128]{2,1,0:T(8,128)(2,1)S(1)}, u32[]{:S(2)}, u32[]{:S(2)}) collective-permute-start(bf16[20,16,128]{2,1,0:T(8,128)(2,1)S(1)} %collective-permute-done.3.cross), channel_id=1, source_target_pairs={{0,1},{1,0},{2,3},{3,2},{4,5},{5,4},{6,7},{7,6},{8,9},{9,8},{10,11... | collective-permute-start | bytes 245768 | tf_op jit(solution)/shard_map/ppermute | solution.py:301
  12.5 3.7 %collective-permute-start.5 = (bf16[4,16,128]{2,1,0:T(8,128)(2,1)S(1)}, bf16[4,16,128]{2,1,0:T(8,128)(2,1)S(1)}, u32[]{:S(2)}, u32[]{:S(2)}) collective-permute-start(bf16[4,16,128]{2,1,0:T(8,128)(2,1)S(1)} %constant_dynamic-update-slice_fusion.2), channel_id=1, source_target_pairs={{0,8},{2,10},{4,12},{6,14},{8,0},{10,2},{12,4},{14,6},{16,24},{18,... | collective-permute-start | bytes 49160 | tf_op jit(solution)/shard_map/ppermute | solution.py:291
  16.3 2.7 %collective-permute-start.9 = (bf16[20,16,128]{2,1,0:T(8,128)(2,1)S(1)}, bf16[20,16,128]{2,1,0:T(8,128)(2,1)S(1)}, u32[]{:S(2)}, u32[]{:S(2)}) collective-permute-start(bf16[20,16,128]{2,1,0:T(8,128)(2,1)S(1)} %get-tuple-element.50), channel_id=1, source_target_pairs={{0,1},{1,0},{2,3},{3,2},{4,5},{5,4},{6,7},{7,6},{8,9},{9,8},{10,11... | collective-permute-start | bytes 245768 | tf_op jit(solution)/shard_map/ppermute | solution.py:309
  16.3 4.9 %collective-permute-start.8 = (bf16[8,16,128]{2,1,0:T(8,128)(2,1)S(1)}, bf16[8,16,128]{2,1,0:T(8,128)(2,1)S(1)}, u32[]{:S(2)}, u32[]{:S(2)}) collective-permute-start(bf16[8,16,128]{2,1,0:T(8,128)(2,1)S(1)} %constant_dynamic-update-slice_fusion.4.known), channel_id=1, source_target_pairs={{0,16},{2,18},{4,20},{6,22},{8,24},{10,26},{12,28},{14,30},{16,0},... | collective-permute-start | bytes 98312 | tf_op jit(solution)/shard_map/ppermute | solution.py:291

commit v7 on v6

--- a/solution.py
+++ b/solution.py
@@ -238,6 +238,8 @@
     others += [(i * cores + c, i * cores + 1 - c) for i in (0, nodes - 1) for c in range(cores)]
 
     cross = lax.ppermute(pack, ("leaf", "sub"), others)
+    pair = lax.ppermute(pack, "leaf", [(i, i ^ 1) for i in range(nodes)])
+    own_other = lax.ppermute(pack, "sub", swap)
 
     entries = near_blocks.shape[1]
 
@@ -291,11 +293,9 @@
         other = lax.ppermute(known, "leaf", [(i, i ^ step) for i in range(nodes)])
         if bit == 0:
             known, other, pack = lax.optimization_barrier((known, other, pack))
-            pair = lax.ppermute(pack, "leaf", [(i, i ^ 1) for i in range(nodes)])
-            own_other = lax.ppermute(pack, "sub", swap)
         if bit == 1:
-            known, other, pair, cross, own_other, weights = lax.optimization_barrier(
-                (known, other, pair, cross, own_other, weights)
+            known, other, cross, pair, own_other, weights = lax.optimization_barrier(
+                (known, other, cross, pair, own_other, weights)
             )
             pair_other = lax.ppermute(pair, "sub", swap)
             cross_other = lax.ppermute(cross, "sub", swap)

time: 22.3 us -> 21.9 us (0.982)
  waiting for transfers between devices: 3.87 us -> 2.46 us
  starting transfers between devices: 11.4 us -> 12.3 us
    ppermute x4, waiting for transfers between devices: 3.85 us -> 2.45 us  [body(): other = lax.ppermute(known, 'leaf', [(i, i ^ step) for i in range(nodes)])]
    ppermute x1, starting transfers between devices: 2.02 us -> 2.97 us  [body(): pair = lax.ppermute(pack, 'leaf', [(i, i ^ 1) for i in range(nodes)])]
  transfers between devices with their start and end apart: 10 -> 10, of which waited for: 4 -> 3; matrix products, arithmetic and copies ran while one was open for 0% -> 0% of each run, Pallas kernels for 18% -> 18%
where the time goes in v7:
time: 21.9 us; the launch traced here: 21.7 us
  starting transfers between devices  12.3 us (56%)
  Pallas kernels  6.64 us (30%)
  waiting for transfers between devices  2.46 us (11%)
    ppermute x4, starting transfers between devices, body(): other = lax.ppermute(known, 'leaf', [(i, i ^ step) for i in range(nodes)])  8.77 us
    ppermute x1, starting transfers between devices, body(): pair = lax.ppermute(pack, 'leaf', [(i, i ^ 1) for i in range(nodes)])  2.97 us
    ppermute x4, waiting for transfers between devices, body(): other = lax.ppermute(known, 'leaf', [(i, i ^ step) for i in range(nodes)])  2.45 us
    pallas_call x1, Pallas kernels, body(): pl.pallas_call(weights_kernel, out_shape=(pltpu.VMEM((nodes, rank, 2 * ra...  1.88 us
    pallas_call x1, Pallas kernels, fields(): pl.pallas_call(field_kernel, out_shape=(pltpu.VMEM((leaves, columns, poin...  1.81 us
    pallas_call x1, Pallas kernels, body(): pl.pallas_call(up_kernel, out_shape=(pltpu.VMEM((leaves, columns, rank),...  1.63 us
    pallas_call x1, Pallas kernels, body(): pl.pallas_call(down_kernel, out_shape=jax.ShapeDtypeStruct((leaves, colum...  1.03 us
  transfers between devices with their start and end apart: 10, of which 3 were waited for; matrix products, arithmetic and copies ran while one was open for 0% of the time, Pallas kernels for 18%

profile of v7, /device:TPU:0, one launch (start us, length us, event | category | flops | bytes accessed | tf_op | source)
XLA Modules:
  0.0 21.7 jit_solution(5231684124153105154)
XLA Ops:
  0.0 1.6 %up.1 = (bf16[8,16,64]{2,1,0:T(8,128)(2,1)S(1)}, bf16[16,128]{1,0:T(8,128)(2,1)S(1)}, bf16[8,16,256]{2,1,0:T(8,128)(2,1)S(1)}) custom-call(bf16[8,16,256]{2,1,0:T(8,128)(2,1)} %bitcast.16, bf16[8,64,256]{2,1,0:T(8,128)(2,1)} %bitcast.15, bf16[8,64,64]{2,1,0:T(8,128)(2,1)} %leaf_up.1, bf16[1,64,64]{2,1,0:T(8,128)(2,1)} %node_up.1), custom_call_target="tpu_custom_call" | custom-call | flops 2000000000 | bytes 5000000 | tf_op jit(solution)/shard_map/up/pallas_call | solution.py:204
  1.6 3.0 %collective-permute-start = (bf16[1,16,128]{2,1,0:T(8,128)(2,1)S(1)}, bf16[1,16,128]{2,1,0:T(8,128)(2,1)S(1)}, u32[]{:S(2)}, u32[]{:S(2)}) collective-permute-start(bf16[1,16,128]{2,1,0:T(8,128)(2,1)S(1)} %bitcast.8), channel_id=1, source_target_pairs={{0,2},{2,0},{4,6},{6,4},{8,10},{10,8},{12,14},{14,12},{16,18},{18,... | collective-permute-start | bytes 12296 | tf_op jit(solution)/shard_map/ppermute | solution.py:293
  4.6 0.0 copy-start.4
  4.6 0.0 copy-start.5
  4.6 0.0 copy-start.6
  4.6 0.0 copy-start.7
  4.6 0.0 copy-start.8
  4.6 0.0 copy-start.9
  4.6 0.0 copy-start.10
  4.6 0.0 copy-start.11
  4.6 0.0 copy-start.12
  4.7 0.1 pack.1.own
  4.7 0.0 collective-permute-start.2
  4.8 3.0 %collective-permute-start.3 = (bf16[20,16,128]{2,1,0:T(8,128)(2,1)S(1)}, bf16[20,16,128]{2,1,0:T(8,128)(2,1)S(1)}, u32[]{:S(2)}, u32[]{:S(2)}) collective-permute-start(bf16[20,16,128]{2,1,0:T(8,128)(2,1)S(1)} %pack.1.own), channel_id=1, source_target_pairs={{0,2},{2,0},{4,6},{6,4},{8,10},{10,8},{12,14},{14,12},{16,18},{18,... | collective-permute-start | bytes 245768 | tf_op jit(solution)/shard_map/ppermute | solution.py:241
  7.7 0.0 collective-permute-start.4
  7.7 0.0 collective-permute-done
  7.8 1.6 %collective-permute-start.1 = (bf16[2,16,128]{2,1,0:T(8,128)(2,1)S(1)}, bf16[2,16,128]{2,1,0:T(8,128)(2,1)S(1)}, u32[]{:S(2)}, u32[]{:S(2)}) collective-permute-start(bf16[2,16,128]{2,1,0:T(8,128)(2,1)S(1)} %constant_dynamic-update-slice_fusion), channel_id=1, source_target_pairs={{0,4},{2,6},{4,0},{6,2},{8,12},{10,14},{12,8},{14,10},{16,20},{18,... | collective-permute-start | bytes 24584 | tf_op jit(solution)/shard_map/ppermute | solution.py:293
  9.3 0.0 copy-done.4
  9.3 0.0 copy-done.5
  9.3 0.0 copy-done.6
  9.3 0.0 copy-done.7
  9.4 0.0 copy-done.8
  9.4 0.0 copy-done.9
  9.4 0.0 copy-done.10
  9.4 0.0 copy-done.11
  9.4 0.0 copy-done.12
  9.4 0.0 copy-start
  9.4 0.0 copy-start.1
  9.4 0.0 copy-start.2
  9.4 0.0 copy-start.3
  9.5 1.9 %weights.1 = (bf16[16,64,128]{2,1,0:T(8,128)(2,1)S(1)}, bf16[8,64,256]{2,1,0:T(8,128)(2,1)S(1)}) custom-call(s32[1,4]{1,0:T(1,128)S(1)} %copy-done.12, s32[4,14]{1,0:T(4,128)S(1)} %bitcast.14, bf16[1,4,64,64]{3,2,1,0:T(8,128)(2,1)S(1)} %copy-done.9, bf16[1,64,64]{2,1,0:T(8,128)(2,1)S(1)} %copy-done.10, bf16[14,4,64,64]{3,2,1,0:T(8,128)(2,1)S(1)} %copy-done.4, ...), custom_call_target="tpu_custom_call" | custom-call | flops 2000000000 | bytes 3000000 | tf_op jit(solution)/shard_map/weights/pallas_call | solution.py:270
  11.3 0.1 collective-permute-done.1
  11.5 0.0 collective-permute-done.2.cross
  11.5 0.0 collective-permute-done.3.pair
  11.5 0.0 collective-permute-done.4.own_other
  11.5 0.2 collective-permute-start.6
  11.7 0.4 %collective-permute-start.7 = (bf16[20,16,128]{2,1,0:T(8,128)(2,1)S(1)}, bf16[20,16,128]{2,1,0:T(8,128)(2,1)S(1)}, u32[]{:S(2)}, u32[]{:S(2)}) collective-permute-start(bf16[20,16,128]{2,1,0:T(8,128)(2,1)S(1)} %collective-permute-done.2.cross), channel_id=1, source_target_pairs={{0,1},{1,0},{2,3},{3,2},{4,5},{5,4},{6,7},{7,6},{8,9},{9,8},{10,11... | collective-permute-start | bytes 245768 | tf_op jit(solution)/shard_map/ppermute | solution.py:301
  12.1 1.6 %collective-permute-start.5 = (bf16[4,16,128]{2,1,0:T(8,128)(2,1)S(1)}, bf16[4,16,128]{2,1,0:T(8,128)(2,1)S(1)}, u32[]{:S(2)}, u32[]{:S(2)}) collective-permute-start(bf16[4,16,128]{2,1,0:T(8,128)(2,1)S(1)} %constant_dynamic-update-slice_fusion.2), channel_id=1, source_target_pairs={{0,8},{2,10},{4,12},{6,14},{8,0},{10,2},{12,4},{14,6},{16,24},{18,... | collective-permute-start | bytes 49160 | tf_op jit(solution)/shard_map/ppermute | solution.py:293
  13.6 0.0 collective-permute-done.6.pair_other
  13.6 0.0 collective-permute-done.7.cross_other
  13.7 0.0 copy-done
  13.7 0.0 copy-done.1
  13.7 0.0 copy-done.2
  13.7 0.0 copy-done.3
  13.7 1.8 %fields.1 = (f32[8,16,256]{2,1,0:T(8,128)S(1)}, f32[8,16,64]{2,1,0:T(8,128)S(1)}, bf16[20,16,128]{2,1,0:T(8,128)(2,1)S(1)}) custom-call(s32[3,8]{1,0:T(4,128)S(1)} %bitcast.10, s32[3,8]{1,0:T(4,128)S(1)} %bitcast.11, bf16[20,16,128]{2,1,0:T(8,128)(2,1)S(1)} %collective-permute-done.3.pair, bf16[20,16,128]{2,1,0:T(8,128)(2,1)S(1)} %pack.1.own, ...), custom_call_target="tpu_custom_call" | custom-call | flops 805306368 | bytes 3145728 | tf_op jit(solution)/shard_map/fields/pallas_call | solution.py:247
  15.5 0.3 %collective-permute-done.5 = bf16[4,16,128]{2,1,0:T(8,128)(2,1)S(1)} collective-permute-done((bf16[4,16,128]{2,1,0:T(8,128)(2,1)S(1)}, bf16[4,16,128]{2,1,0:T(8,128)(2,1)S(1)}, u32[]{:S(2)}, u32[]{:S(2)}) %collective-permute-start.5) | collective-permute-done | bytes 16416 | tf_op jit(solution)/shard_map/ppermute | solution.py:293
  15.8 0.0 collective-permute-start.9
  15.8 2.7 %collective-permute-start.8 = (bf16[8,16,128]{2,1,0:T(8,128)(2,1)S(1)}, bf16[8,16,128]{2,1,0:T(8,128)(2,1)S(1)}, u32[]{:S(2)}, u32[]{:S(2)}) collective-permute-start(bf16[8,16,128]{2,1,0:T(8,128)(2,1)S(1)} %constant_dynamic-update-slice_fusion.4.known), channel_id=1, source_target_pairs={{0,16},{2,18},{4,20},{6,22},{8,24},{10,26},{12,28},{14,30},{16,0},... | collective-permute-start | bytes 98312 | tf_op jit(solution)/shard_map/ppermute | solution.py:293
  18.5 0.0 collective-permute-done.9.received
  18.5 0.2 base.1
  18.7 2.0 %collective-permute-done.8.other = bf16[8,16,128]{2,1,0:T(8,128)(2,1)S(1)} collective-permute-done((bf16[8,16,128]{2,1,0:T(8,128)(2,1)S(1)}, bf16[8,16,128]{2,1,0:T(8,128)(2,1)S(1)}, u32[]{:S(2)}, u32[]{:S(2)}) %collective-permute-start.8) | collective-permute-done | bytes 32800 | tf_op jit(solution)/shard_map/ppermute | solution.py:293
  20.7 1.0 %down.1 = bf16[8,16,256]{2,1,0:T(8,128)(2,1)} custom-call(bf16[8,16,128]{2,1,0:T(8,128)(2,1)S(1)} %constant_dynamic-update-slice_fusion.4.known, bf16[8,16,128]{2,1,0:T(8,128)(2,1)S(1)} %collective-permute-done.8.other, bf16[16,64,128]{2,1,0:T(8,128)(2,1)S(1)} %get-tuple-element.52.to_field, bf16[8,64,256]{2,1,0:T(8,128)(2,1)S(1)} %get-tuple-element.53.to_points, ...), custom_call_target="tpu_custom_call" | custom-call | tf_op jit(solution)/shard_map/down/pallas_call | solution.py:322
  (6 shorter events, 0.0 us)
Async XLA Ops:
  1.6 6.1 %collective-permute-start = (bf16[1,16,128]{2,1,0:T(8,128)(2,1)S(1)}, bf16[1,16,128]{2,1,0:T(8,128)(2,1)S(1)}, u32[]{:S(2)}, u32[]{:S(2)}) collective-permute-start(bf16[1,16,128]{2,1,0:T(8,128)(2,1)S(1)} %bitcast.8), channel_id=1, source_target_pairs={{0,2},{2,0},{4,6},{6,4},{8,10},{10,8},{12,14},{14,12},{16,18},{18,... | collective-permute-start | bytes 12296 | tf_op jit(solution)/shard_map/ppermute | solution.py:293
  4.6 4.8 %copy-start.4 = (bf16[14,4,64,64]{3,2,1,0:T(8,128)(2,1)S(1)}, bf16[14,4,64,64]{3,2,1,0:T(8,128)(2,1)}, u32[]{:S(2)}) copy-start(bf16[14,4,64,64]{3,2,1,0:T(8,128)(2,1)} %upper_coup.1) | copy-start | bytes 1376260
  4.6 4.8 %copy-start.5 = (bf16[8,256,64]{1,2,0:T(8,128)(2,1)S(1)}, bf16[8,256,64]{1,2,0:T(8,128)(2,1)}, u32[]{:S(2)}) copy-start(bf16[8,256,64]{1,2,0:T(8,128)(2,1)} %param.21) | copy-start | bytes 786436
  4.6 4.8 %copy-start.6 = (bf16[12,64,64]{2,1,0:T(8,128)(2,1)S(1)}, bf16[12,64,64]{2,1,0:T(8,128)(2,1)}, u32[]{:S(2)}) copy-start(bf16[12,64,64]{2,1,0:T(8,128)(2,1)} %upper_up.1) | copy-start | bytes 294916
  4.6 4.8 %copy-start.7 = (bf16[12,64,64]{2,1,0:T(8,128)(2,1)S(1)}, bf16[12,64,64]{2,1,0:T(8,128)(2,1)}, u32[]{:S(2)}) copy-start(bf16[12,64,64]{2,1,0:T(8,128)(2,1)} %upper_down.1) | copy-start | bytes 294916
  4.6 4.8 %copy-start.8 = (bf16[8,64,64]{2,1,0:T(8,128)(2,1)S(1)}, bf16[8,64,64]{2,1,0:T(8,128)(2,1)}, u32[]{:S(2)}) copy-start(bf16[8,64,64]{2,1,0:T(8,128)(2,1)} %leaf_down.1) | copy-start | bytes 196612
  4.6 4.8 %copy-start.9 = (bf16[1,4,64,64]{3,2,1,0:T(8,128)(2,1)S(1)}, bf16[1,4,64,64]{3,2,1,0:T(8,128)(2,1)}, u32[]{:S(2)}) copy-start(bf16[1,4,64,64]{3,2,1,0:T(8,128)(2,1)} %node_coup.1) | copy-start | bytes 98308
  4.6 4.8 %copy-start.10 = (bf16[1,64,64]{2,1,0:T(8,128)(2,1)S(1)}, bf16[1,64,64]{2,1,0:T(8,128)(2,1)}, u32[]{:S(2)}) copy-start(bf16[1,64,64]{2,1,0:T(8,128)(2,1)} %node_down.1) | copy-start | bytes 24580
  4.6 4.8 %copy-start.11 = (s32[14,4]{0,1:T(4,128)S(1)}, s32[14,4]{0,1:T(4,128)}, u32[]{:S(2)}) copy-start(s32[14,4]{0,1:T(4,128)} %param.31) | copy-start | bytes 676
  4.6 4.8 %copy-start.12 = (s32[1,4]{1,0:T(1,128)S(1)}, s32[1,4]{1,0:T(1,128)}, u32[]{:S(2)}) copy-start(s32[1,4]{1,0:T(1,128)} %node_list.1) | copy-start | bytes 52
  4.7 6.7 %collective-permute-start.2 = (bf16[20,16,128]{2,1,0:T(8,128)(2,1)S(1)}, bf16[20,16,128]{2,1,0:T(8,128)(2,1)S(1)}, u32[]{:S(2)}, u32[]{:S(2)}) collective-permute-start(bf16[20,16,128]{2,1,0:T(8,128)(2,1)S(1)} %pack.1.own), channel_id=1, source_target_pairs={{2,4},{3,5},{4,2},{5,3},{6,8},{7,9},{8,6},{9,7},{10,12},{11,13},{1... | collective-permute-start | bytes 245768 | tf_op jit(solution)/shard_map/ppermute | solution.py:240
  4.8 6.7 %collective-permute-start.3 = (bf16[20,16,128]{2,1,0:T(8,128)(2,1)S(1)}, bf16[20,16,128]{2,1,0:T(8,128)(2,1)S(1)}, u32[]{:S(2)}, u32[]{:S(2)}) collective-permute-start(bf16[20,16,128]{2,1,0:T(8,128)(2,1)S(1)} %pack.1.own), channel_id=1, source_target_pairs={{0,2},{2,0},{4,6},{6,4},{8,10},{10,8},{12,14},{14,12},{16,18},{18,... | collective-permute-start | bytes 245768 | tf_op jit(solution)/shard_map/ppermute | solution.py:241
  7.7 3.7 %collective-permute-start.4 = (bf16[20,16,128]{2,1,0:T(8,128)(2,1)S(1)}, bf16[20,16,128]{2,1,0:T(8,128)(2,1)S(1)}, u32[]{:S(2)}, u32[]{:S(2)}) collective-permute-start(bf16[20,16,128]{2,1,0:T(8,128)(2,1)S(1)} %pack.1.own), channel_id=1, source_target_pairs={{0,1},{1,0},{2,3},{3,2},{4,5},{5,4},{6,7},{7,6},{8,9},{9,8},{10,11... | collective-permute-start | bytes 245768 | tf_op jit(solution)/shard_map/ppermute | solution.py:242
  7.8 3.7 %collective-permute-start.1 = (bf16[2,16,128]{2,1,0:T(8,128)(2,1)S(1)}, bf16[2,16,128]{2,1,0:T(8,128)(2,1)S(1)}, u32[]{:S(2)}, u32[]{:S(2)}) collective-permute-start(bf16[2,16,128]{2,1,0:T(8,128)(2,1)S(1)} %constant_dynamic-update-slice_fusion), channel_id=1, source_target_pairs={{0,4},{2,6},{4,0},{6,2},{8,12},{10,14},{12,8},{14,10},{16,20},{18,... | collective-permute-start | bytes 24584 | tf_op jit(solution)/shard_map/ppermute | solution.py:293
  9.4 4.3 %copy-start = (bf16[8,3,256,256]{3,2,1,0:T(8,128)(2,1)S(1)}, bf16[8,3,256,256]{3,2,1,0:T(8,128)(2,1)}, u32[]{:S(2)}) copy-start(bf16[8,3,256,256]{3,2,1,0:T(8,128)(2,1)} %near.1) | copy-start | bytes 9437188
  9.4 4.2 %copy-start.1 = (bf16[8,3,64,64]{3,2,1,0:T(8,128)(2,1)S(1)}, bf16[8,3,64,64]{3,2,1,0:T(8,128)(2,1)}, u32[]{:S(2)}) copy-start(bf16[8,3,64,64]{3,2,1,0:T(8,128)(2,1)} %coup.1) | copy-start | bytes 589828
  9.4 4.2 %copy-start.2 = (s32[8,3]{0,1:T(4,128)S(1)}, s32[8,3]{0,1:T(4,128)}, u32[]{:S(2)}) copy-start(s32[8,3]{0,1:T(4,128)} %param.19) | copy-start | bytes 292
  9.4 4.2 %copy-start.3 = (s32[8,3]{0,1:T(4,128)S(1)}, s32[8,3]{0,1:T(4,128)}, u32[]{:S(2)}) copy-start(s32[8,3]{0,1:T(4,128)} %param.23) | copy-start | bytes 292
  11.5 2.2 %collective-permute-start.6 = (bf16[20,16,128]{2,1,0:T(8,128)(2,1)S(1)}, bf16[20,16,128]{2,1,0:T(8,128)(2,1)S(1)}, u32[]{:S(2)}, u32[]{:S(2)}) collective-permute-start(bf16[20,16,128]{2,1,0:T(8,128)(2,1)S(1)} %collective-permute-done.3.pair), channel_id=1, source_target_pairs={{0,1},{1,0},{2,3},{3,2},{4,5},{5,4},{6,7},{7,6},{8,9},{9,8},{10,11... | collective-permute-start | bytes 245768 | tf_op jit(solution)/shard_map/ppermute | solution.py:300
  11.7 2.0 %collective-permute-start.7 = (bf16[20,16,128]{2,1,0:T(8,128)(2,1)S(1)}, bf16[20,16,128]{2,1,0:T(8,128)(2,1)S(1)}, u32[]{:S(2)}, u32[]{:S(2)}) collective-permute-start(bf16[20,16,128]{2,1,0:T(8,128)(2,1)S(1)} %collective-permute-done.2.cross), channel_id=1, source_target_pairs={{0,1},{1,0},{2,3},{3,2},{4,5},{5,4},{6,7},{7,6},{8,9},{9,8},{10,11... | collective-permute-start | bytes 245768 | tf_op jit(solution)/shard_map/ppermute | solution.py:301
  12.1 3.7 %collective-permute-start.5 = (bf16[4,16,128]{2,1,0:T(8,128)(2,1)S(1)}, bf16[4,16,128]{2,1,0:T(8,128)(2,1)S(1)}, u32[]{:S(2)}, u32[]{:S(2)}) collective-permute-start(bf16[4,16,128]{2,1,0:T(8,128)(2,1)S(1)} %constant_dynamic-update-slice_fusion.2), channel_id=1, source_target_pairs={{0,8},{2,10},{4,12},{6,14},{8,0},{10,2},{12,4},{14,6},{16,24},{18,... | collective-permute-start | bytes 49160 | tf_op jit(solution)/shard_map/ppermute | solution.py:293
  15.8 2.7 %collective-permute-start.9 = (bf16[20,16,128]{2,1,0:T(8,128)(2,1)S(1)}, bf16[20,16,128]{2,1,0:T(8,128)(2,1)S(1)}, u32[]{:S(2)}, u32[]{:S(2)}) collective-permute-start(bf16[20,16,128]{2,1,0:T(8,128)(2,1)S(1)} %get-tuple-element.50), channel_id=1, source_target_pairs={{0,1},{1,0},{2,3},{3,2},{4,5},{5,4},{6,7},{7,6},{8,9},{9,8},{10,11... | collective-permute-start | bytes 245768 | tf_op jit(solution)/shard_map/ppermute | solution.py:309
  15.8 4.9 %collective-permute-start.8 = (bf16[8,16,128]{2,1,0:T(8,128)(2,1)S(1)}, bf16[8,16,128]{2,1,0:T(8,128)(2,1)S(1)}, u32[]{:S(2)}, u32[]{:S(2)}) collective-permute-start(bf16[8,16,128]{2,1,0:T(8,128)(2,1)S(1)} %constant_dynamic-update-slice_fusion.4.known), channel_id=1, source_target_pairs={{0,16},{2,18},{4,20},{6,22},{8,24},{10,26},{12,28},{14,30},{16,0},... | collective-permute-start | bytes 98312 | tf_op jit(solution)/shard_map/ppermute | solution.py:293

commit v8 on v7

--- a/solution.py
+++ b/solution.py
@@ -32,16 +32,14 @@
 def up_kernel(dens, col, leaf_up, node_up, coeff_out, message, dens_out):
     leaves = dens.shape[0]
     dens_out[...] = dens[...]
-    rank = col.shape[1]
-    node = None
+    coeffs = [mm(dens[t], col[t], LAST).astype(jnp.bfloat16) for t in range(leaves)]
+    total = None
     for t in range(leaves):
-        coeff = mm(dens[t], col[t], LAST).astype(jnp.bfloat16)
-        coeff_out[t] = coeff
-        term = mm(coeff, leaf_up[t], PLAIN)
-        node = term if node is None else node + term
-    node = node.astype(jnp.bfloat16)
-    message[:, :rank] = node
-    message[:, rank:] = mm(node, node_up[0], PLAIN).astype(jnp.bfloat16)
+        coeff_out[t] = coeffs[t]
+        lift = mm(leaf_up[t], node_up[0], PLAIN).astype(jnp.bfloat16)
+        term = mm(coeffs[t], jnp.concatenate([leaf_up[t], lift], axis=1), PLAIN)
+        total = term if total is None else total + term
+    message[...] = total.astype(jnp.bfloat16)
 
 
 def pack_rows(pack, t, leaves, long, short):
@@ -82,7 +80,7 @@
 
 
 def field_kernel(
-    near_list, far_list, pair, own, cross, pair_other, own_other, cross_other, coup, near,
+    near_list, far_list, pair, own, cross, own_other, both_other, coup, near,
     near_out, far_out, send, ext, ext_coeff,
 ):
     leaves, entries = near.shape[0], near.shape[1]
@@ -91,6 +89,8 @@
     halves = near.shape[-1] // 128
     me = lax.axis_index("leaf")
     odd = me & 1
+    tiles = own.shape[0]
+    pair_other, cross_other = both_other.at[:tiles], both_other.at[tiles:]
     for slot, pair_of_cores in (
         (2 - 2 * odd, (pair, pair_other)),
         (1, (own, own_other)),
@@ -119,15 +119,13 @@
 
 
 def weights_kernel(
-    node_list, upper_list, node_coup, node_down, upper_coup, upper_up, upper_down, leaf_down, row,
-    to_field, to_points, named, *tree,
+    node_list, upper_list, node_coup, node_down, upper_coup, upper_up, upper_down,
+    to_field, named, *tree,
 ):
     nodes, rank = to_field.shape[0], to_field.shape[1]
     farc = node_coup.shape[1]
     levels = nodes.bit_length() - 1
     me = lax.axis_index("leaf")
-    for t in range(leaf_down.shape[0]):
-        to_points[t] = mm(leaf_down[t], row[t], (((0,), (0,)), ((), ()))).astype(jnp.bfloat16)
     named[...] = jnp.zeros_like(named)
     for j in range(farc):
         place = node_list[0, j] ^ me
@@ -155,13 +153,14 @@
         to_field[place, :, :rank] = named[place].astype(jnp.bfloat16)
 
 
-def base_kernel(near, far, received, row, base):
+def base_kernel(near, far, received, row, leaf_down, base, to_points):
     leaves, rank = row.shape[0], row.shape[1]
     halves = near.shape[2] // 128
     for t in range(leaves):
         local = far[t] + unpack_short(received, t, leaves, halves, rank).astype(jnp.float32)
         close = near[t] + unpack_long(received, t, halves).astype(jnp.float32)
         base[t] = close + mm(local.astype(jnp.bfloat16), row[t], PLAIN)
+        to_points[t] = mm(leaf_down[t], row[t], (((0,), (0,)), ((), ()))).astype(jnp.bfloat16)
 
 
 def down_kernel(known, other, to_field, to_points, base, out):
@@ -251,7 +250,7 @@
                 pltpu.VMEM((leaves, columns, rank), f32),
                 pltpu.VMEM((tiles, columns, 128), bf16),
             ),
-            in_specs=[smem()] * 2 + [vmem()] * 8,
+            in_specs=[smem()] * 2 + [vmem()] * 7,
             out_specs=(vmem(),) * 3,
             scratch_shapes=[
                 pltpu.VMEM((3 * leaves, 2 * columns, points), bf16),
@@ -267,14 +266,11 @@
         )(staged[0], staged[1], *packs, staged[2], staged[3])
 
     row = jnp.swapaxes(row_basis, 1, 2)
-    weights = pl.pallas_call(
+    to_field = pl.pallas_call(
         weights_kernel,
-        out_shape=(
-            pltpu.VMEM((nodes, rank, 2 * rank), bf16),
-            pltpu.VMEM((leaves, rank, points), bf16),
-        ),
-        in_specs=[smem()] * 2 + [vmem()] * 7,
-        out_specs=(vmem(),) * 2,
+        out_shape=pltpu.VMEM((nodes, rank, 2 * rank), bf16),
+        in_specs=[smem()] * 2 + [vmem()] * 5,
+        out_specs=vmem(),
         scratch_shapes=[pltpu.VMEM((nodes, rank, rank), f32)]
         + [pltpu.VMEM((2**height, rank, rank), f32) for height in range(1, levels)],
         compiler_params=limit(16),
@@ -284,7 +280,6 @@
         name="weights",
     )(
         node_list, upper_list.T, node_coupling, node_down, upper_coupling, upper_up, upper_down,
-        leaf_down, row,
     )
 
     known = message[None]
@@ -294,30 +289,32 @@
         if bit == 0:
             known, other, pack = lax.optimization_barrier((known, other, pack))
         if bit == 1:
-            known, other, cross, pair, own_other, weights = lax.optimization_barrier(
-                (known, other, cross, pair, own_other, weights)
+            known, other, cross, pair, own_other, to_field = lax.optimization_barrier(
+                (known, other, cross, pair, own_other, to_field)
             )
-            pair_other = lax.ppermute(pair, "sub", swap)
-            cross_other = lax.ppermute(cross, "sub", swap)
+            both_other = lax.ppermute(jnp.concatenate([pair, cross], axis=0), "sub", swap)
         if bit == levels - 2:
-            near, far, send = fields(pair, pack, cross, pair_other, own_other, cross_other)
+            near, far, send = fields(pair, pack, cross, own_other, both_other)
             known, other, near, far, send = lax.optimization_barrier(
                 (known, other, near, far, send)
             )
         if bit < levels - 1:
             known = jnp.concatenate([known, other], axis=0)
     received = lax.ppermute(send, "sub", swap)
-    base = pl.pallas_call(
+    base, to_points = pl.pallas_call(
         base_kernel,
-        out_shape=pltpu.VMEM((leaves, columns, points), f32),
-        in_specs=[vmem()] * 4,
-        out_specs=vmem(),
+        out_shape=(
+            pltpu.VMEM((leaves, columns, points), f32),
+            pltpu.VMEM((leaves, rank, points), bf16),
+        ),
+        in_specs=[vmem()] * 5,
+        out_specs=(vmem(),) * 2,
         compiler_params=limit(4),
         cost_estimate=pl.CostEstimate(
             flops=1_000_000_000, bytes_accessed=1_000_000, transcendentals=0
         ),
         name="base",
-    )(near, far, received, row)
+    )(near, far, received, row, leaf_down)
     other, base = lax.optimization_barrier((other, base))
     out = pl.pallas_call(
         down_kernel,
@@ -326,7 +323,7 @@
         out_specs=vmem(),
         compiler_params=limit(8),
         name="down",
-    )(known, other, *weights, base)
+    )(known, other, to_field, to_points, base)
     return jnp.swapaxes(out, 1, 2)
 
 

time: 21.9 us -> 21.3 us (0.973)
  starting transfers between devices: 12.3 us -> 11.9 us
    ppermute x2 -> x1, starting transfers between devices: 0.58 us -> 0.14 us  [body(): lax.ppermute(jnp.concatenate([pair, cross], axis=0), 'sub', swap)]
  transfers between devices with their start and end apart: 10 -> 9, of which waited for: 3 -> 3; matrix products, arithmetic and copies ran while one was open for 0% -> 0% of each run, Pallas kernels for 18% -> 19%
where the time goes in v8:
time: 21.3 us; the launch traced here: 21.1 us
  starting transfers between devices  11.9 us (56%)
  Pallas kernels  6.5 us (31%)
  waiting for transfers between devices  2.42 us (11%)
    ppermute x4, starting transfers between devices, body(): other = lax.ppermute(known, 'leaf', [(i, i ^ step) for i in range(nodes)])  8.78 us
    ppermute x1, starting transfers between devices, body(): pair = lax.ppermute(pack, 'leaf', [(i, i ^ 1) for i in range(nodes)])  2.97 us
    ppermute x4, waiting for transfers between devices, body(): other = lax.ppermute(known, 'leaf', [(i, i ^ step) for i in range(nodes)])  2.41 us
    pallas_call x1, Pallas kernels, body(): pl.pallas_call(weights_kernel, out_shape=pltpu.VMEM((nodes, rank, 2 * ran...  1.83 us
    pallas_call x1, Pallas kernels, fields(): pl.pallas_call(field_kernel, out_shape=(pltpu.VMEM((leaves, columns, poin...  1.81 us
    pallas_call x1, Pallas kernels, body(): pl.pallas_call(up_kernel, out_shape=(pltpu.VMEM((leaves, columns, rank),...  1.45 us
    pallas_call x1, Pallas kernels, body(): pl.pallas_call(down_kernel, out_shape=jax.ShapeDtypeStruct((leaves, colum...  1.03 us
  transfers between devices with their start and end apart: 9, of which 3 were waited for; matrix products, arithmetic and copies ran while one was open for 0% of the time, Pallas kernels for 19%

profile of v8, /device:TPU:0, one launch (start us, length us, event | category | flops | bytes accessed | tf_op | source)
XLA Modules:
  0.0 21.1 jit_solution(18190675398936959550)
XLA Ops:
  0.0 1.5 %up.1 = (bf16[8,16,64]{2,1,0:T(8,128)(2,1)S(1)}, bf16[16,128]{1,0:T(8,128)(2,1)S(1)}, bf16[8,16,256]{2,1,0:T(8,128)(2,1)S(1)}) custom-call(bf16[8,16,256]{2,1,0:T(8,128)(2,1)} %bitcast.15, bf16[8,64,256]{2,1,0:T(8,128)(2,1)} %bitcast.14, bf16[8,64,64]{2,1,0:T(8,128)(2,1)} %leaf_up.1, bf16[1,64,64]{2,1,0:T(8,128)(2,1)} %node_up.1), custom_call_target="tpu_custom_call" | custom-call | flops 2000000000 | bytes 5000000 | tf_op jit(solution)/shard_map/up/pallas_call | solution.py:203
  1.5 2.9 %collective-permute-start = (bf16[1,16,128]{2,1,0:T(8,128)(2,1)S(1)}, bf16[1,16,128]{2,1,0:T(8,128)(2,1)S(1)}, u32[]{:S(2)}, u32[]{:S(2)}) collective-permute-start(bf16[1,16,128]{2,1,0:T(8,128)(2,1)S(1)} %bitcast.8), channel_id=1, source_target_pairs={{0,2},{2,0},{4,6},{6,4},{8,10},{10,8},{12,14},{14,12},{16,18},{18,... | collective-permute-start | bytes 12296 | tf_op jit(solution)/shard_map/ppermute | solution.py:288
  4.4 0.0 copy-start.4
  4.4 0.0 copy-start.6
  4.4 0.0 copy-start.7
  4.4 0.0 copy-start.9
  4.4 0.0 copy-start.10
  4.4 0.0 copy-start.11
  4.4 0.0 copy-start.12
  4.4 0.1 pack.1.own
  4.5 0.0 collective-permute-start.2
  4.6 3.0 %collective-permute-start.3 = (bf16[20,16,128]{2,1,0:T(8,128)(2,1)S(1)}, bf16[20,16,128]{2,1,0:T(8,128)(2,1)S(1)}, u32[]{:S(2)}, u32[]{:S(2)}) collective-permute-start(bf16[20,16,128]{2,1,0:T(8,128)(2,1)S(1)} %pack.1.own), channel_id=1, source_target_pairs={{0,2},{2,0},{4,6},{6,4},{8,10},{10,8},{12,14},{14,12},{16,18},{18,... | collective-permute-start | bytes 245768 | tf_op jit(solution)/shard_map/ppermute | solution.py:240
  7.5 0.0 collective-permute-start.4
  7.5 0.0 collective-permute-done
  7.5 1.6 %collective-permute-start.1 = (bf16[2,16,128]{2,1,0:T(8,128)(2,1)S(1)}, bf16[2,16,128]{2,1,0:T(8,128)(2,1)S(1)}, u32[]{:S(2)}, u32[]{:S(2)}) collective-permute-start(bf16[2,16,128]{2,1,0:T(8,128)(2,1)S(1)} %constant_dynamic-update-slice_fusion), channel_id=1, source_target_pairs={{0,4},{2,6},{4,0},{6,2},{8,12},{10,14},{12,8},{14,10},{16,20},{18,... | collective-permute-start | bytes 24584 | tf_op jit(solution)/shard_map/ppermute | solution.py:288
  9.1 0.0 copy-done.4
  9.1 0.0 copy-done.6
  9.1 0.0 copy-done.7
  9.1 0.0 copy-done.9
  9.1 0.0 copy-done.10
  9.2 0.0 copy-done.11
  9.2 0.0 copy-done.12
  9.2 0.0 copy-start
  9.2 0.0 copy-start.1
  9.2 0.0 copy-start.2
  9.2 0.0 copy-start.3
  9.2 1.8 %weights.1.to_field = bf16[16,64,128]{2,1,0:T(8,128)(2,1)S(1)} custom-call(s32[1,4]{1,0:T(1,128)S(1)} %copy-done.12, s32[4,14]{1,0:T(4,128)S(1)} %bitcast.13, bf16[1,4,64,64]{3,2,1,0:T(8,128)(2,1)S(1)} %copy-done.9, bf16[1,64,64]{2,1,0:T(8,128)(2,1)S(1)} %copy-done.10, bf16[14,4,64,64]{3,2,1,0:T(8,128)(2,1)S(1)} %copy-done.4, ...), custom_call_target="tpu_custom_call" | custom-call | flops 2000000000 | bytes 3000000 | tf_op jit(solution)/shard_map/weights/pallas_call | solution.py:269
  11.1 0.0 copy-start.5
  11.1 0.0 copy-start.8
  11.1 0.2 collective-permute-done.1
  11.3 0.0 collective-permute-done.2.cross
  11.3 0.0 collective-permute-done.3.pair
  11.3 0.0 collective-permute-done.4.own_other
  11.3 0.1 collective-permute-start.6
  11.4 1.6 %collective-permute-start.5 = (bf16[4,16,128]{2,1,0:T(8,128)(2,1)S(1)}, bf16[4,16,128]{2,1,0:T(8,128)(2,1)S(1)}, u32[]{:S(2)}, u32[]{:S(2)}) collective-permute-start(bf16[4,16,128]{2,1,0:T(8,128)(2,1)S(1)} %constant_dynamic-update-slice_fusion.2), channel_id=1, source_target_pairs={{0,8},{2,10},{4,12},{6,14},{8,0},{10,2},{12,4},{14,6},{16,24},{18,... | collective-permute-start | bytes 49160 | tf_op jit(solution)/shard_map/ppermute | solution.py:288
  13.0 0.0 collective-permute-done.6.both_other
  13.0 0.0 copy-done
  13.1 0.0 copy-done.1
  13.1 0.0 copy-done.2
  13.1 0.0 copy-done.3
  13.1 1.8 %fields.1 = (f32[8,16,256]{2,1,0:T(8,128)S(1)}, f32[8,16,64]{2,1,0:T(8,128)S(1)}, bf16[20,16,128]{2,1,0:T(8,128)(2,1)S(1)}) custom-call(s32[3,8]{1,0:T(4,128)S(1)} %bitcast.10, s32[3,8]{1,0:T(4,128)S(1)} %bitcast.11, bf16[20,16,128]{2,1,0:T(8,128)(2,1)S(1)} %collective-permute-done.3.pair, bf16[20,16,128]{2,1,0:T(8,128)(2,1)S(1)} %pack.1.own, ...), custom_call_target="tpu_custom_call" | custom-call | flops 805306368 | bytes 3145728 | tf_op jit(solution)/shard_map/fields/pallas_call | solution.py:246
  14.9 0.3 %collective-permute-done.5 = bf16[4,16,128]{2,1,0:T(8,128)(2,1)S(1)} collective-permute-done((bf16[4,16,128]{2,1,0:T(8,128)(2,1)S(1)}, bf16[4,16,128]{2,1,0:T(8,128)(2,1)S(1)}, u32[]{:S(2)}, u32[]{:S(2)}) %collective-permute-start.5) | collective-permute-done | bytes 16416 | tf_op jit(solution)/shard_map/ppermute | solution.py:288
  15.2 0.0 collective-permute-start.8
  15.2 2.7 %collective-permute-start.7 = (bf16[8,16,128]{2,1,0:T(8,128)(2,1)S(1)}, bf16[8,16,128]{2,1,0:T(8,128)(2,1)S(1)}, u32[]{:S(2)}, u32[]{:S(2)}) collective-permute-start(bf16[8,16,128]{2,1,0:T(8,128)(2,1)S(1)} %constant_dynamic-update-slice_fusion.4.known), channel_id=1, source_target_pairs={{0,16},{2,18},{4,20},{6,22},{8,24},{10,26},{12,28},{14,30},{16,0},... | collective-permute-start | bytes 98312 | tf_op jit(solution)/shard_map/ppermute | solution.py:288
  17.9 0.0 collective-permute-done.8.received
  17.9 0.0 copy-done.5
  17.9 0.0 copy-done.8
  17.9 0.3 %base.1 = (f32[8,16,256]{2,1,0:T(8,128)S(1)}, bf16[8,64,256]{2,1,0:T(8,128)(2,1)S(1)}) custom-call(f32[8,16,256]{2,1,0:T(8,128)S(1)} %get-tuple-element.45.near, f32[8,16,64]{2,1,0:T(8,128)S(1)} %get-tuple-element.46.far, bf16[20,16,128]{2,1,0:T(8,128)(2,1)S(1)} %collective-permute-done.8.received, bf16[8,64,256]{2,1,0:T(8,128)(2,1)S(1)} %bitcast.12, ...), custom_call_target="tpu_custom_call" | custom-call | flops 1000000000 | bytes 1000000 | tf_op jit(solution)/shard_map/base/pallas_call | solution.py:304
  18.2 1.9 %collective-permute-done.7.other = bf16[8,16,128]{2,1,0:T(8,128)(2,1)S(1)} collective-permute-done((bf16[8,16,128]{2,1,0:T(8,128)(2,1)S(1)}, bf16[8,16,128]{2,1,0:T(8,128)(2,1)S(1)}, u32[]{:S(2)}, u32[]{:S(2)}) %collective-permute-start.7) | collective-permute-done | bytes 32800 | tf_op jit(solution)/shard_map/ppermute | solution.py:288
  20.1 1.0 %down.1 = bf16[8,16,256]{2,1,0:T(8,128)(2,1)} custom-call(bf16[8,16,128]{2,1,0:T(8,128)(2,1)S(1)} %constant_dynamic-update-slice_fusion.4.known, bf16[8,16,128]{2,1,0:T(8,128)(2,1)S(1)} %collective-permute-done.7.other, bf16[16,64,128]{2,1,0:T(8,128)(2,1)S(1)} %weights.1.to_field, bf16[8,64,256]{2,1,0:T(8,128)(2,1)S(1)} %get-tuple-element.51.to_points, ...), custom_call_target="tpu_custom_call" | custom-call | tf_op jit(solution)/shard_map/down/pallas_call | solution.py:319
  (7 shorter events, 0.0 us)
Async XLA Ops:
  1.5 6.1 %collective-permute-start = (bf16[1,16,128]{2,1,0:T(8,128)(2,1)S(1)}, bf16[1,16,128]{2,1,0:T(8,128)(2,1)S(1)}, u32[]{:S(2)}, u32[]{:S(2)}) collective-permute-start(bf16[1,16,128]{2,1,0:T(8,128)(2,1)S(1)} %bitcast.8), channel_id=1, source_target_pairs={{0,2},{2,0},{4,6},{6,4},{8,10},{10,8},{12,14},{14,12},{16,18},{18,... | collective-permute-start | bytes 12296 | tf_op jit(solution)/shard_map/ppermute | solution.py:288
  4.4 4.7 %copy-start.4 = (bf16[14,4,64,64]{3,2,1,0:T(8,128)(2,1)S(1)}, bf16[14,4,64,64]{3,2,1,0:T(8,128)(2,1)}, u32[]{:S(2)}) copy-start(bf16[14,4,64,64]{3,2,1,0:T(8,128)(2,1)} %upper_coup.1) | copy-start | bytes 1376260
  4.4 4.7 %copy-start.6 = (bf16[12,64,64]{2,1,0:T(8,128)(2,1)S(1)}, bf16[12,64,64]{2,1,0:T(8,128)(2,1)}, u32[]{:S(2)}) copy-start(bf16[12,64,64]{2,1,0:T(8,128)(2,1)} %upper_up.1) | copy-start | bytes 294916
  4.4 4.7 %copy-start.7 = (bf16[12,64,64]{2,1,0:T(8,128)(2,1)S(1)}, bf16[12,64,64]{2,1,0:T(8,128)(2,1)}, u32[]{:S(2)}) copy-start(bf16[12,64,64]{2,1,0:T(8,128)(2,1)} %upper_down.1) | copy-start | bytes 294916
  4.4 4.7 %copy-start.9 = (bf16[1,4,64,64]{3,2,1,0:T(8,128)(2,1)S(1)}, bf16[1,4,64,64]{3,2,1,0:T(8,128)(2,1)}, u32[]{:S(2)}) copy-start(bf16[1,4,64,64]{3,2,1,0:T(8,128)(2,1)} %node_coup.1) | copy-start | bytes 98308
  4.4 4.7 %copy-start.10 = (bf16[1,64,64]{2,1,0:T(8,128)(2,1)S(1)}, bf16[1,64,64]{2,1,0:T(8,128)(2,1)}, u32[]{:S(2)}) copy-start(bf16[1,64,64]{2,1,0:T(8,128)(2,1)} %node_down.1) | copy-start | bytes 24580
  4.4 4.7 %copy-start.11 = (s32[14,4]{0,1:T(4,128)S(1)}, s32[14,4]{0,1:T(4,128)}, u32[]{:S(2)}) copy-start(s32[14,4]{0,1:T(4,128)} %param.31) | copy-start | bytes 676
  4.4 4.7 %copy-start.12 = (s32[1,4]{1,0:T(1,128)S(1)}, s32[1,4]{1,0:T(1,128)}, u32[]{:S(2)}) copy-start(s32[1,4]{1,0:T(1,128)} %node_list.1) | copy-start | bytes 52
  4.5 6.7 %collective-permute-start.2 = (bf16[20,16,128]{2,1,0:T(8,128)(2,1)S(1)}, bf16[20,16,128]{2,1,0:T(8,128)(2,1)S(1)}, u32[]{:S(2)}, u32[]{:S(2)}) collective-permute-start(bf16[20,16,128]{2,1,0:T(8,128)(2,1)S(1)} %pack.1.own), channel_id=1, source_target_pairs={{2,4},{3,5},{4,2},{5,3},{6,8},{7,9},{8,6},{9,7},{10,12},{11,13},{1... | collective-permute-start | bytes 245768 | tf_op jit(solution)/shard_map/ppermute | solution.py:239
  4.6 6.7 %collective-permute-start.3 = (bf16[20,16,128]{2,1,0:T(8,128)(2,1)S(1)}, bf16[20,16,128]{2,1,0:T(8,128)(2,1)S(1)}, u32[]{:S(2)}, u32[]{:S(2)}) collective-permute-start(bf16[20,16,128]{2,1,0:T(8,128)(2,1)S(1)} %pack.1.own), channel_id=1, source_target_pairs={{0,2},{2,0},{4,6},{6,4},{8,10},{10,8},{12,14},{14,12},{16,18},{18,... | collective-permute-start | bytes 245768 | tf_op jit(solution)/shard_map/ppermute | solution.py:240
  7.5 3.7 %collective-permute-start.4 = (bf16[20,16,128]{2,1,0:T(8,128)(2,1)S(1)}, bf16[20,16,128]{2,1,0:T(8,128)(2,1)S(1)}, u32[]{:S(2)}, u32[]{:S(2)}) collective-permute-start(bf16[20,16,128]{2,1,0:T(8,128)(2,1)S(1)} %pack.1.own), channel_id=1, source_target_pairs={{0,1},{1,0},{2,3},{3,2},{4,5},{5,4},{6,7},{7,6},{8,9},{9,8},{10,11... | collective-permute-start | bytes 245768 | tf_op jit(solution)/shard_map/ppermute | solution.py:241
  7.5 3.7 %collective-permute-start.1 = (bf16[2,16,128]{2,1,0:T(8,128)(2,1)S(1)}, bf16[2,16,128]{2,1,0:T(8,128)(2,1)S(1)}, u32[]{:S(2)}, u32[]{:S(2)}) collective-permute-start(bf16[2,16,128]{2,1,0:T(8,128)(2,1)S(1)} %constant_dynamic-update-slice_fusion), channel_id=1, source_target_pairs={{0,4},{2,6},{4,0},{6,2},{8,12},{10,14},{12,8},{14,10},{16,20},{18,... | collective-permute-start | bytes 24584 | tf_op jit(solution)/shard_map/ppermute | solution.py:288
  9.2 3.9 %copy-start = (bf16[8,3,256,256]{3,2,1,0:T(8,128)(2,1)S(1)}, bf16[8,3,256,256]{3,2,1,0:T(8,128)(2,1)}, u32[]{:S(2)}) copy-start(bf16[8,3,256,256]{3,2,1,0:T(8,128)(2,1)} %near.1) | copy-start | bytes 9437188
  9.2 3.9 %copy-start.1 = (bf16[8,3,64,64]{3,2,1,0:T(8,128)(2,1)S(1)}, bf16[8,3,64,64]{3,2,1,0:T(8,128)(2,1)}, u32[]{:S(2)}) copy-start(bf16[8,3,64,64]{3,2,1,0:T(8,128)(2,1)} %coup.1) | copy-start | bytes 589828
  9.2 3.9 %copy-start.2 = (s32[8,3]{0,1:T(4,128)S(1)}, s32[8,3]{0,1:T(4,128)}, u32[]{:S(2)}) copy-start(s32[8,3]{0,1:T(4,128)} %param.19) | copy-start | bytes 292
  9.2 3.9 %copy-start.3 = (s32[8,3]{0,1:T(4,128)S(1)}, s32[8,3]{0,1:T(4,128)}, u32[]{:S(2)}) copy-start(s32[8,3]{0,1:T(4,128)} %param.23) | copy-start | bytes 292
  11.1 6.8 %copy-start.5 = (bf16[8,256,64]{1,2,0:T(8,128)(2,1)S(1)}, bf16[8,256,64]{1,2,0:T(8,128)(2,1)}, u32[]{:S(2)}) copy-start(bf16[8,256,64]{1,2,0:T(8,128)(2,1)} %param.21) | copy-start | bytes 786436
  11.1 6.8 %copy-start.8 = (bf16[8,64,64]{2,1,0:T(8,128)(2,1)S(1)}, bf16[8,64,64]{2,1,0:T(8,128)(2,1)}, u32[]{:S(2)}) copy-start(bf16[8,64,64]{2,1,0:T(8,128)(2,1)} %leaf_down.1) | copy-start | bytes 196612
  11.3 1.7 %collective-permute-start.6 = (bf16[40,16,128]{2,1,0:T(8,128)(2,1)S(1)}, bf16[40,16,128]{2,1,0:T(8,128)(2,1)S(1)}, u32[]{:S(2)}, u32[]{:S(2)}) collective-permute-start(bf16[40,16,128]{2,1,0:T(8,128)(2,1)S(1)} %pad_maximum_fusion), channel_id=1, source_target_pairs={{0,1},{1,0},{2,3},{3,2},{4,5},{5,4},{6,7},{7,6},{8,9},{9,8},{10,11... | collective-permute-start | bytes 491528 | tf_op jit(solution)/shard_map/ppermute | solution.py:295
  11.4 3.8 %collective-permute-start.5 = (bf16[4,16,128]{2,1,0:T(8,128)(2,1)S(1)}, bf16[4,16,128]{2,1,0:T(8,128)(2,1)S(1)}, u32[]{:S(2)}, u32[]{:S(2)}) collective-permute-start(bf16[4,16,128]{2,1,0:T(8,128)(2,1)S(1)} %constant_dynamic-update-slice_fusion.2), channel_id=1, source_target_pairs={{0,8},{2,10},{4,12},{6,14},{8,0},{10,2},{12,4},{14,6},{16,24},{18,... | collective-permute-start | bytes 49160 | tf_op jit(solution)/shard_map/ppermute | solution.py:288
  15.2 2.7 %collective-permute-start.8 = (bf16[20,16,128]{2,1,0:T(8,128)(2,1)S(1)}, bf16[20,16,128]{2,1,0:T(8,128)(2,1)S(1)}, u32[]{:S(2)}, u32[]{:S(2)}) collective-permute-start(bf16[20,16,128]{2,1,0:T(8,128)(2,1)S(1)} %get-tuple-element.47), channel_id=1, source_target_pairs={{0,1},{1,0},{2,3},{3,2},{4,5},{5,4},{6,7},{7,6},{8,9},{9,8},{10,11... | collective-permute-start | bytes 245768 | tf_op jit(solution)/shard_map/ppermute | solution.py:303
  15.2 4.9 %collective-permute-start.7 = (bf16[8,16,128]{2,1,0:T(8,128)(2,1)S(1)}, bf16[8,16,128]{2,1,0:T(8,128)(2,1)S(1)}, u32[]{:S(2)}, u32[]{:S(2)}) collective-permute-start(bf16[8,16,128]{2,1,0:T(8,128)(2,1)S(1)} %constant_dynamic-update-slice_fusion.4.known), channel_id=1, source_target_pairs={{0,16},{2,18},{4,20},{6,22},{8,24},{10,26},{12,28},{14,30},{16,0},... | collective-permute-start | bytes 98312 | tf_op jit(solution)/shard_map/ppermute | solution.py:288

commit v9 on v7

--- a/solution.py
+++ b/solution.py
@@ -30,18 +30,25 @@
 
 
 def up_kernel(dens, col, leaf_up, node_up, coeff_out, message, dens_out):
-    leaves = dens.shape[0]
+    leaves, columns, _ = dens.shape
+    rank = col.shape[1]
     dens_out[...] = dens[...]
-    rank = col.shape[1]
-    node = None
-    for t in range(leaves):
-        coeff = mm(dens[t], col[t], LAST).astype(jnp.bfloat16)
-        coeff_out[t] = coeff
-        term = mm(coeff, leaf_up[t], PLAIN)
-        node = term if node is None else node + term
-    node = node.astype(jnp.bfloat16)
-    message[:, :rank] = node
-    message[:, rank:] = mm(node, node_up[0], PLAIN).astype(jnp.bfloat16)
+    lift = leaf_up[...].reshape(leaves * rank, rank)
+    lift = jnp.concatenate(
+        [lift, mm(lift, node_up[0], PLAIN).astype(jnp.bfloat16)], axis=1
+    )
+    side = lax.broadcasted_iota(jnp.int32, (columns, 2 * rank), 1) < rank
+    coeffs = []
+    for t in range(0, leaves, 2):
+        both = mm(
+            jnp.concatenate([dens[t], dens[t + 1]], axis=0),
+            jnp.concatenate([col[t], col[t + 1]], axis=0),
+            LAST,
+        ).astype(jnp.bfloat16)
+        coeff_out[t] = both[:columns, :rank]
+        coeff_out[t + 1] = both[columns:, rank:]
+        coeffs.append(jnp.where(side, both[:columns], both[columns:]))
+    message[...] = mm(jnp.concatenate(coeffs, axis=1), lift, PLAIN).astype(jnp.bfloat16)
 
 
 def pack_rows(pack, t, leaves, long, short):
@@ -82,40 +89,38 @@
 
 
 def field_kernel(
-    near_list, far_list, pair, own, cross, pair_other, own_other, cross_other, coup, near,
-    near_out, far_out, send, ext, ext_coeff,
+    near_list, far_list, pair, own, cross, all_other, coup, near, row,
+    keep, send, ext, ext_coeff,
 ):
     leaves, entries = near.shape[0], near.shape[1]
     columns = own.shape[1]
     rank = coup.shape[-1]
     halves = near.shape[-1] // 128
+    tiles = own.shape[0]
     me = lax.axis_index("leaf")
     odd = me & 1
-    for slot, pair_of_cores in (
-        (2 - 2 * odd, (pair, pair_other)),
-        (1, (own, own_other)),
-        (2 * odd, (cross, cross_other)),
-    ):
-        for c, ref in enumerate(pair_of_cores):
+    for k, (slot, ref) in enumerate(((2 - 2 * odd, pair), (2 * odd, cross), (1, own))):
+        for c, part in enumerate((ref, all_other.at[k * tiles : (k + 1) * tiles])):
             rows = slice(c * columns, (c + 1) * columns)
             for t in range(leaves):
-                ext[slot * leaves + t, rows] = unpack_long(ref, t, halves)
-                ext_coeff[slot * leaves + t, rows] = unpack_short(ref, t, leaves, halves, rank)
+                ext[slot * leaves + t, rows] = unpack_long(part, t, halves)
+                ext_coeff[slot * leaves + t, rows] = unpack_short(part, t, leaves, halves, rank)
     offset = (me - 1) * leaves
     for t in range(leaves):
-        total = None
-        for j in range(entries):
-            term = mm(ext[near_list[j, t] - offset], near[t, j], LAST)
-            total = term if total is None else total + term
         far = None
         for j in range(entries):
             term = mm(ext_coeff[far_list[j, t] - offset], coup[t, j], LAST)
             far = term if far is None else far + term
-        near_out[t] = total[:columns]
-        far_out[t] = far[:columns]
-        pack_rows(
-            send, t, leaves, total[columns:].astype(jnp.bfloat16), far[columns:].astype(jnp.bfloat16)
-        )
+        total = mm(far.astype(jnp.bfloat16), row[t], PLAIN)
+        for j in range(entries):
+            total = total + mm(ext[near_list[j, t] - offset], near[t, j], LAST)
+        keep[t] = total[:columns]
+        send[t] = total[columns:].astype(jnp.bfloat16)
+
+
+def place_of(distance, nodes):
+    block = (4896 >> (4 * (distance & 3))) & 3
+    return block * (nodes // 4) + (distance >> 2)
 
 
 def weights_kernel(
@@ -130,7 +135,7 @@
         to_points[t] = mm(leaf_down[t], row[t], (((0,), (0,)), ((), ()))).astype(jnp.bfloat16)
     named[...] = jnp.zeros_like(named)
     for j in range(farc):
-        place = node_list[0, j] ^ me
+        place = place_of(node_list[0, j] ^ me, nodes)
         named[place] = named[place] + node_coup[0, j].astype(jnp.float32)
     for height in range(1, levels):
         breadth = 2**height
@@ -150,28 +155,20 @@
         lifted = mm(node_down[0], tree[levels - 2][parent].astype(jnp.bfloat16), PLAIN)
         lifted = lifted.astype(jnp.bfloat16)
         for n in (2 * parent, 2 * parent + 1):
-            to_field[n ^ me, :, rank:] = lifted
+            to_field[place_of(n ^ me, nodes), :, rank:] = lifted
     for place in range(nodes):
         to_field[place, :, :rank] = named[place].astype(jnp.bfloat16)
 
 
-def base_kernel(near, far, received, row, base):
-    leaves, rank = row.shape[0], row.shape[1]
-    halves = near.shape[2] // 128
-    for t in range(leaves):
-        local = far[t] + unpack_short(received, t, leaves, halves, rank).astype(jnp.float32)
-        close = near[t] + unpack_long(received, t, halves).astype(jnp.float32)
-        base[t] = close + mm(local.astype(jnp.bfloat16), row[t], PLAIN)
-
-
-def down_kernel(known, other, to_field, to_points, base, out):
-    half = known.shape[0]
-    messages = [known[p] for p in range(half)] + [other[p] for p in range(half)]
-    matrices = [to_field[p] for p in range(2 * half)]
+def down_kernel(to_field, to_points, keep, received, *rest):
+    *gathered, out = rest
+    messages = [part[p] for part in gathered for p in range(part.shape[0])]
+    matrices = [to_field[p] for p in range(to_field.shape[0])]
     field = mm(jnp.concatenate(messages, axis=1), jnp.concatenate(matrices, axis=1), LAST)
     field = field.astype(jnp.bfloat16)
     for t in range(out.shape[0]):
-        out[t] = (base[t] + mm(field, to_points[t], PLAIN)).astype(jnp.bfloat16)
+        rest = keep[t] + received[t].astype(jnp.float32)
+        out[t] = (rest + mm(field, to_points[t], PLAIN)).astype(jnp.bfloat16)
 
 
 def body(
@@ -201,6 +198,7 @@
     swap = [(0, 1), (1, 0)]
 
     dens = jnp.swapaxes(density, 1, 2)
+    row = jnp.swapaxes(row_basis, 1, 2)
     coeff, message, dens_here = pl.pallas_call(
         up_kernel,
         out_shape=(
@@ -228,7 +226,6 @@
         ),
         name="pack",
     )(pinned(dens_here, pltpu.VMEM), pinned(coeff, pltpu.VMEM))
-    staged = (near_index.T, leaf_list.T, leaf_coupling, near_blocks)
     cores = lax.axis_size("sub")
     others = [
         (i * cores + c, (i + 1 if i % 2 else i - 1) * cores + c)
@@ -239,7 +236,6 @@
 
     cross = lax.ppermute(pack, ("leaf", "sub"), others)
     pair = lax.ppermute(pack, "leaf", [(i, i ^ 1) for i in range(nodes)])
-    own_other = lax.ppermute(pack, "sub", swap)
 
     entries = near_blocks.shape[1]
 
@@ -248,11 +244,10 @@
             field_kernel,
             out_shape=(
                 pltpu.VMEM((leaves, columns, points), f32),
-                pltpu.VMEM((leaves, columns, rank), f32),
-                pltpu.VMEM((tiles, columns, 128), bf16),
+                pltpu.VMEM((leaves, columns, points), bf16),
             ),
-            in_specs=[smem()] * 2 + [vmem()] * 8,
-            out_specs=(vmem(),) * 3,
+            in_specs=[smem()] * 2 + [vmem()] * 7,
+            out_specs=(vmem(),) * 2,
             scratch_shapes=[
                 pltpu.VMEM((3 * leaves, 2 * columns, points), bf16),
                 pltpu.VMEM((3 * leaves, 2 * columns, rank), bf16),
@@ -264,9 +259,8 @@
                 transcendentals=0,
             ),
             name="fields",
-        )(staged[0], staged[1], *packs, staged[2], staged[3])
-
-    row = jnp.swapaxes(row_basis, 1, 2)
+        )(near_index.T, leaf_list.T, *packs, leaf_coupling, near_blocks, row)
+
     weights = pl.pallas_call(
         weights_kernel,
         out_shape=(
@@ -288,45 +282,31 @@
     )
 
     known = message[None]
-    for bit in range(levels):
+    for bit in range(2, levels):
         step = 1 << bit
         other = lax.ppermute(known, "leaf", [(i, i ^ step) for i in range(nodes)])
-        if bit == 0:
+        if bit == 2:
             known, other, pack = lax.optimization_barrier((known, other, pack))
-        if bit == 1:
-            known, other, cross, pair, own_other, weights = lax.optimization_barrier(
-                (known, other, cross, pair, own_other, weights)
+        if bit == 3:
+            known, other, cross, pair, weights = lax.optimization_barrier(
+                (known, other, cross, pair, weights)
             )
-            pair_other = lax.ppermute(pair, "sub", swap)
-            cross_other = lax.ppermute(cross, "sub", swap)
-        if bit == levels - 2:
-            near, far, send = fields(pair, pack, cross, pair_other, own_other, cross_other)
-            known, other, near, far, send = lax.optimization_barrier(
-                (known, other, near, far, send)
-            )
-        if bit < levels - 1:
-            known = jnp.concatenate([known, other], axis=0)
+        known = jnp.concatenate([known, other], axis=0)
+    all_other = lax.ppermute(jnp.concatenate([pair, cross, pack], axis=0), "sub", swap)
+    others = [
+        lax.ppermute(known, "leaf", [(i, i ^ step) for i in range(nodes)]) for step in (3, 1, 2)
+    ]
+    keep, send = fields(pair, pack, cross, all_other)
+    others, keep, send = lax.optimization_barrier((others, keep, send))
     received = lax.ppermute(send, "sub", swap)
-    base = pl.pallas_call(
-        base_kernel,
-        out_shape=pltpu.VMEM((leaves, columns, points), f32),
-        in_specs=[vmem()] * 4,
-        out_specs=vmem(),
-        compiler_params=limit(4),
-        cost_estimate=pl.CostEstimate(
-            flops=1_000_000_000, bytes_accessed=1_000_000, transcendentals=0
-        ),
-        name="base",
-    )(near, far, received, row)
-    other, base = lax.optimization_barrier((other, base))
     out = pl.pallas_call(
         down_kernel,
         out_shape=jax.ShapeDtypeStruct((leaves, columns, points), bf16),
-        in_specs=[vmem()] * 5,
+        in_specs=[vmem()] * 8,
         out_specs=vmem(),
         compiler_params=limit(8),
         name="down",
-    )(known, other, *weights, base)
+    )(*weights, keep, received, known, *others)
     return jnp.swapaxes(out, 1, 2)
 
 

time: 21.9 us -> 20.6 us (0.941)
  waiting for transfers between devices: 2.46 us -> 1.26 us
    ppermute x4 -> x2, starting transfers between devices: 8.77 us -> 5.69 us  [body(): other = lax.ppermute(known, 'leaf', [(i, i ^ step) for i in range(nodes)])]
    ppermute x3 -> x4, starting transfers between devices: 0.58 us -> 3.62 us  [the longest x3 3.55 us: body(): lax.ppermute(known, 'leaf', [(i, i ^ step) for i in range(nodes)])]
    ppermute x4 -> x2, waiting for transfers between devices: 2.45 us -> 0.01 us  [body(): other = lax.ppermute(known, 'leaf', [(i, i ^ step) for i in range(nodes)])]
    ppermute x1, waiting for transfers between devices: 0.01 us -> 1.24 us  [body(): received = lax.ppermute(send, 'sub', swap)]
    pallas_call x1, Pallas kernels: 1.81 us -> 2.08 us  [fields(): pl.pallas_call(field_kernel, out_shape=(pltpu.VMEM((leaves, columns, poin...]
    pallas_call x1, Pallas kernels: 1.63 us -> 1.4 us  [body(): pl.pallas_call(up_kernel, out_shape=(pltpu.VMEM((leaves, columns, rank),...]
  transfers between devices with their start and end apart: 10 -> 9, of which waited for: 3 -> 1; matrix products, arithmetic and copies ran while one was open for 0% -> 0% of each run, Pallas kernels for 18% -> 20%
where the time goes in v9:
time: 20.6 us; the launch traced here: 20.5 us
  starting transfers between devices  12.4 us (60%)
  Pallas kernels  6.46 us (31%)
  waiting for transfers between devices  1.26 us (6%)
  between operations  0.25 us (1%)
    ppermute x2, starting transfers between devices, body(): other = lax.ppermute(known, 'leaf', [(i, i ^ step) for i in range(nodes)])  5.69 us
    ppermute x3, starting transfers between devices, body(): lax.ppermute(known, 'leaf', [(i, i ^ step) for i in range(nodes)])  3.55 us
    ppermute x1, starting transfers between devices, body(): pair = lax.ppermute(pack, 'leaf', [(i, i ^ 1) for i in range(nodes)])  2.97 us
    pallas_call x1, Pallas kernels, fields(): pl.pallas_call(field_kernel, out_shape=(pltpu.VMEM((leaves, columns, poin...  2.08 us
    pallas_call x1, Pallas kernels, body(): pl.pallas_call(weights_kernel, out_shape=(pltpu.VMEM((nodes, rank, 2 * ra...  1.88 us
    pallas_call x1, Pallas kernels, body(): pl.pallas_call(up_kernel, out_shape=(pltpu.VMEM((leaves, columns, rank),...  1.4 us
    ppermute x1, waiting for transfers between devices, body(): received = lax.ppermute(send, 'sub', swap)  1.24 us
    pallas_call x1, Pallas kernels, body(): pl.pallas_call(down_kernel, out_shape=jax.ShapeDtypeStruct((leaves, colum...  1.02 us
  transfers between devices with their start and end apart: 9, of which 1 were waited for; matrix products, arithmetic and copies ran while one was open for 0% of the time, Pallas kernels for 20%

profile of v9, /device:TPU:0, one launch (start us, length us, event | category | flops | bytes accessed | tf_op | source)
XLA Modules:
  0.0 20.5 jit_solution(7002791200054657794)
XLA Ops:
  0.0 1.4 %up.1 = (bf16[8,16,64]{2,1,0:T(8,128)(2,1)S(1)}, bf16[16,128]{1,0:T(8,128)(2,1)S(1)}, bf16[8,16,256]{2,1,0:T(8,128)(2,1)S(1)}) custom-call(bf16[8,16,256]{2,1,0:T(8,128)(2,1)} %bitcast.16, bf16[8,64,256]{2,1,0:T(8,128)(2,1)} %bitcast.15, bf16[8,64,64]{2,1,0:T(8,128)(2,1)} %leaf_up.1, bf16[1,64,64]{2,1,0:T(8,128)(2,1)} %node_up.1), custom_call_target="tpu_custom_call" | custom-call | flops 2000000000 | bytes 5000000 | tf_op jit(solution)/shard_map/up/pallas_call | solution.py:202
  1.4 3.0 %collective-permute-start = (bf16[1,16,128]{2,1,0:T(8,128)(2,1)S(1)}, bf16[1,16,128]{2,1,0:T(8,128)(2,1)S(1)}, u32[]{:S(2)}, u32[]{:S(2)}) collective-permute-start(bf16[1,16,128]{2,1,0:T(8,128)(2,1)S(1)} %bitcast.10), channel_id=1, source_target_pairs={{0,8},{2,10},{4,12},{6,14},{8,0},{10,2},{12,4},{14,6},{16,24},{18,... | collective-permute-start | bytes 12296 | tf_op jit(solution)/shard_map/ppermute | solution.py:287
  4.4 0.0 copy-start.2
  4.4 0.0 copy-start.5
  4.4 0.0 copy-start.6
  4.4 0.0 copy-start.7
  4.4 0.0 copy-start.8
  4.5 0.0 copy-start.9
  4.5 0.0 copy-start.10
  4.5 0.0 copy-start.11
  4.5 0.0 copy-start.12
  4.5 0.1 pack.1.own
  4.6 0.0 collective-permute-start.2
  4.6 3.0 %collective-permute-start.3 = (bf16[20,16,128]{2,1,0:T(8,128)(2,1)S(1)}, bf16[20,16,128]{2,1,0:T(8,128)(2,1)S(1)}, u32[]{:S(2)}, u32[]{:S(2)}) collective-permute-start(bf16[20,16,128]{2,1,0:T(8,128)(2,1)S(1)} %pack.1.own), channel_id=1, source_target_pairs={{0,2},{2,0},{4,6},{6,4},{8,10},{10,8},{12,14},{14,12},{16,18},{18,... | collective-permute-start | bytes 245768 | tf_op jit(solution)/shard_map/ppermute | solution.py:238
  7.6 0.0 collective-permute-done
  7.6 2.7 %collective-permute-start.1 = (bf16[2,16,128]{2,1,0:T(8,128)(2,1)S(1)}, bf16[2,16,128]{2,1,0:T(8,128)(2,1)S(1)}, u32[]{:S(2)}, u32[]{:S(2)}) collective-permute-start(bf16[2,16,128]{2,1,0:T(8,128)(2,1)S(1)} %constant_dynamic-update-slice_fusion), channel_id=1, source_target_pairs={{0,16},{2,18},{4,20},{6,22},{8,24},{10,26},{12,28},{14,30},{16,0},... | collective-permute-start | bytes 24584 | tf_op jit(solution)/shard_map/ppermute | solution.py:287
  10.2 0.0 copy-done.2
  10.3 0.0 copy-done.5
  10.3 0.0 copy-done.6
  10.3 0.0 copy-done.7
  10.3 0.0 copy-done.8
  10.3 0.0 copy-done.9
  10.3 0.0 copy-done.10
  10.3 0.0 copy-done.11
  10.3 0.0 copy-done.12
  10.3 0.0 copy-start
  10.3 0.0 copy-start.1
  10.3 0.0 copy-start.3
  10.3 0.0 copy-start.4
  10.4 1.9 %weights.1 = (bf16[16,64,128]{2,1,0:T(8,128)(2,1)S(1)}, bf16[8,64,256]{2,1,0:T(8,128)(2,1)S(1)}) custom-call(s32[1,4]{1,0:T(1,128)S(1)} %copy-done.12, s32[4,14]{1,0:T(4,128)S(1)} %bitcast.14, bf16[1,4,64,64]{3,2,1,0:T(8,128)(2,1)S(1)} %copy-done.9, bf16[1,64,64]{2,1,0:T(8,128)(2,1)S(1)} %copy-done.10, bf16[14,4,64,64]{3,2,1,0:T(8,128)(2,1)S(1)} %copy-done.5, ...), custom_call_target="tpu_custom_call" | custom-call | flops 2000000000 | bytes 3000000 | tf_op jit(solution)/shard_map/weights/pallas_call | solution.py:264
  12.2 0.0 collective-permute-done.1
  12.3 0.0 collective-permute-done.2.cross
  12.3 0.0 collective-permute-done.3.pair
  12.3 0.1 collective-permute-start.7
  12.4 1.5 %collective-permute-start.4 = (bf16[4,16,128]{2,1,0:T(8,128)(2,1)S(1)}, bf16[4,16,128]{2,1,0:T(8,128)(2,1)S(1)}, u32[]{:S(2)}, u32[]{:S(2)}) collective-permute-start(bf16[4,16,128]{2,1,0:T(8,128)(2,1)S(1)} %constant_dynamic-update-slice_fusion.2.rest_0_), channel_id=1, source_target_pairs={{0,6},{2,4},{4,2},{6,0},{8,14},{10,12},{12,10},{14,8},{16,22},{18,... | collective-permute-start | bytes 49160 | tf_op jit(solution)/shard_map/ppermute | solution.py:297
  13.9 0.4 %collective-permute-start.5 = (bf16[4,16,128]{2,1,0:T(8,128)(2,1)S(1)}, bf16[4,16,128]{2,1,0:T(8,128)(2,1)S(1)}, u32[]{:S(2)}, u32[]{:S(2)}) collective-permute-start(bf16[4,16,128]{2,1,0:T(8,128)(2,1)S(1)} %constant_dynamic-update-slice_fusion.2.rest_0_), channel_id=1, source_target_pairs={{0,2},{2,0},{4,6},{6,4},{8,10},{10,8},{12,14},{14,12},{16,18},{18,... | collective-permute-start | bytes 49160 | tf_op jit(solution)/shard_map/ppermute | solution.py:297
  14.3 1.6 %collective-permute-start.6 = (bf16[4,16,128]{2,1,0:T(8,128)(2,1)S(1)}, bf16[4,16,128]{2,1,0:T(8,128)(2,1)S(1)}, u32[]{:S(2)}, u32[]{:S(2)}) collective-permute-start(bf16[4,16,128]{2,1,0:T(8,128)(2,1)S(1)} %constant_dynamic-update-slice_fusion.2.rest_0_), channel_id=1, source_target_pairs={{0,4},{2,6},{4,0},{6,2},{8,12},{10,14},{12,8},{14,10},{16,20},{18,... | collective-permute-start | bytes 49160 | tf_op jit(solution)/shard_map/ppermute | solution.py:297
  16.0 0.0 collective-permute-done.7.all_other
  16.0 0.0 copy-done
  16.0 0.0 copy-done.1
  16.0 0.0 copy-done.3
  16.0 0.0 copy-done.4
  16.0 2.1 %fields.1 = (f32[8,16,256]{2,1,0:T(8,128)S(1)}, bf16[8,16,256]{2,1,0:T(8,128)(2,1)S(1)}) custom-call(s32[3,8]{1,0:T(4,128)S(1)} %bitcast.12, s32[3,8]{1,0:T(4,128)S(1)} %bitcast.13, bf16[20,16,128]{2,1,0:T(8,128)(2,1)S(1)} %collective-permute-done.3.pair, bf16[20,16,128]{2,1,0:T(8,128)(2,1)S(1)} %pack.1.own, ...), custom_call_target="tpu_custom_call" | custom-call | flops 805306368 | bytes 3145728 | tf_op jit(solution)/shard_map/fields/pallas_call | solution.py:243
  18.1 0.0 collective-permute-done.4.rest_1_
  18.1 0.0 collective-permute-done.5.rest_2_
  18.1 0.0 collective-permute-done.6.rest_3_
  18.1 0.1 collective-permute-start.8
  18.2 1.2 %collective-permute-done.8.received = bf16[8,16,256]{2,1,0:T(8,128)(2,1)S(1)} collective-permute-done((bf16[8,16,256]{2,1,0:T(8,128)(2,1)S(1)}, bf16[8,16,256]{2,1,0:T(8,128)(2,1)S(1)}, u32[]{:S(2)}, u32[]{:S(2)}) %collective-permute-start.8) | collective-permute-done | bytes 65568 | tf_op jit(solution)/shard_map/ppermute | solution.py:301
  19.4 1.0 %down.1 = bf16[8,16,256]{2,1,0:T(8,128)(2,1)} custom-call(bf16[16,64,128]{2,1,0:T(8,128)(2,1)S(1)} %get-tuple-element.33.to_field, bf16[8,64,256]{2,1,0:T(8,128)(2,1)S(1)} %get-tuple-element.34.to_points, f32[8,16,256]{2,1,0:T(8,128)S(1)} %get-tuple-element.42.keep, bf16[8,16,256]{2,1,0:T(8,128)(2,1)S(1)} %collective-permute-done.8.received, ...), custom_call_target="tpu_custom_call" | custom-call | tf_op jit(solution)/shard_map/down/pallas_call | solution.py:302
  (5 shorter events, 0.1 us)
Async XLA Ops:
  1.4 6.2 %collective-permute-start = (bf16[1,16,128]{2,1,0:T(8,128)(2,1)S(1)}, bf16[1,16,128]{2,1,0:T(8,128)(2,1)S(1)}, u32[]{:S(2)}, u32[]{:S(2)}) collective-permute-start(bf16[1,16,128]{2,1,0:T(8,128)(2,1)S(1)} %bitcast.10), channel_id=1, source_target_pairs={{0,8},{2,10},{4,12},{6,14},{8,0},{10,2},{12,4},{14,6},{16,24},{18,... | collective-permute-start | bytes 12296 | tf_op jit(solution)/shard_map/ppermute | solution.py:287
  4.4 5.8 %copy-start.2 = (bf16[8,256,64]{1,2,0:T(8,128)(2,1)S(1)}, bf16[8,256,64]{1,2,0:T(8,128)(2,1)}, u32[]{:S(2)}) copy-start(bf16[8,256,64]{1,2,0:T(8,128)(2,1)} %param.21) | copy-start | bytes 786436
  4.4 5.8 %copy-start.5 = (bf16[14,4,64,64]{3,2,1,0:T(8,128)(2,1)S(1)}, bf16[14,4,64,64]{3,2,1,0:T(8,128)(2,1)}, u32[]{:S(2)}) copy-start(bf16[14,4,64,64]{3,2,1,0:T(8,128)(2,1)} %upper_coup.1) | copy-start | bytes 1376260
  4.4 5.8 %copy-start.6 = (bf16[12,64,64]{2,1,0:T(8,128)(2,1)S(1)}, bf16[12,64,64]{2,1,0:T(8,128)(2,1)}, u32[]{:S(2)}) copy-start(bf16[12,64,64]{2,1,0:T(8,128)(2,1)} %upper_up.1) | copy-start | bytes 294916
  4.4 5.8 %copy-start.7 = (bf16[12,64,64]{2,1,0:T(8,128)(2,1)S(1)}, bf16[12,64,64]{2,1,0:T(8,128)(2,1)}, u32[]{:S(2)}) copy-start(bf16[12,64,64]{2,1,0:T(8,128)(2,1)} %upper_down.1) | copy-start | bytes 294916
  4.4 5.8 %copy-start.8 = (bf16[8,64,64]{2,1,0:T(8,128)(2,1)S(1)}, bf16[8,64,64]{2,1,0:T(8,128)(2,1)}, u32[]{:S(2)}) copy-start(bf16[8,64,64]{2,1,0:T(8,128)(2,1)} %leaf_down.1) | copy-start | bytes 196612
  4.5 5.8 %copy-start.9 = (bf16[1,4,64,64]{3,2,1,0:T(8,128)(2,1)S(1)}, bf16[1,4,64,64]{3,2,1,0:T(8,128)(2,1)}, u32[]{:S(2)}) copy-start(bf16[1,4,64,64]{3,2,1,0:T(8,128)(2,1)} %node_coup.1) | copy-start | bytes 98308
  4.5 5.8 %copy-start.10 = (bf16[1,64,64]{2,1,0:T(8,128)(2,1)S(1)}, bf16[1,64,64]{2,1,0:T(8,128)(2,1)}, u32[]{:S(2)}) copy-start(bf16[1,64,64]{2,1,0:T(8,128)(2,1)} %node_down.1) | copy-start | bytes 24580
  4.5 5.8 %copy-start.11 = (s32[14,4]{0,1:T(4,128)S(1)}, s32[14,4]{0,1:T(4,128)}, u32[]{:S(2)}) copy-start(s32[14,4]{0,1:T(4,128)} %param.31) | copy-start | bytes 676
  4.5 5.8 %copy-start.12 = (s32[1,4]{1,0:T(1,128)S(1)}, s32[1,4]{1,0:T(1,128)}, u32[]{:S(2)}) copy-start(s32[1,4]{1,0:T(1,128)} %node_list.1) | copy-start | bytes 52
  4.6 7.7 %collective-permute-start.2 = (bf16[20,16,128]{2,1,0:T(8,128)(2,1)S(1)}, bf16[20,16,128]{2,1,0:T(8,128)(2,1)S(1)}, u32[]{:S(2)}, u32[]{:S(2)}) collective-permute-start(bf16[20,16,128]{2,1,0:T(8,128)(2,1)S(1)} %pack.1.own), channel_id=1, source_target_pairs={{2,4},{3,5},{4,2},{5,3},{6,8},{7,9},{8,6},{9,7},{10,12},{11,13},{1... | collective-permute-start | bytes 245768 | tf_op jit(solution)/shard_map/ppermute | solution.py:237
  4.6 7.7 %collective-permute-start.3 = (bf16[20,16,128]{2,1,0:T(8,128)(2,1)S(1)}, bf16[20,16,128]{2,1,0:T(8,128)(2,1)S(1)}, u32[]{:S(2)}, u32[]{:S(2)}) collective-permute-start(bf16[20,16,128]{2,1,0:T(8,128)(2,1)S(1)} %pack.1.own), channel_id=1, source_target_pairs={{0,2},{2,0},{4,6},{6,4},{8,10},{10,8},{12,14},{14,12},{16,18},{18,... | collective-permute-start | bytes 245768 | tf_op jit(solution)/shard_map/ppermute | solution.py:238
  7.6 4.7 %collective-permute-start.1 = (bf16[2,16,128]{2,1,0:T(8,128)(2,1)S(1)}, bf16[2,16,128]{2,1,0:T(8,128)(2,1)S(1)}, u32[]{:S(2)}, u32[]{:S(2)}) collective-permute-start(bf16[2,16,128]{2,1,0:T(8,128)(2,1)S(1)} %constant_dynamic-update-slice_fusion), channel_id=1, source_target_pairs={{0,16},{2,18},{4,20},{6,22},{8,24},{10,26},{12,28},{14,30},{16,0},... | collective-permute-start | bytes 24584 | tf_op jit(solution)/shard_map/ppermute | solution.py:287
  10.3 5.7 %copy-start = (bf16[8,3,256,256]{3,2,1,0:T(8,128)(2,1)S(1)}, bf16[8,3,256,256]{3,2,1,0:T(8,128)(2,1)}, u32[]{:S(2)}) copy-start(bf16[8,3,256,256]{3,2,1,0:T(8,128)(2,1)} %near.1) | copy-start | bytes 9437188
  10.3 5.7 %copy-start.1 = (bf16[8,3,64,64]{3,2,1,0:T(8,128)(2,1)S(1)}, bf16[8,3,64,64]{3,2,1,0:T(8,128)(2,1)}, u32[]{:S(2)}) copy-start(bf16[8,3,64,64]{3,2,1,0:T(8,128)(2,1)} %coup.1) | copy-start | bytes 589828
  10.3 5.7 %copy-start.3 = (s32[8,3]{0,1:T(4,128)S(1)}, s32[8,3]{0,1:T(4,128)}, u32[]{:S(2)}) copy-start(s32[8,3]{0,1:T(4,128)} %param.19) | copy-start | bytes 292
  10.3 5.7 %copy-start.4 = (s32[8,3]{0,1:T(4,128)S(1)}, s32[8,3]{0,1:T(4,128)}, u32[]{:S(2)}) copy-start(s32[8,3]{0,1:T(4,128)} %param.23) | copy-start | bytes 292
  12.3 3.7 %collective-permute-start.7 = (bf16[60,16,128]{2,1,0:T(8,128)(2,1)S(1)}, bf16[60,16,128]{2,1,0:T(8,128)(2,1)S(1)}, u32[]{:S(2)}, u32[]{:S(2)}) collective-permute-start(bf16[60,16,128]{2,1,0:T(8,128)(2,1)S(1)} %pad_maximum_fusion), channel_id=1, source_target_pairs={{0,1},{1,0},{2,3},{3,2},{4,5},{5,4},{6,7},{7,6},{8,9},{9,8},{10,11... | collective-permute-start | bytes 737288 | tf_op jit(solution)/shard_map/ppermute | solution.py:295
  12.4 5.7 %collective-permute-start.4 = (bf16[4,16,128]{2,1,0:T(8,128)(2,1)S(1)}, bf16[4,16,128]{2,1,0:T(8,128)(2,1)S(1)}, u32[]{:S(2)}, u32[]{:S(2)}) collective-permute-start(bf16[4,16,128]{2,1,0:T(8,128)(2,1)S(1)} %constant_dynamic-update-slice_fusion.2.rest_0_), channel_id=1, source_target_pairs={{0,6},{2,4},{4,2},{6,0},{8,14},{10,12},{12,10},{14,8},{16,22},{18,... | collective-permute-start | bytes 49160 | tf_op jit(solution)/shard_map/ppermute | solution.py:297
  13.9 4.2 %collective-permute-start.5 = (bf16[4,16,128]{2,1,0:T(8,128)(2,1)S(1)}, bf16[4,16,128]{2,1,0:T(8,128)(2,1)S(1)}, u32[]{:S(2)}, u32[]{:S(2)}) collective-permute-start(bf16[4,16,128]{2,1,0:T(8,128)(2,1)S(1)} %constant_dynamic-update-slice_fusion.2.rest_0_), channel_id=1, source_target_pairs={{0,2},{2,0},{4,6},{6,4},{8,10},{10,8},{12,14},{14,12},{16,18},{18,... | collective-permute-start | bytes 49160 | tf_op jit(solution)/shard_map/ppermute | solution.py:297
  14.3 3.8 %collective-permute-start.6 = (bf16[4,16,128]{2,1,0:T(8,128)(2,1)S(1)}, bf16[4,16,128]{2,1,0:T(8,128)(2,1)S(1)}, u32[]{:S(2)}, u32[]{:S(2)}) collective-permute-start(bf16[4,16,128]{2,1,0:T(8,128)(2,1)S(1)} %constant_dynamic-update-slice_fusion.2.rest_0_), channel_id=1, source_target_pairs={{0,4},{2,6},{4,0},{6,2},{8,12},{10,14},{12,8},{14,10},{16,20},{18,... | collective-permute-start | bytes 49160 | tf_op jit(solution)/shard_map/ppermute | solution.py:297
  18.1 1.3 %collective-permute-start.8 = (bf16[8,16,256]{2,1,0:T(8,128)(2,1)S(1)}, bf16[8,16,256]{2,1,0:T(8,128)(2,1)S(1)}, u32[]{:S(2)}, u32[]{:S(2)}) collective-permute-start(bf16[8,16,256]{2,1,0:T(8,128)(2,1)S(1)} %get-tuple-element.43), channel_id=1, source_target_pairs={{0,1},{1,0},{2,3},{3,2},{4,5},{5,4},{6,7},{7,6},{8,9},{9,8},{10,11... | collective-permute-start | bytes 196616 | tf_op jit(solution)/shard_map/ppermute | solution.py:301

commit v10 on v9

--- a/solution.py
+++ b/solution.py
@@ -111,9 +111,12 @@
         for j in range(entries):
             term = mm(ext_coeff[far_list[j, t] - offset], coup[t, j], LAST)
             far = term if far is None else far + term
+        sources = [ext[near_list[j, t] - offset] for j in range(entries)]
+        matrices = [near[t, j] for j in range(entries)]
         total = mm(far.astype(jnp.bfloat16), row[t], PLAIN)
-        for j in range(entries):
-            total = total + mm(ext[near_list[j, t] - offset], near[t, j], LAST)
+        total = total + mm(
+            jnp.concatenate(sources, axis=1), jnp.concatenate(matrices, axis=1), LAST
+        )
         keep[t] = total[:columns]
         send[t] = total[columns:].astype(jnp.bfloat16)
 
@@ -160,15 +163,14 @@
         to_field[place, :, :rank] = named[place].astype(jnp.bfloat16)
 
 
-def down_kernel(to_field, to_points, keep, received, *rest):
+def down_kernel(to_field, to_points, keep, *rest):
     *gathered, out = rest
     messages = [part[p] for part in gathered for p in range(part.shape[0])]
     matrices = [to_field[p] for p in range(to_field.shape[0])]
     field = mm(jnp.concatenate(messages, axis=1), jnp.concatenate(matrices, axis=1), LAST)
     field = field.astype(jnp.bfloat16)
     for t in range(out.shape[0]):
-        rest = keep[t] + received[t].astype(jnp.float32)
-        out[t] = (rest + mm(field, to_points[t], PLAIN)).astype(jnp.bfloat16)
+        out[t] = keep[t] + mm(field, to_points[t], PLAIN)
 
 
 def body(
@@ -299,14 +301,18 @@
     keep, send = fields(pair, pack, cross, all_other)
     others, keep, send = lax.optimization_barrier((others, keep, send))
     received = lax.ppermute(send, "sub", swap)
-    out = pl.pallas_call(
+    part = pl.pallas_call(
         down_kernel,
-        out_shape=jax.ShapeDtypeStruct((leaves, columns, points), bf16),
-        in_specs=[vmem()] * 8,
+        out_shape=pltpu.VMEM((leaves, columns, points), f32),
+        in_specs=[vmem()] * 7,
         out_specs=vmem(),
         compiler_params=limit(8),
+        cost_estimate=pl.CostEstimate(
+            flops=1_000_000_000, bytes_accessed=1_000_000, transcendentals=0
+        ),
         name="down",
-    )(*weights, keep, received, known, *others)
+    )(*weights, keep, known, *others)
+    out = (part + received.astype(f32)).astype(bf16)
     return jnp.swapaxes(out, 1, 2)
 
 

time: 20.6 us -> 20.2 us (0.981)
  Pallas kernels: 6.46 us -> 5.61 us
  other arithmetic: 0.03 us -> 0.68 us
    transpose x0 -> x1, other arithmetic: none -> 0.65 us  [body(): return jnp.swapaxes(out, 1, 2)]
    pallas_call x1, Pallas kernels: 1.02 us -> 0.38 us  [body(): pl.pallas_call(down_kernel, out_shape=pltpu.VMEM((leaves, columns, points...]
    ppermute x1, waiting for transfers between devices: 1.24 us -> 0.86 us  [body(): received = lax.ppermute(send, 'sub', swap)]
  transfers between devices with their start and end apart: 9 -> 9, of which waited for: 1 -> 2; matrix products, arithmetic and copies ran while one was open for 0% -> 0% of each run, Pallas kernels for 20% -> 21%
where the time goes in v10:
time: 20.2 us; the launch traced here: 20 us
  starting transfers between devices  12.3 us (61%)
  Pallas kernels  5.61 us (28%)
  waiting for transfers between devices  1.06 us (5%)
  other arithmetic  0.68 us (3%)
  between operations  0.24 us (1%)
    ppermute x2, starting transfers between devices, body(): other = lax.ppermute(known, 'leaf', [(i, i ^ step) for i in range(nodes)])  5.69 us
    ppermute x3, starting transfers between devices, body(): lax.ppermute(known, 'leaf', [(i, i ^ step) for i in range(nodes)])  3.55 us
    ppermute x1, starting transfers between devices, body(): pair = lax.ppermute(pack, 'leaf', [(i, i ^ 1) for i in range(nodes)])  2.97 us
    pallas_call x1, Pallas kernels, body(): pl.pallas_call(weights_kernel, out_shape=(pltpu.VMEM((nodes, rank, 2 * ra...  1.88 us
    pallas_call x1, Pallas kernels, fields(): pl.pallas_call(field_kernel, out_shape=(pltpu.VMEM((leaves, columns, poin...  1.88 us
    pallas_call x1, Pallas kernels, body(): pl.pallas_call(up_kernel, out_shape=(pltpu.VMEM((leaves, columns, rank),...  1.4 us
    ppermute x1, waiting for transfers between devices, body(): received = lax.ppermute(send, 'sub', swap)  0.86 us
    transpose x1, other arithmetic, body(): return jnp.swapaxes(out, 1, 2)  0.65 us
  transfers between devices with their start and end apart: 9, of which 2 were waited for; matrix products, arithmetic and copies ran while one was open for 0% of the time, Pallas kernels for 21%

profile of v10, /device:TPU:0, one launch (start us, length us, event | category | flops | bytes accessed | tf_op | source)
XLA Modules:
  0.0 20.0 jit_solution(9935519650374636609)
XLA Ops:
  0.0 1.4 %up.1 = (bf16[8,16,64]{2,1,0:T(8,128)(2,1)S(1)}, bf16[16,128]{1,0:T(8,128)(2,1)S(1)}, bf16[8,16,256]{2,1,0:T(8,128)(2,1)S(1)}) custom-call(bf16[8,16,256]{2,1,0:T(8,128)(2,1)} %bitcast.17, bf16[8,64,256]{2,1,0:T(8,128)(2,1)} %bitcast.16, bf16[8,64,64]{2,1,0:T(8,128)(2,1)} %leaf_up.1, bf16[1,64,64]{2,1,0:T(8,128)(2,1)} %node_up.1), custom_call_target="tpu_custom_call" | custom-call | flops 2000000000 | bytes 5000000 | tf_op jit(solution)/shard_map/up/pallas_call | solution.py:204
  1.4 3.0 %collective-permute-start = (bf16[1,16,128]{2,1,0:T(8,128)(2,1)S(1)}, bf16[1,16,128]{2,1,0:T(8,128)(2,1)S(1)}, u32[]{:S(2)}, u32[]{:S(2)}) collective-permute-start(bf16[1,16,128]{2,1,0:T(8,128)(2,1)S(1)} %bitcast.11), channel_id=1, source_target_pairs={{0,8},{2,10},{4,12},{6,14},{8,0},{10,2},{12,4},{14,6},{16,24},{18,... | collective-permute-start | bytes 12296 | tf_op jit(solution)/shard_map/ppermute | solution.py:289
  4.4 0.0 copy-start.2
  4.4 0.0 copy-start.5
  4.4 0.0 copy-start.6
  4.4 0.0 copy-start.7
  4.4 0.0 copy-start.8
  4.5 0.0 copy-start.9
  4.5 0.0 copy-start.10
  4.5 0.0 copy-start.11
  4.5 0.0 copy-start.12
  4.5 0.1 pack.1.own
  4.6 0.0 collective-permute-start.2
  4.6 3.0 %collective-permute-start.3 = (bf16[20,16,128]{2,1,0:T(8,128)(2,1)S(1)}, bf16[20,16,128]{2,1,0:T(8,128)(2,1)S(1)}, u32[]{:S(2)}, u32[]{:S(2)}) collective-permute-start(bf16[20,16,128]{2,1,0:T(8,128)(2,1)S(1)} %pack.1.own), channel_id=1, source_target_pairs={{0,2},{2,0},{4,6},{6,4},{8,10},{10,8},{12,14},{14,12},{16,18},{18,... | collective-permute-start | bytes 245768 | tf_op jit(solution)/shard_map/ppermute | solution.py:240
  7.6 0.0 collective-permute-done
  7.6 2.7 %collective-permute-start.1 = (bf16[2,16,128]{2,1,0:T(8,128)(2,1)S(1)}, bf16[2,16,128]{2,1,0:T(8,128)(2,1)S(1)}, u32[]{:S(2)}, u32[]{:S(2)}) collective-permute-start(bf16[2,16,128]{2,1,0:T(8,128)(2,1)S(1)} %constant_dynamic-update-slice_fusion), channel_id=1, source_target_pairs={{0,16},{2,18},{4,20},{6,22},{8,24},{10,26},{12,28},{14,30},{16,0},... | collective-permute-start | bytes 24584 | tf_op jit(solution)/shard_map/ppermute | solution.py:289
  10.2 0.0 copy-done.2
  10.3 0.0 copy-done.5
  10.3 0.0 copy-done.6
  10.3 0.0 copy-done.7
  10.3 0.0 copy-done.8
  10.3 0.0 copy-done.9
  10.3 0.0 copy-done.10
  10.3 0.0 copy-done.11
  10.3 0.0 copy-done.12
  10.3 0.0 copy-start
  10.3 0.0 copy-start.1
  10.3 0.0 copy-start.3
  10.3 0.0 copy-start.4
  10.4 1.9 %weights.1 = (bf16[16,64,128]{2,1,0:T(8,128)(2,1)S(1)}, bf16[8,64,256]{2,1,0:T(8,128)(2,1)S(1)}) custom-call(s32[1,4]{1,0:T(1,128)S(1)} %copy-done.12, s32[4,14]{1,0:T(4,128)S(1)} %bitcast.15, bf16[1,4,64,64]{3,2,1,0:T(8,128)(2,1)S(1)} %copy-done.9, bf16[1,64,64]{2,1,0:T(8,128)(2,1)S(1)} %copy-done.10, bf16[14,4,64,64]{3,2,1,0:T(8,128)(2,1)S(1)} %copy-done.5, ...), custom_call_target="tpu_custom_call" | custom-call | flops 2000000000 | bytes 3000000 | tf_op jit(solution)/shard_map/weights/pallas_call | solution.py:266
  12.2 0.0 collective-permute-done.1
  12.3 0.0 collective-permute-done.2.cross
  12.3 0.0 collective-permute-done.3.pair
  12.3 0.1 collective-permute-start.7
  12.4 1.5 %collective-permute-start.4 = (bf16[4,16,128]{2,1,0:T(8,128)(2,1)S(1)}, bf16[4,16,128]{2,1,0:T(8,128)(2,1)S(1)}, u32[]{:S(2)}, u32[]{:S(2)}) collective-permute-start(bf16[4,16,128]{2,1,0:T(8,128)(2,1)S(1)} %constant_dynamic-update-slice_fusion.2.rest_0_), channel_id=1, source_target_pairs={{0,6},{2,4},{4,2},{6,0},{8,14},{10,12},{12,10},{14,8},{16,22},{18,... | collective-permute-start | bytes 49160 | tf_op jit(solution)/shard_map/ppermute | solution.py:299
  13.9 0.4 %collective-permute-start.5 = (bf16[4,16,128]{2,1,0:T(8,128)(2,1)S(1)}, bf16[4,16,128]{2,1,0:T(8,128)(2,1)S(1)}, u32[]{:S(2)}, u32[]{:S(2)}) collective-permute-start(bf16[4,16,128]{2,1,0:T(8,128)(2,1)S(1)} %constant_dynamic-update-slice_fusion.2.rest_0_), channel_id=1, source_target_pairs={{0,2},{2,0},{4,6},{6,4},{8,10},{10,8},{12,14},{14,12},{16,18},{18,... | collective-permute-start | bytes 49160 | tf_op jit(solution)/shard_map/ppermute | solution.py:299
  14.3 1.6 %collective-permute-start.6 = (bf16[4,16,128]{2,1,0:T(8,128)(2,1)S(1)}, bf16[4,16,128]{2,1,0:T(8,128)(2,1)S(1)}, u32[]{:S(2)}, u32[]{:S(2)}) collective-permute-start(bf16[4,16,128]{2,1,0:T(8,128)(2,1)S(1)} %constant_dynamic-update-slice_fusion.2.rest_0_), channel_id=1, source_target_pairs={{0,4},{2,6},{4,0},{6,2},{8,12},{10,14},{12,8},{14,10},{16,20},{18,... | collective-permute-start | bytes 49160 | tf_op jit(solution)/shard_map/ppermute | solution.py:299
  16.0 0.0 collective-permute-done.7.all_other
  16.0 0.0 copy-done
  16.0 0.0 copy-done.1
  16.0 0.0 copy-done.3
  16.0 0.0 copy-done.4
  16.0 1.9 %fields.1 = (f32[8,16,256]{2,1,0:T(8,128)S(1)}, bf16[8,16,256]{2,1,0:T(8,128)(2,1)S(1)}) custom-call(s32[3,8]{1,0:T(4,128)S(1)} %bitcast.13, s32[3,8]{1,0:T(4,128)S(1)} %bitcast.14, bf16[20,16,128]{2,1,0:T(8,128)(2,1)S(1)} %collective-permute-done.3.pair, bf16[20,16,128]{2,1,0:T(8,128)(2,1)S(1)} %pack.1.own, ...), custom_call_target="tpu_custom_call" | custom-call | flops 805306368 | bytes 3145728 | tf_op jit(solution)/shard_map/fields/pallas_call | solution.py:245
  17.9 0.0 collective-permute-done.4.rest_1_
  17.9 0.0 collective-permute-done.5.rest_2_
  17.9 0.2 collective-permute-done.6.rest_3_
  18.1 0.0 collective-permute-start.8
  18.1 0.4 %down.1 = f32[8,16,256]{2,1,0:T(8,128)S(1)} custom-call(bf16[16,64,128]{2,1,0:T(8,128)(2,1)S(1)} %get-tuple-element.33.to_field, bf16[8,64,256]{2,1,0:T(8,128)(2,1)S(1)} %get-tuple-element.34.to_points, f32[8,16,256]{2,1,0:T(8,128)S(1)} %get-tuple-element.42.keep, bf16[4,16,128]{2,1,0:T(8,128)(2,1)S(1)} %constant_dynamic-update-slice_fusion.2.rest_0_, ...), custom_call_target="tpu_custom_call" | custom-call | flops 1000000000 | bytes 1000000 | tf_op jit(solution)/shard_map/down/pallas_call | solution.py:304
  18.5 0.9 %collective-permute-done.8 = bf16[8,16,256]{2,1,0:T(8,128)(2,1)S(1)} collective-permute-done((bf16[8,16,256]{2,1,0:T(8,128)(2,1)S(1)}, bf16[8,16,256]{2,1,0:T(8,128)(2,1)S(1)}, u32[]{:S(2)}, u32[]{:S(2)}) %collective-permute-start.8) | collective-permute-done | bytes 65568 | tf_op jit(solution)/shard_map/ppermute | solution.py:303
  19.3 0.6 %fusion = bf16[8,256,16]{1,2,0:T(8,128)(2,1)} fusion(f32[8,16,256]{2,1,0:T(8,128)S(1)} %down.1, bf16[8,16,256]{2,1,0:T(8,128)(2,1)S(1)} %collective-permute-done.8), kind=kLoop, calls=%fused_computation.2 | loop fusion | flops 98304 | bytes 262144 | tf_op jit(solution)/shard_map/transpose | solution.py:316
  (5 shorter events, 0.1 us)
Async XLA Ops:
  1.4 6.2 %collective-permute-start = (bf16[1,16,128]{2,1,0:T(8,128)(2,1)S(1)}, bf16[1,16,128]{2,1,0:T(8,128)(2,1)S(1)}, u32[]{:S(2)}, u32[]{:S(2)}) collective-permute-start(bf16[1,16,128]{2,1,0:T(8,128)(2,1)S(1)} %bitcast.11), channel_id=1, source_target_pairs={{0,8},{2,10},{4,12},{6,14},{8,0},{10,2},{12,4},{14,6},{16,24},{18,... | collective-permute-start | bytes 12296 | tf_op jit(solution)/shard_map/ppermute | solution.py:289
  4.4 5.8 %copy-start.2 = (bf16[8,256,64]{1,2,0:T(8,128)(2,1)S(1)}, bf16[8,256,64]{1,2,0:T(8,128)(2,1)}, u32[]{:S(2)}) copy-start(bf16[8,256,64]{1,2,0:T(8,128)(2,1)} %param.21) | copy-start | bytes 786436
  4.4 5.8 %copy-start.5 = (bf16[14,4,64,64]{3,2,1,0:T(8,128)(2,1)S(1)}, bf16[14,4,64,64]{3,2,1,0:T(8,128)(2,1)}, u32[]{:S(2)}) copy-start(bf16[14,4,64,64]{3,2,1,0:T(8,128)(2,1)} %upper_coup.1) | copy-start | bytes 1376260
  4.4 5.8 %copy-start.6 = (bf16[12,64,64]{2,1,0:T(8,128)(2,1)S(1)}, bf16[12,64,64]{2,1,0:T(8,128)(2,1)}, u32[]{:S(2)}) copy-start(bf16[12,64,64]{2,1,0:T(8,128)(2,1)} %upper_up.1) | copy-start | bytes 294916
  4.4 5.8 %copy-start.7 = (bf16[12,64,64]{2,1,0:T(8,128)(2,1)S(1)}, bf16[12,64,64]{2,1,0:T(8,128)(2,1)}, u32[]{:S(2)}) copy-start(bf16[12,64,64]{2,1,0:T(8,128)(2,1)} %upper_down.1) | copy-start | bytes 294916
  4.4 5.8 %copy-start.8 = (bf16[8,64,64]{2,1,0:T(8,128)(2,1)S(1)}, bf16[8,64,64]{2,1,0:T(8,128)(2,1)}, u32[]{:S(2)}) copy-start(bf16[8,64,64]{2,1,0:T(8,128)(2,1)} %leaf_down.1) | copy-start | bytes 196612
  4.5 5.8 %copy-start.9 = (bf16[1,4,64,64]{3,2,1,0:T(8,128)(2,1)S(1)}, bf16[1,4,64,64]{3,2,1,0:T(8,128)(2,1)}, u32[]{:S(2)}) copy-start(bf16[1,4,64,64]{3,2,1,0:T(8,128)(2,1)} %node_coup.1) | copy-start | bytes 98308
  4.5 5.8 %copy-start.10 = (bf16[1,64,64]{2,1,0:T(8,128)(2,1)S(1)}, bf16[1,64,64]{2,1,0:T(8,128)(2,1)}, u32[]{:S(2)}) copy-start(bf16[1,64,64]{2,1,0:T(8,128)(2,1)} %node_down.1) | copy-start | bytes 24580
  4.5 5.8 %copy-start.11 = (s32[14,4]{0,1:T(4,128)S(1)}, s32[14,4]{0,1:T(4,128)}, u32[]{:S(2)}) copy-start(s32[14,4]{0,1:T(4,128)} %param.31) | copy-start | bytes 676
  4.5 5.8 %copy-start.12 = (s32[1,4]{1,0:T(1,128)S(1)}, s32[1,4]{1,0:T(1,128)}, u32[]{:S(2)}) copy-start(s32[1,4]{1,0:T(1,128)} %node_list.1) | copy-start | bytes 52
  4.6 7.7 %collective-permute-start.2 = (bf16[20,16,128]{2,1,0:T(8,128)(2,1)S(1)}, bf16[20,16,128]{2,1,0:T(8,128)(2,1)S(1)}, u32[]{:S(2)}, u32[]{:S(2)}) collective-permute-start(bf16[20,16,128]{2,1,0:T(8,128)(2,1)S(1)} %pack.1.own), channel_id=1, source_target_pairs={{2,4},{3,5},{4,2},{5,3},{6,8},{7,9},{8,6},{9,7},{10,12},{11,13},{1... | collective-permute-start | bytes 245768 | tf_op jit(solution)/shard_map/ppermute | solution.py:239
  4.6 7.7 %collective-permute-start.3 = (bf16[20,16,128]{2,1,0:T(8,128)(2,1)S(1)}, bf16[20,16,128]{2,1,0:T(8,128)(2,1)S(1)}, u32[]{:S(2)}, u32[]{:S(2)}) collective-permute-start(bf16[20,16,128]{2,1,0:T(8,128)(2,1)S(1)} %pack.1.own), channel_id=1, source_target_pairs={{0,2},{2,0},{4,6},{6,4},{8,10},{10,8},{12,14},{14,12},{16,18},{18,... | collective-permute-start | bytes 245768 | tf_op jit(solution)/shard_map/ppermute | solution.py:240
  7.6 4.7 %collective-permute-start.1 = (bf16[2,16,128]{2,1,0:T(8,128)(2,1)S(1)}, bf16[2,16,128]{2,1,0:T(8,128)(2,1)S(1)}, u32[]{:S(2)}, u32[]{:S(2)}) collective-permute-start(bf16[2,16,128]{2,1,0:T(8,128)(2,1)S(1)} %constant_dynamic-update-slice_fusion), channel_id=1, source_target_pairs={{0,16},{2,18},{4,20},{6,22},{8,24},{10,26},{12,28},{14,30},{16,0},... | collective-permute-start | bytes 24584 | tf_op jit(solution)/shard_map/ppermute | solution.py:289
  10.3 5.7 %copy-start = (bf16[8,3,256,256]{3,2,1,0:T(8,128)(2,1)S(1)}, bf16[8,3,256,256]{3,2,1,0:T(8,128)(2,1)}, u32[]{:S(2)}) copy-start(bf16[8,3,256,256]{3,2,1,0:T(8,128)(2,1)} %near.1) | copy-start | bytes 9437188
  10.3 5.7 %copy-start.1 = (bf16[8,3,64,64]{3,2,1,0:T(8,128)(2,1)S(1)}, bf16[8,3,64,64]{3,2,1,0:T(8,128)(2,1)}, u32[]{:S(2)}) copy-start(bf16[8,3,64,64]{3,2,1,0:T(8,128)(2,1)} %coup.1) | copy-start | bytes 589828
  10.3 5.7 %copy-start.3 = (s32[8,3]{0,1:T(4,128)S(1)}, s32[8,3]{0,1:T(4,128)}, u32[]{:S(2)}) copy-start(s32[8,3]{0,1:T(4,128)} %param.19) | copy-start | bytes 292
  10.3 5.7 %copy-start.4 = (s32[8,3]{0,1:T(4,128)S(1)}, s32[8,3]{0,1:T(4,128)}, u32[]{:S(2)}) copy-start(s32[8,3]{0,1:T(4,128)} %param.23) | copy-start | bytes 292
  12.3 3.7 %collective-permute-start.7 = (bf16[60,16,128]{2,1,0:T(8,128)(2,1)S(1)}, bf16[60,16,128]{2,1,0:T(8,128)(2,1)S(1)}, u32[]{:S(2)}, u32[]{:S(2)}) collective-permute-start(bf16[60,16,128]{2,1,0:T(8,128)(2,1)S(1)} %pad_maximum_fusion), channel_id=1, source_target_pairs={{0,1},{1,0},{2,3},{3,2},{4,5},{5,4},{6,7},{7,6},{8,9},{9,8},{10,11... | collective-permute-start | bytes 737288 | tf_op jit(solution)/shard_map/ppermute | solution.py:297
  12.4 5.5 %collective-permute-start.4 = (bf16[4,16,128]{2,1,0:T(8,128)(2,1)S(1)}, bf16[4,16,128]{2,1,0:T(8,128)(2,1)S(1)}, u32[]{:S(2)}, u32[]{:S(2)}) collective-permute-start(bf16[4,16,128]{2,1,0:T(8,128)(2,1)S(1)} %constant_dynamic-update-slice_fusion.2.rest_0_), channel_id=1, source_target_pairs={{0,6},{2,4},{4,2},{6,0},{8,14},{10,12},{12,10},{14,8},{16,22},{18,... | collective-permute-start | bytes 49160 | tf_op jit(solution)/shard_map/ppermute | solution.py:299
  13.9 4.0 %collective-permute-start.5 = (bf16[4,16,128]{2,1,0:T(8,128)(2,1)S(1)}, bf16[4,16,128]{2,1,0:T(8,128)(2,1)S(1)}, u32[]{:S(2)}, u32[]{:S(2)}) collective-permute-start(bf16[4,16,128]{2,1,0:T(8,128)(2,1)S(1)} %constant_dynamic-update-slice_fusion.2.rest_0_), channel_id=1, source_target_pairs={{0,2},{2,0},{4,6},{6,4},{8,10},{10,8},{12,14},{14,12},{16,18},{18,... | collective-permute-start | bytes 49160 | tf_op jit(solution)/shard_map/ppermute | solution.py:299
  14.3 3.7 %collective-permute-start.6 = (bf16[4,16,128]{2,1,0:T(8,128)(2,1)S(1)}, bf16[4,16,128]{2,1,0:T(8,128)(2,1)S(1)}, u32[]{:S(2)}, u32[]{:S(2)}) collective-permute-start(bf16[4,16,128]{2,1,0:T(8,128)(2,1)S(1)} %constant_dynamic-update-slice_fusion.2.rest_0_), channel_id=1, source_target_pairs={{0,4},{2,6},{4,0},{6,2},{8,12},{10,14},{12,8},{14,10},{16,20},{18,... | collective-permute-start | bytes 49160 | tf_op jit(solution)/shard_map/ppermute | solution.py:299
  18.1 1.3 %collective-permute-start.8 = (bf16[8,16,256]{2,1,0:T(8,128)(2,1)S(1)}, bf16[8,16,256]{2,1,0:T(8,128)(2,1)S(1)}, u32[]{:S(2)}, u32[]{:S(2)}) collective-permute-start(bf16[8,16,256]{2,1,0:T(8,128)(2,1)S(1)} %get-tuple-element.46), channel_id=1, source_target_pairs={{0,1},{1,0},{2,3},{3,2},{4,5},{5,4},{6,7},{7,6},{8,9},{9,8},{10,11... | collective-permute-start | bytes 196616 | tf_op jit(solution)/shard_map/ppermute | solution.py:303

commit v11 on v10

--- a/solution.py
+++ b/solution.py
@@ -127,10 +127,10 @@
 
 
 def weights_kernel(
-    node_list, upper_list, node_coup, node_down, upper_coup, upper_up, upper_down, leaf_down, row,
+    node_list, upper_list, node_coup, upper_coup, upper_up, upper_down, leaf_down, row,
     to_field, to_points, named, *tree,
 ):
-    nodes, rank = to_field.shape[0], to_field.shape[1]
+    nodes, rank = to_field.shape[0], row.shape[1]
     farc = node_coup.shape[1]
     levels = nodes.bit_length() - 1
     me = lax.axis_index("leaf")
@@ -152,23 +152,30 @@
             for parent in range(breadth // 2):
                 above = tree[height - 2][parent].astype(jnp.bfloat16)
                 above = mm(upper_down[node - 4], above, PLAIN).astype(jnp.bfloat16)
-                for m in (2 * parent, 2 * parent + 1):
-                    level[m] = level[m] + mm(above, upper_up[breadth + m - 4], LAST)
+                first = breadth + 2 * parent - 4
+                pair = mm(above, upper_up[first : first + 2].reshape(2 * rank, rank), LAST)
+                for side in range(2):
+                    m = 2 * parent + side
+                    level[m] = level[m] + pair[:, side * rank : (side + 1) * rank]
+    blank = jnp.zeros((rank, rank), jnp.bfloat16)
+    for place in range(nodes):
+        block = jnp.concatenate([named[place].astype(jnp.bfloat16), blank], axis=1)
+        to_field[place, :rank] = block
     for parent in range(nodes // 2):
-        lifted = mm(node_down[0], tree[levels - 2][parent].astype(jnp.bfloat16), PLAIN)
-        lifted = lifted.astype(jnp.bfloat16)
+        composed = tree[levels - 2][parent].astype(jnp.bfloat16)
+        composed = jnp.concatenate([blank, composed], axis=1)
         for n in (2 * parent, 2 * parent + 1):
-            to_field[place_of(n ^ me, nodes), :, rank:] = lifted
-    for place in range(nodes):
-        to_field[place, :, :rank] = named[place].astype(jnp.bfloat16)
-
-
-def down_kernel(to_field, to_points, keep, *rest):
+            to_field[place_of(n ^ me, nodes), rank:] = composed
+
+
+def down_kernel(to_field, to_points, node_down, keep, *rest):
     *gathered, out = rest
     messages = [part[p] for part in gathered for p in range(part.shape[0])]
     matrices = [to_field[p] for p in range(to_field.shape[0])]
-    field = mm(jnp.concatenate(messages, axis=1), jnp.concatenate(matrices, axis=1), LAST)
-    field = field.astype(jnp.bfloat16)
+    fields = mm(jnp.concatenate(messages, axis=1), jnp.concatenate(matrices, axis=1), LAST)
+    rank = node_down.shape[-1]
+    parent = fields[:, rank:].astype(jnp.bfloat16)
+    field = (fields[:, :rank] + mm(parent, node_down[0], LAST)).astype(jnp.bfloat16)
     for t in range(out.shape[0]):
         out[t] = keep[t] + mm(field, to_points[t], PLAIN)
 
@@ -266,10 +273,10 @@
     weights = pl.pallas_call(
         weights_kernel,
         out_shape=(
-            pltpu.VMEM((nodes, rank, 2 * rank), bf16),
+            pltpu.VMEM((nodes, 2 * rank, 2 * rank), bf16),
             pltpu.VMEM((leaves, rank, points), bf16),
         ),
-        in_specs=[smem()] * 2 + [vmem()] * 7,
+        in_specs=[smem()] * 2 + [vmem()] * 6,
         out_specs=(vmem(),) * 2,
         scratch_shapes=[pltpu.VMEM((nodes, rank, rank), f32)]
         + [pltpu.VMEM((2**height, rank, rank), f32) for height in range(1, levels)],
@@ -279,7 +286,7 @@
         ),
         name="weights",
     )(
-        node_list, upper_list.T, node_coupling, node_down, upper_coupling, upper_up, upper_down,
+        node_list, upper_list.T, node_coupling, upper_coupling, upper_up, upper_down,
         leaf_down, row,
     )
 
@@ -304,14 +311,14 @@
     part = pl.pallas_call(
         down_kernel,
         out_shape=pltpu.VMEM((leaves, columns, points), f32),
-        in_specs=[vmem()] * 7,
+        in_specs=[vmem()] * 8,
         out_specs=vmem(),
         compiler_params=limit(8),
         cost_estimate=pl.CostEstimate(
             flops=1_000_000_000, bytes_accessed=1_000_000, transcendentals=0
         ),
         name="down",
-    )(*weights, keep, known, *others)
+    )(*weights, node_down, keep, known, *others)
     out = (part + received.astype(f32)).astype(bf16)
     return jnp.swapaxes(out, 1, 2)
 

time: 20.2 us -> 20.1 us (level)
    pallas_call x1, Pallas kernels: 1.88 us -> 1.57 us  [body(): pl.pallas_call(weights_kernel, out_shape=(pltpu.VMEM((nodes, 2 * rank, 2...]
    ppermute x2, waiting for transfers between devices: 0.01 us -> 0.28 us  [body(): other = lax.ppermute(known, 'leaf', [(i, i ^ step) for i in range(nodes)])]
    ppermute x1, waiting for transfers between devices: 0.86 us -> 0.61 us  [body(): received = lax.ppermute(send, 'sub', swap)]
    pallas_call x1, Pallas kernels: 0.38 us -> 0.63 us  [body(): pl.pallas_call(down_kernel, out_shape=pltpu.VMEM((leaves, columns, points...]
  transfers between devices with their start and end apart: 9 -> 9, of which waited for: 2 -> 3; matrix products, arithmetic and copies ran while one was open for 0% -> 0% of each run, Pallas kernels for 21% -> 21%
where the time goes in v11:
time: 20.1 us; the launch traced here: 19.9 us
  starting transfers between devices  12.3 us (61%)
  Pallas kernels  5.55 us (28%)
  waiting for transfers between devices  1.04 us (5%)
  other arithmetic  0.67 us (3%)
    ppermute x2, starting transfers between devices, body(): other = lax.ppermute(known, 'leaf', [(i, i ^ step) for i in range(nodes)])  5.69 us
    ppermute x3, starting transfers between devices, body(): lax.ppermute(known, 'leaf', [(i, i ^ step) for i in range(nodes)])  3.55 us
    ppermute x1, starting transfers between devices, body(): pair = lax.ppermute(pack, 'leaf', [(i, i ^ 1) for i in range(nodes)])  2.97 us
    pallas_call x1, Pallas kernels, fields(): pl.pallas_call(field_kernel, out_shape=(pltpu.VMEM((leaves, columns, poin...  1.88 us
    pallas_call x1, Pallas kernels, body(): pl.pallas_call(weights_kernel, out_shape=(pltpu.VMEM((nodes, 2 * rank, 2...  1.57 us
    pallas_call x1, Pallas kernels, body(): pl.pallas_call(up_kernel, out_shape=(pltpu.VMEM((leaves, columns, rank),...  1.4 us
    transpose x1, other arithmetic, body(): return jnp.swapaxes(out, 1, 2)  0.65 us
    pallas_call x1, Pallas kernels, body(): pl.pallas_call(down_kernel, out_shape=pltpu.VMEM((leaves, columns, points...  0.63 us
  transfers between devices with their start and end apart: 9, of which 3 were waited for; matrix products, arithmetic and copies ran while one was open for 0% of the time, Pallas kernels for 21%

profile of v11, /device:TPU:0, one launch (start us, length us, event | category | flops | bytes accessed | tf_op | source)
XLA Modules:
  0.0 19.9 jit_solution(11921744626265892507)
XLA Ops:
  0.0 1.4 %up.1 = (bf16[8,16,64]{2,1,0:T(8,128)(2,1)S(1)}, bf16[16,128]{1,0:T(8,128)(2,1)S(1)}, bf16[8,16,256]{2,1,0:T(8,128)(2,1)S(1)}) custom-call(bf16[8,16,256]{2,1,0:T(8,128)(2,1)} %bitcast.17, bf16[8,64,256]{2,1,0:T(8,128)(2,1)} %bitcast.16, bf16[8,64,64]{2,1,0:T(8,128)(2,1)} %leaf_up.1, bf16[1,64,64]{2,1,0:T(8,128)(2,1)} %node_up.1), custom_call_target="tpu_custom_call" | custom-call | flops 2000000000 | bytes 5000000 | tf_op jit(solution)/shard_map/up/pallas_call | solution.py:211
  1.4 3.0 %collective-permute-start = (bf16[1,16,128]{2,1,0:T(8,128)(2,1)S(1)}, bf16[1,16,128]{2,1,0:T(8,128)(2,1)S(1)}, u32[]{:S(2)}, u32[]{:S(2)}) collective-permute-start(bf16[1,16,128]{2,1,0:T(8,128)(2,1)S(1)} %bitcast.11), channel_id=1, source_target_pairs={{0,8},{2,10},{4,12},{6,14},{8,0},{10,2},{12,4},{14,6},{16,24},{18,... | collective-permute-start | bytes 12296 | tf_op jit(solution)/shard_map/ppermute | solution.py:296
  4.4 0.0 copy-start.2
  4.4 0.0 copy-start.5
  4.4 0.0 copy-start.6
  4.4 0.0 copy-start.7
  4.4 0.0 copy-start.8
  4.5 0.0 copy-start.9
  4.5 0.0 copy-start.11
  4.5 0.0 copy-start.12
  4.5 0.1 pack.1.own
  4.6 0.0 collective-permute-start.2
  4.6 3.0 %collective-permute-start.3 = (bf16[20,16,128]{2,1,0:T(8,128)(2,1)S(1)}, bf16[20,16,128]{2,1,0:T(8,128)(2,1)S(1)}, u32[]{:S(2)}, u32[]{:S(2)}) collective-permute-start(bf16[20,16,128]{2,1,0:T(8,128)(2,1)S(1)} %pack.1.own), channel_id=1, source_target_pairs={{0,2},{2,0},{4,6},{6,4},{8,10},{10,8},{12,14},{14,12},{16,18},{18,... | collective-permute-start | bytes 245768 | tf_op jit(solution)/shard_map/ppermute | solution.py:247
  7.6 0.0 collective-permute-done
  7.6 2.7 %collective-permute-start.1 = (bf16[2,16,128]{2,1,0:T(8,128)(2,1)S(1)}, bf16[2,16,128]{2,1,0:T(8,128)(2,1)S(1)}, u32[]{:S(2)}, u32[]{:S(2)}) collective-permute-start(bf16[2,16,128]{2,1,0:T(8,128)(2,1)S(1)} %constant_dynamic-update-slice_fusion), channel_id=1, source_target_pairs={{0,16},{2,18},{4,20},{6,22},{8,24},{10,26},{12,28},{14,30},{16,0},... | collective-permute-start | bytes 24584 | tf_op jit(solution)/shard_map/ppermute | solution.py:296
  10.2 0.0 copy-done.2
  10.2 0.0 copy-done.5
  10.2 0.0 copy-done.6
  10.2 0.0 copy-done.7
  10.3 0.0 copy-done.8
  10.3 0.0 copy-done.9
  10.3 0.0 copy-done.11
  10.3 0.0 copy-done.12
  10.3 0.0 copy-start
  10.3 0.0 copy-start.1
  10.3 0.0 copy-start.3
  10.3 0.0 copy-start.4
  10.3 1.6 %weights.1 = (bf16[16,128,128]{2,1,0:T(8,128)(2,1)S(1)}, bf16[8,64,256]{2,1,0:T(8,128)(2,1)S(1)}) custom-call(s32[1,4]{1,0:T(1,128)S(1)} %copy-done.12, s32[4,14]{1,0:T(4,128)S(1)} %bitcast.15, bf16[1,4,64,64]{3,2,1,0:T(8,128)(2,1)S(1)} %copy-done.9, bf16[14,4,64,64]{3,2,1,0:T(8,128)(2,1)S(1)} %copy-done.5, bf16[12,64,64]{2,1,0:T(8,128)(2,1)S(1)} %copy-done.6, ...), custom_call_target="tpu_custom_call" | custom-call | flops 2000000000 | bytes 3000000 | tf_op jit(solution)/shard_map/weights/pallas_call | solution.py:273
  11.9 0.0 copy-start.10
  11.9 0.3 %collective-permute-done.1 = bf16[2,16,128]{2,1,0:T(8,128)(2,1)S(1)} collective-permute-done((bf16[2,16,128]{2,1,0:T(8,128)(2,1)S(1)}, bf16[2,16,128]{2,1,0:T(8,128)(2,1)S(1)}, u32[]{:S(2)}, u32[]{:S(2)}) %collective-permute-start.1) | collective-permute-done | bytes 8224 | tf_op jit(solution)/shard_map/ppermute | solution.py:296
  12.2 0.0 collective-permute-done.2.cross
  12.2 0.0 collective-permute-done.3.pair
  12.2 0.1 collective-permute-start.7
  12.3 1.5 %collective-permute-start.4 = (bf16[4,16,128]{2,1,0:T(8,128)(2,1)S(1)}, bf16[4,16,128]{2,1,0:T(8,128)(2,1)S(1)}, u32[]{:S(2)}, u32[]{:S(2)}) collective-permute-start(bf16[4,16,128]{2,1,0:T(8,128)(2,1)S(1)} %constant_dynamic-update-slice_fusion.2.rest_0_), channel_id=1, source_target_pairs={{0,6},{2,4},{4,2},{6,0},{8,14},{10,12},{12,10},{14,8},{16,22},{18,... | collective-permute-start | bytes 49160 | tf_op jit(solution)/shard_map/ppermute | solution.py:306
  13.8 0.4 %collective-permute-start.5 = (bf16[4,16,128]{2,1,0:T(8,128)(2,1)S(1)}, bf16[4,16,128]{2,1,0:T(8,128)(2,1)S(1)}, u32[]{:S(2)}, u32[]{:S(2)}) collective-permute-start(bf16[4,16,128]{2,1,0:T(8,128)(2,1)S(1)} %constant_dynamic-update-slice_fusion.2.rest_0_), channel_id=1, source_target_pairs={{0,2},{2,0},{4,6},{6,4},{8,10},{10,8},{12,14},{14,12},{16,18},{18,... | collective-permute-start | bytes 49160 | tf_op jit(solution)/shard_map/ppermute | solution.py:306
  14.2 1.7 %collective-permute-start.6 = (bf16[4,16,128]{2,1,0:T(8,128)(2,1)S(1)}, bf16[4,16,128]{2,1,0:T(8,128)(2,1)S(1)}, u32[]{:S(2)}, u32[]{:S(2)}) collective-permute-start(bf16[4,16,128]{2,1,0:T(8,128)(2,1)S(1)} %constant_dynamic-update-slice_fusion.2.rest_0_), channel_id=1, source_target_pairs={{0,4},{2,6},{4,0},{6,2},{8,12},{10,14},{12,8},{14,10},{16,20},{18,... | collective-permute-start | bytes 49160 | tf_op jit(solution)/shard_map/ppermute | solution.py:306
  15.9 0.0 collective-permute-done.7.all_other
  15.9 0.0 copy-done
  15.9 0.0 copy-done.1
  15.9 0.0 copy-done.3
  15.9 0.0 copy-done.4
  15.9 1.9 %fields.1 = (f32[8,16,256]{2,1,0:T(8,128)S(1)}, bf16[8,16,256]{2,1,0:T(8,128)(2,1)S(1)}) custom-call(s32[3,8]{1,0:T(4,128)S(1)} %bitcast.13, s32[3,8]{1,0:T(4,128)S(1)} %bitcast.14, bf16[20,16,128]{2,1,0:T(8,128)(2,1)S(1)} %collective-permute-done.3.pair, bf16[20,16,128]{2,1,0:T(8,128)(2,1)S(1)} %pack.1.own, ...), custom_call_target="tpu_custom_call" | custom-call | flops 805306368 | bytes 3145728 | tf_op jit(solution)/shard_map/fields/pallas_call | solution.py:252
  17.8 0.0 collective-permute-done.4.rest_1_
  17.8 0.0 collective-permute-done.5.rest_2_
  17.8 0.1 collective-permute-done.6.rest_3_
  18.0 0.0 collective-permute-start.8
  18.0 0.0 copy-done.10
  18.0 0.6 %down.1 = f32[8,16,256]{2,1,0:T(8,128)S(1)} custom-call(bf16[16,128,128]{2,1,0:T(8,128)(2,1)S(1)} %get-tuple-element.33.to_field, bf16[8,64,256]{2,1,0:T(8,128)(2,1)S(1)} %get-tuple-element.34.to_points, bf16[1,64,64]{2,1,0:T(8,128)(2,1)S(1)} %copy-done.10, f32[8,16,256]{2,1,0:T(8,128)S(1)} %get-tuple-element.42.keep, ...), custom_call_target="tpu_custom_call" | custom-call | flops 1000000000 | bytes 1000000 | tf_op jit(solution)/shard_map/down/pallas_call | solution.py:311
  18.6 0.6 %collective-permute-done.8 = bf16[8,16,256]{2,1,0:T(8,128)(2,1)S(1)} collective-permute-done((bf16[8,16,256]{2,1,0:T(8,128)(2,1)S(1)}, bf16[8,16,256]{2,1,0:T(8,128)(2,1)S(1)}, u32[]{:S(2)}, u32[]{:S(2)}) %collective-permute-start.8) | collective-permute-done | bytes 65568 | tf_op jit(solution)/shard_map/ppermute | solution.py:310
  19.2 0.6 %fusion = bf16[8,256,16]{1,2,0:T(8,128)(2,1)} fusion(f32[8,16,256]{2,1,0:T(8,128)S(1)} %down.1, bf16[8,16,256]{2,1,0:T(8,128)(2,1)S(1)} %collective-permute-done.8), kind=kLoop, calls=%fused_computation.2 | loop fusion | flops 98304 | bytes 262144 | tf_op jit(solution)/shard_map/transpose | solution.py:323
  (5 shorter events, 0.0 us)
Async XLA Ops:
  1.4 6.2 %collective-permute-start = (bf16[1,16,128]{2,1,0:T(8,128)(2,1)S(1)}, bf16[1,16,128]{2,1,0:T(8,128)(2,1)S(1)}, u32[]{:S(2)}, u32[]{:S(2)}) collective-permute-start(bf16[1,16,128]{2,1,0:T(8,128)(2,1)S(1)} %bitcast.11), channel_id=1, source_target_pairs={{0,8},{2,10},{4,12},{6,14},{8,0},{10,2},{12,4},{14,6},{16,24},{18,... | collective-permute-start | bytes 12296 | tf_op jit(solution)/shard_map/ppermute | solution.py:296
  4.4 5.8 %copy-start.2 = (bf16[8,256,64]{1,2,0:T(8,128)(2,1)S(1)}, bf16[8,256,64]{1,2,0:T(8,128)(2,1)}, u32[]{:S(2)}) copy-start(bf16[8,256,64]{1,2,0:T(8,128)(2,1)} %param.21) | copy-start | bytes 786436
  4.4 5.8 %copy-start.5 = (bf16[14,4,64,64]{3,2,1,0:T(8,128)(2,1)S(1)}, bf16[14,4,64,64]{3,2,1,0:T(8,128)(2,1)}, u32[]{:S(2)}) copy-start(bf16[14,4,64,64]{3,2,1,0:T(8,128)(2,1)} %upper_coup.1) | copy-start | bytes 1376260
  4.4 5.8 %copy-start.6 = (bf16[12,64,64]{2,1,0:T(8,128)(2,1)S(1)}, bf16[12,64,64]{2,1,0:T(8,128)(2,1)}, u32[]{:S(2)}) copy-start(bf16[12,64,64]{2,1,0:T(8,128)(2,1)} %upper_up.1) | copy-start | bytes 294916
  4.4 5.8 %copy-start.7 = (bf16[12,64,64]{2,1,0:T(8,128)(2,1)S(1)}, bf16[12,64,64]{2,1,0:T(8,128)(2,1)}, u32[]{:S(2)}) copy-start(bf16[12,64,64]{2,1,0:T(8,128)(2,1)} %upper_down.1) | copy-start | bytes 294916
  4.4 5.8 %copy-start.8 = (bf16[8,64,64]{2,1,0:T(8,128)(2,1)S(1)}, bf16[8,64,64]{2,1,0:T(8,128)(2,1)}, u32[]{:S(2)}) copy-start(bf16[8,64,64]{2,1,0:T(8,128)(2,1)} %leaf_down.1) | copy-start | bytes 196612
  4.5 5.8 %copy-start.9 = (bf16[1,4,64,64]{3,2,1,0:T(8,128)(2,1)S(1)}, bf16[1,4,64,64]{3,2,1,0:T(8,128)(2,1)}, u32[]{:S(2)}) copy-start(bf16[1,4,64,64]{3,2,1,0:T(8,128)(2,1)} %node_coup.1) | copy-start | bytes 98308
  4.5 5.8 %copy-start.11 = (s32[14,4]{0,1:T(4,128)S(1)}, s32[14,4]{0,1:T(4,128)}, u32[]{:S(2)}) copy-start(s32[14,4]{0,1:T(4,128)} %param.31) | copy-start | bytes 676
  4.5 5.8 %copy-start.12 = (s32[1,4]{1,0:T(1,128)S(1)}, s32[1,4]{1,0:T(1,128)}, u32[]{:S(2)}) copy-start(s32[1,4]{1,0:T(1,128)} %node_list.1) | copy-start | bytes 52
  4.6 7.6 %collective-permute-start.2 = (bf16[20,16,128]{2,1,0:T(8,128)(2,1)S(1)}, bf16[20,16,128]{2,1,0:T(8,128)(2,1)S(1)}, u32[]{:S(2)}, u32[]{:S(2)}) collective-permute-start(bf16[20,16,128]{2,1,0:T(8,128)(2,1)S(1)} %pack.1.own), channel_id=1, source_target_pairs={{2,4},{3,5},{4,2},{5,3},{6,8},{7,9},{8,6},{9,7},{10,12},{11,13},{1... | collective-permute-start | bytes 245768 | tf_op jit(solution)/shard_map/ppermute | solution.py:246
  4.6 7.6 %collective-permute-start.3 = (bf16[20,16,128]{2,1,0:T(8,128)(2,1)S(1)}, bf16[20,16,128]{2,1,0:T(8,128)(2,1)S(1)}, u32[]{:S(2)}, u32[]{:S(2)}) collective-permute-start(bf16[20,16,128]{2,1,0:T(8,128)(2,1)S(1)} %pack.1.own), channel_id=1, source_target_pairs={{0,2},{2,0},{4,6},{6,4},{8,10},{10,8},{12,14},{14,12},{16,18},{18,... | collective-permute-start | bytes 245768 | tf_op jit(solution)/shard_map/ppermute | solution.py:247
  7.6 4.6 %collective-permute-start.1 = (bf16[2,16,128]{2,1,0:T(8,128)(2,1)S(1)}, bf16[2,16,128]{2,1,0:T(8,128)(2,1)S(1)}, u32[]{:S(2)}, u32[]{:S(2)}) collective-permute-start(bf16[2,16,128]{2,1,0:T(8,128)(2,1)S(1)} %constant_dynamic-update-slice_fusion), channel_id=1, source_target_pairs={{0,16},{2,18},{4,20},{6,22},{8,24},{10,26},{12,28},{14,30},{16,0},... | collective-permute-start | bytes 24584 | tf_op jit(solution)/shard_map/ppermute | solution.py:296
  10.3 5.6 %copy-start = (bf16[8,3,256,256]{3,2,1,0:T(8,128)(2,1)S(1)}, bf16[8,3,256,256]{3,2,1,0:T(8,128)(2,1)}, u32[]{:S(2)}) copy-start(bf16[8,3,256,256]{3,2,1,0:T(8,128)(2,1)} %near.1) | copy-start | bytes 9437188
  10.3 5.6 %copy-start.1 = (bf16[8,3,64,64]{3,2,1,0:T(8,128)(2,1)S(1)}, bf16[8,3,64,64]{3,2,1,0:T(8,128)(2,1)}, u32[]{:S(2)}) copy-start(bf16[8,3,64,64]{3,2,1,0:T(8,128)(2,1)} %coup.1) | copy-start | bytes 589828
  10.3 5.6 %copy-start.3 = (s32[8,3]{0,1:T(4,128)S(1)}, s32[8,3]{0,1:T(4,128)}, u32[]{:S(2)}) copy-start(s32[8,3]{0,1:T(4,128)} %param.19) | copy-start | bytes 292
  10.3 5.6 %copy-start.4 = (s32[8,3]{0,1:T(4,128)S(1)}, s32[8,3]{0,1:T(4,128)}, u32[]{:S(2)}) copy-start(s32[8,3]{0,1:T(4,128)} %param.23) | copy-start | bytes 292
  11.9 6.1 %copy-start.10 = (bf16[1,64,64]{2,1,0:T(8,128)(2,1)S(1)}, bf16[1,64,64]{2,1,0:T(8,128)(2,1)}, u32[]{:S(2)}) copy-start(bf16[1,64,64]{2,1,0:T(8,128)(2,1)} %node_down.1) | copy-start | bytes 24580
  12.2 3.7 %collective-permute-start.7 = (bf16[60,16,128]{2,1,0:T(8,128)(2,1)S(1)}, bf16[60,16,128]{2,1,0:T(8,128)(2,1)S(1)}, u32[]{:S(2)}, u32[]{:S(2)}) collective-permute-start(bf16[60,16,128]{2,1,0:T(8,128)(2,1)S(1)} %pad_maximum_fusion), channel_id=1, source_target_pairs={{0,1},{1,0},{2,3},{3,2},{4,5},{5,4},{6,7},{7,6},{8,9},{9,8},{10,11... | collective-permute-start | bytes 737288 | tf_op jit(solution)/shard_map/ppermute | solution.py:304
  12.3 5.5 %collective-permute-start.4 = (bf16[4,16,128]{2,1,0:T(8,128)(2,1)S(1)}, bf16[4,16,128]{2,1,0:T(8,128)(2,1)S(1)}, u32[]{:S(2)}, u32[]{:S(2)}) collective-permute-start(bf16[4,16,128]{2,1,0:T(8,128)(2,1)S(1)} %constant_dynamic-update-slice_fusion.2.rest_0_), channel_id=1, source_target_pairs={{0,6},{2,4},{4,2},{6,0},{8,14},{10,12},{12,10},{14,8},{16,22},{18,... | collective-permute-start | bytes 49160 | tf_op jit(solution)/shard_map/ppermute | solution.py:306
  13.8 4.0 %collective-permute-start.5 = (bf16[4,16,128]{2,1,0:T(8,128)(2,1)S(1)}, bf16[4,16,128]{2,1,0:T(8,128)(2,1)S(1)}, u32[]{:S(2)}, u32[]{:S(2)}) collective-permute-start(bf16[4,16,128]{2,1,0:T(8,128)(2,1)S(1)} %constant_dynamic-update-slice_fusion.2.rest_0_), channel_id=1, source_target_pairs={{0,2},{2,0},{4,6},{6,4},{8,10},{10,8},{12,14},{14,12},{16,18},{18,... | collective-permute-start | bytes 49160 | tf_op jit(solution)/shard_map/ppermute | solution.py:306
  14.2 3.7 %collective-permute-start.6 = (bf16[4,16,128]{2,1,0:T(8,128)(2,1)S(1)}, bf16[4,16,128]{2,1,0:T(8,128)(2,1)S(1)}, u32[]{:S(2)}, u32[]{:S(2)}) collective-permute-start(bf16[4,16,128]{2,1,0:T(8,128)(2,1)S(1)} %constant_dynamic-update-slice_fusion.2.rest_0_), channel_id=1, source_target_pairs={{0,4},{2,6},{4,0},{6,2},{8,12},{10,14},{12,8},{14,10},{16,20},{18,... | collective-permute-start | bytes 49160 | tf_op jit(solution)/shard_map/ppermute | solution.py:306
  18.0 1.3 %collective-permute-start.8 = (bf16[8,16,256]{2,1,0:T(8,128)(2,1)S(1)}, bf16[8,16,256]{2,1,0:T(8,128)(2,1)S(1)}, u32[]{:S(2)}, u32[]{:S(2)}) collective-permute-start(bf16[8,16,256]{2,1,0:T(8,128)(2,1)S(1)} %get-tuple-element.46), channel_id=1, source_target_pairs={{0,1},{1,0},{2,3},{3,2},{4,5},{5,4},{6,7},{7,6},{8,9},{9,8},{10,11... | collective-permute-start | bytes 196616 | tf_op jit(solution)/shard_map/ppermute | solution.py:310

commit v12 on v11

--- a/solution.py
+++ b/solution.py
@@ -122,7 +122,7 @@
 
 
 def place_of(distance, nodes):
-    block = (4896 >> (4 * (distance & 3))) & 3
+    block = (8976 >> (4 * (distance & 3))) & 3
     return block * (nodes // 4) + (distance >> 2)
 
 
@@ -303,7 +303,7 @@
         known = jnp.concatenate([known, other], axis=0)
     all_other = lax.ppermute(jnp.concatenate([pair, cross, pack], axis=0), "sub", swap)
     others = [
-        lax.ppermute(known, "leaf", [(i, i ^ step) for i in range(nodes)]) for step in (3, 1, 2)
+        lax.ppermute(known, "leaf", [(i, i ^ step) for i in range(nodes)]) for step in (1, 3, 2)
     ]
     keep, send = fields(pair, pack, cross, all_other)
     others, keep, send = lax.optimization_barrier((others, keep, send))

time: 20.1 us -> 20.1 us (level)
  no operation moved by 1% of the time
where the time goes in v12:
time: 20.1 us; the launch traced here: 19.9 us
  starting transfers between devices  12.3 us (61%)
  Pallas kernels  5.55 us (28%)
  waiting for transfers between devices  1.04 us (5%)
  other arithmetic  0.67 us (3%)
    ppermute x2, starting transfers between devices, body(): other = lax.ppermute(known, 'leaf', [(i, i ^ step) for i in range(nodes)])  5.69 us
    ppermute x3, starting transfers between devices, body(): lax.ppermute(known, 'leaf', [(i, i ^ step) for i in range(nodes)])  3.55 us
    ppermute x1, starting transfers between devices, body(): pair = lax.ppermute(pack, 'leaf', [(i, i ^ 1) for i in range(nodes)])  2.97 us
    pallas_call x1, Pallas kernels, fields(): pl.pallas_call(field_kernel, out_shape=(pltpu.VMEM((leaves, columns, poin...  1.88 us
    pallas_call x1, Pallas kernels, body(): pl.pallas_call(weights_kernel, out_shape=(pltpu.VMEM((nodes, 2 * rank, 2...  1.57 us
    pallas_call x1, Pallas kernels, body(): pl.pallas_call(up_kernel, out_shape=(pltpu.VMEM((leaves, columns, rank),...  1.4 us
    transpose x1, other arithmetic, body(): return jnp.swapaxes(out, 1, 2)  0.65 us
    pallas_call x1, Pallas kernels, body(): pl.pallas_call(down_kernel, out_shape=pltpu.VMEM((leaves, columns, points...  0.63 us
  transfers between devices with their start and end apart: 9, of which 3 were waited for; matrix products, arithmetic and copies ran while one was open for 0% of the time, Pallas kernels for 21%

profile of v12, /device:TPU:0, one launch (start us, length us, event | category | flops | bytes accessed | tf_op | source)
XLA Modules:
  0.0 19.9 jit_solution(11791439096114474020)
XLA Ops:
  0.0 1.4 %up.1 = (bf16[8,16,64]{2,1,0:T(8,128)(2,1)S(1)}, bf16[16,128]{1,0:T(8,128)(2,1)S(1)}, bf16[8,16,256]{2,1,0:T(8,128)(2,1)S(1)}) custom-call(bf16[8,16,256]{2,1,0:T(8,128)(2,1)} %bitcast.17, bf16[8,64,256]{2,1,0:T(8,128)(2,1)} %bitcast.16, bf16[8,64,64]{2,1,0:T(8,128)(2,1)} %leaf_up.1, bf16[1,64,64]{2,1,0:T(8,128)(2,1)} %node_up.1), custom_call_target="tpu_custom_call" | custom-call | flops 2000000000 | bytes 5000000 | tf_op jit(solution)/shard_map/up/pallas_call | solution.py:211
  1.4 3.0 %collective-permute-start = (bf16[1,16,128]{2,1,0:T(8,128)(2,1)S(1)}, bf16[1,16,128]{2,1,0:T(8,128)(2,1)S(1)}, u32[]{:S(2)}, u32[]{:S(2)}) collective-permute-start(bf16[1,16,128]{2,1,0:T(8,128)(2,1)S(1)} %bitcast.11), channel_id=1, source_target_pairs={{0,8},{2,10},{4,12},{6,14},{8,0},{10,2},{12,4},{14,6},{16,24},{18,... | collective-permute-start | bytes 12296 | tf_op jit(solution)/shard_map/ppermute | solution.py:296
  4.4 0.0 copy-start.2
  4.4 0.0 copy-start.5
  4.4 0.0 copy-start.6
  4.4 0.0 copy-start.7
  4.4 0.0 copy-start.8
  4.5 0.0 copy-start.9
  4.5 0.0 copy-start.11
  4.5 0.0 copy-start.12
  4.5 0.1 pack.1.own
  4.6 0.0 collective-permute-start.2
  4.6 3.0 %collective-permute-start.3 = (bf16[20,16,128]{2,1,0:T(8,128)(2,1)S(1)}, bf16[20,16,128]{2,1,0:T(8,128)(2,1)S(1)}, u32[]{:S(2)}, u32[]{:S(2)}) collective-permute-start(bf16[20,16,128]{2,1,0:T(8,128)(2,1)S(1)} %pack.1.own), channel_id=1, source_target_pairs={{0,2},{2,0},{4,6},{6,4},{8,10},{10,8},{12,14},{14,12},{16,18},{18,... | collective-permute-start | bytes 245768 | tf_op jit(solution)/shard_map/ppermute | solution.py:247
  7.6 0.0 collective-permute-done
  7.6 2.7 %collective-permute-start.1 = (bf16[2,16,128]{2,1,0:T(8,128)(2,1)S(1)}, bf16[2,16,128]{2,1,0:T(8,128)(2,1)S(1)}, u32[]{:S(2)}, u32[]{:S(2)}) collective-permute-start(bf16[2,16,128]{2,1,0:T(8,128)(2,1)S(1)} %constant_dynamic-update-slice_fusion), channel_id=1, source_target_pairs={{0,16},{2,18},{4,20},{6,22},{8,24},{10,26},{12,28},{14,30},{16,0},... | collective-permute-start | bytes 24584 | tf_op jit(solution)/shard_map/ppermute | solution.py:296
  10.2 0.0 copy-done.2
  10.2 0.0 copy-done.5
  10.2 0.0 copy-done.6
  10.2 0.0 copy-done.7
  10.3 0.0 copy-done.8
  10.3 0.0 copy-done.9
  10.3 0.0 copy-done.11
  10.3 0.0 copy-done.12
  10.3 0.0 copy-start
  10.3 0.0 copy-start.1
  10.3 0.0 copy-start.3
  10.3 0.0 copy-start.4
  10.3 1.6 %weights.1 = (bf16[16,128,128]{2,1,0:T(8,128)(2,1)S(1)}, bf16[8,64,256]{2,1,0:T(8,128)(2,1)S(1)}) custom-call(s32[1,4]{1,0:T(1,128)S(1)} %copy-done.12, s32[4,14]{1,0:T(4,128)S(1)} %bitcast.15, bf16[1,4,64,64]{3,2,1,0:T(8,128)(2,1)S(1)} %copy-done.9, bf16[14,4,64,64]{3,2,1,0:T(8,128)(2,1)S(1)} %copy-done.5, bf16[12,64,64]{2,1,0:T(8,128)(2,1)S(1)} %copy-done.6, ...), custom_call_target="tpu_custom_call" | custom-call | flops 2000000000 | bytes 3000000 | tf_op jit(solution)/shard_map/weights/pallas_call | solution.py:273
  11.9 0.0 copy-start.10
  11.9 0.3 %collective-permute-done.1 = bf16[2,16,128]{2,1,0:T(8,128)(2,1)S(1)} collective-permute-done((bf16[2,16,128]{2,1,0:T(8,128)(2,1)S(1)}, bf16[2,16,128]{2,1,0:T(8,128)(2,1)S(1)}, u32[]{:S(2)}, u32[]{:S(2)}) %collective-permute-start.1) | collective-permute-done | bytes 8224 | tf_op jit(solution)/shard_map/ppermute | solution.py:296
  12.2 0.0 collective-permute-done.2.cross
  12.2 0.0 collective-permute-done.3.pair
  12.2 0.1 collective-permute-start.7
  12.3 0.8 %collective-permute-start.4 = (bf16[4,16,128]{2,1,0:T(8,128)(2,1)S(1)}, bf16[4,16,128]{2,1,0:T(8,128)(2,1)S(1)}, u32[]{:S(2)}, u32[]{:S(2)}) collective-permute-start(bf16[4,16,128]{2,1,0:T(8,128)(2,1)S(1)} %constant_dynamic-update-slice_fusion.2.rest_0_), channel_id=1, source_target_pairs={{0,2},{2,0},{4,6},{6,4},{8,10},{10,8},{12,14},{14,12},{16,18},{18,... | collective-permute-start | bytes 49160 | tf_op jit(solution)/shard_map/ppermute | solution.py:306
  13.2 1.1 %collective-permute-start.5 = (bf16[4,16,128]{2,1,0:T(8,128)(2,1)S(1)}, bf16[4,16,128]{2,1,0:T(8,128)(2,1)S(1)}, u32[]{:S(2)}, u32[]{:S(2)}) collective-permute-start(bf16[4,16,128]{2,1,0:T(8,128)(2,1)S(1)} %constant_dynamic-update-slice_fusion.2.rest_0_), channel_id=1, source_target_pairs={{0,6},{2,4},{4,2},{6,0},{8,14},{10,12},{12,10},{14,8},{16,22},{18,... | collective-permute-start | bytes 49160 | tf_op jit(solution)/shard_map/ppermute | solution.py:306
  14.2 1.7 %collective-permute-start.6 = (bf16[4,16,128]{2,1,0:T(8,128)(2,1)S(1)}, bf16[4,16,128]{2,1,0:T(8,128)(2,1)S(1)}, u32[]{:S(2)}, u32[]{:S(2)}) collective-permute-start(bf16[4,16,128]{2,1,0:T(8,128)(2,1)S(1)} %constant_dynamic-update-slice_fusion.2.rest_0_), channel_id=1, source_target_pairs={{0,4},{2,6},{4,0},{6,2},{8,12},{10,14},{12,8},{14,10},{16,20},{18,... | collective-permute-start | bytes 49160 | tf_op jit(solution)/shard_map/ppermute | solution.py:306
  15.9 0.0 collective-permute-done.7.all_other
  15.9 0.0 copy-done
  15.9 0.0 copy-done.1
  15.9 0.0 copy-done.3
  15.9 0.0 copy-done.4
  15.9 1.9 %fields.1 = (f32[8,16,256]{2,1,0:T(8,128)S(1)}, bf16[8,16,256]{2,1,0:T(8,128)(2,1)S(1)}) custom-call(s32[3,8]{1,0:T(4,128)S(1)} %bitcast.13, s32[3,8]{1,0:T(4,128)S(1)} %bitcast.14, bf16[20,16,128]{2,1,0:T(8,128)(2,1)S(1)} %collective-permute-done.3.pair, bf16[20,16,128]{2,1,0:T(8,128)(2,1)S(1)} %pack.1.own, ...), custom_call_target="tpu_custom_call" | custom-call | flops 805306368 | bytes 3145728 | tf_op jit(solution)/shard_map/fields/pallas_call | solution.py:252
  17.8 0.0 collective-permute-done.4.rest_1_
  17.8 0.0 collective-permute-done.5.rest_2_
  17.8 0.1 collective-permute-done.6.rest_3_
  18.0 0.0 collective-permute-start.8
  18.0 0.0 copy-done.10
  18.0 0.6 %down.1 = f32[8,16,256]{2,1,0:T(8,128)S(1)} custom-call(bf16[16,128,128]{2,1,0:T(8,128)(2,1)S(1)} %get-tuple-element.33.to_field, bf16[8,64,256]{2,1,0:T(8,128)(2,1)S(1)} %get-tuple-element.34.to_points, bf16[1,64,64]{2,1,0:T(8,128)(2,1)S(1)} %copy-done.10, f32[8,16,256]{2,1,0:T(8,128)S(1)} %get-tuple-element.42.keep, ...), custom_call_target="tpu_custom_call" | custom-call | flops 1000000000 | bytes 1000000 | tf_op jit(solution)/shard_map/down/pallas_call | solution.py:311
  18.6 0.6 %collective-permute-done.8 = bf16[8,16,256]{2,1,0:T(8,128)(2,1)S(1)} collective-permute-done((bf16[8,16,256]{2,1,0:T(8,128)(2,1)S(1)}, bf16[8,16,256]{2,1,0:T(8,128)(2,1)S(1)}, u32[]{:S(2)}, u32[]{:S(2)}) %collective-permute-start.8) | collective-permute-done | bytes 65568 | tf_op jit(solution)/shard_map/ppermute | solution.py:310
  19.2 0.6 %fusion = bf16[8,256,16]{1,2,0:T(8,128)(2,1)} fusion(f32[8,16,256]{2,1,0:T(8,128)S(1)} %down.1, bf16[8,16,256]{2,1,0:T(8,128)(2,1)S(1)} %collective-permute-done.8), kind=kLoop, calls=%fused_computation.2 | loop fusion | flops 98304 | bytes 262144 | tf_op jit(solution)/shard_map/transpose | solution.py:323
  (5 shorter events, 0.0 us)
Async XLA Ops:
  1.4 6.2 %collective-permute-start = (bf16[1,16,128]{2,1,0:T(8,128)(2,1)S(1)}, bf16[1,16,128]{2,1,0:T(8,128)(2,1)S(1)}, u32[]{:S(2)}, u32[]{:S(2)}) collective-permute-start(bf16[1,16,128]{2,1,0:T(8,128)(2,1)S(1)} %bitcast.11), channel_id=1, source_target_pairs={{0,8},{2,10},{4,12},{6,14},{8,0},{10,2},{12,4},{14,6},{16,24},{18,... | collective-permute-start | bytes 12296 | tf_op jit(solution)/shard_map/ppermute | solution.py:296
  4.4 5.8 %copy-start.2 = (bf16[8,256,64]{1,2,0:T(8,128)(2,1)S(1)}, bf16[8,256,64]{1,2,0:T(8,128)(2,1)}, u32[]{:S(2)}) copy-start(bf16[8,256,64]{1,2,0:T(8,128)(2,1)} %param.21) | copy-start | bytes 786436
  4.4 5.8 %copy-start.5 = (bf16[14,4,64,64]{3,2,1,0:T(8,128)(2,1)S(1)}, bf16[14,4,64,64]{3,2,1,0:T(8,128)(2,1)}, u32[]{:S(2)}) copy-start(bf16[14,4,64,64]{3,2,1,0:T(8,128)(2,1)} %upper_coup.1) | copy-start | bytes 1376260
  4.4 5.8 %copy-start.6 = (bf16[12,64,64]{2,1,0:T(8,128)(2,1)S(1)}, bf16[12,64,64]{2,1,0:T(8,128)(2,1)}, u32[]{:S(2)}) copy-start(bf16[12,64,64]{2,1,0:T(8,128)(2,1)} %upper_up.1) | copy-start | bytes 294916
  4.4 5.8 %copy-start.7 = (bf16[12,64,64]{2,1,0:T(8,128)(2,1)S(1)}, bf16[12,64,64]{2,1,0:T(8,128)(2,1)}, u32[]{:S(2)}) copy-start(bf16[12,64,64]{2,1,0:T(8,128)(2,1)} %upper_down.1) | copy-start | bytes 294916
  4.4 5.8 %copy-start.8 = (bf16[8,64,64]{2,1,0:T(8,128)(2,1)S(1)}, bf16[8,64,64]{2,1,0:T(8,128)(2,1)}, u32[]{:S(2)}) copy-start(bf16[8,64,64]{2,1,0:T(8,128)(2,1)} %leaf_down.1) | copy-start | bytes 196612
  4.5 5.8 %copy-start.9 = (bf16[1,4,64,64]{3,2,1,0:T(8,128)(2,1)S(1)}, bf16[1,4,64,64]{3,2,1,0:T(8,128)(2,1)}, u32[]{:S(2)}) copy-start(bf16[1,4,64,64]{3,2,1,0:T(8,128)(2,1)} %node_coup.1) | copy-start | bytes 98308
  4.5 5.8 %copy-start.11 = (s32[14,4]{0,1:T(4,128)S(1)}, s32[14,4]{0,1:T(4,128)}, u32[]{:S(2)}) copy-start(s32[14,4]{0,1:T(4,128)} %param.31) | copy-start | bytes 676
  4.5 5.8 %copy-start.12 = (s32[1,4]{1,0:T(1,128)S(1)}, s32[1,4]{1,0:T(1,128)}, u32[]{:S(2)}) copy-start(s32[1,4]{1,0:T(1,128)} %node_list.1) | copy-start | bytes 52
  4.6 7.6 %collective-permute-start.2 = (bf16[20,16,128]{2,1,0:T(8,128)(2,1)S(1)}, bf16[20,16,128]{2,1,0:T(8,128)(2,1)S(1)}, u32[]{:S(2)}, u32[]{:S(2)}) collective-permute-start(bf16[20,16,128]{2,1,0:T(8,128)(2,1)S(1)} %pack.1.own), channel_id=1, source_target_pairs={{2,4},{3,5},{4,2},{5,3},{6,8},{7,9},{8,6},{9,7},{10,12},{11,13},{1... | collective-permute-start | bytes 245768 | tf_op jit(solution)/shard_map/ppermute | solution.py:246
  4.6 7.6 %collective-permute-start.3 = (bf16[20,16,128]{2,1,0:T(8,128)(2,1)S(1)}, bf16[20,16,128]{2,1,0:T(8,128)(2,1)S(1)}, u32[]{:S(2)}, u32[]{:S(2)}) collective-permute-start(bf16[20,16,128]{2,1,0:T(8,128)(2,1)S(1)} %pack.1.own), channel_id=1, source_target_pairs={{0,2},{2,0},{4,6},{6,4},{8,10},{10,8},{12,14},{14,12},{16,18},{18,... | collective-permute-start | bytes 245768 | tf_op jit(solution)/shard_map/ppermute | solution.py:247
  7.6 4.6 %collective-permute-start.1 = (bf16[2,16,128]{2,1,0:T(8,128)(2,1)S(1)}, bf16[2,16,128]{2,1,0:T(8,128)(2,1)S(1)}, u32[]{:S(2)}, u32[]{:S(2)}) collective-permute-start(bf16[2,16,128]{2,1,0:T(8,128)(2,1)S(1)} %constant_dynamic-update-slice_fusion), channel_id=1, source_target_pairs={{0,16},{2,18},{4,20},{6,22},{8,24},{10,26},{12,28},{14,30},{16,0},... | collective-permute-start | bytes 24584 | tf_op jit(solution)/shard_map/ppermute | solution.py:296
  10.3 5.6 %copy-start = (bf16[8,3,256,256]{3,2,1,0:T(8,128)(2,1)S(1)}, bf16[8,3,256,256]{3,2,1,0:T(8,128)(2,1)}, u32[]{:S(2)}) copy-start(bf16[8,3,256,256]{3,2,1,0:T(8,128)(2,1)} %near.1) | copy-start | bytes 9437188
  10.3 5.6 %copy-start.1 = (bf16[8,3,64,64]{3,2,1,0:T(8,128)(2,1)S(1)}, bf16[8,3,64,64]{3,2,1,0:T(8,128)(2,1)}, u32[]{:S(2)}) copy-start(bf16[8,3,64,64]{3,2,1,0:T(8,128)(2,1)} %coup.1) | copy-start | bytes 589828
  10.3 5.6 %copy-start.3 = (s32[8,3]{0,1:T(4,128)S(1)}, s32[8,3]{0,1:T(4,128)}, u32[]{:S(2)}) copy-start(s32[8,3]{0,1:T(4,128)} %param.19) | copy-start | bytes 292
  10.3 5.6 %copy-start.4 = (s32[8,3]{0,1:T(4,128)S(1)}, s32[8,3]{0,1:T(4,128)}, u32[]{:S(2)}) copy-start(s32[8,3]{0,1:T(4,128)} %param.23) | copy-start | bytes 292
  11.9 6.1 %copy-start.10 = (bf16[1,64,64]{2,1,0:T(8,128)(2,1)S(1)}, bf16[1,64,64]{2,1,0:T(8,128)(2,1)}, u32[]{:S(2)}) copy-start(bf16[1,64,64]{2,1,0:T(8,128)(2,1)} %node_down.1) | copy-start | bytes 24580
  12.2 3.7 %collective-permute-start.7 = (bf16[60,16,128]{2,1,0:T(8,128)(2,1)S(1)}, bf16[60,16,128]{2,1,0:T(8,128)(2,1)S(1)}, u32[]{:S(2)}, u32[]{:S(2)}) collective-permute-start(bf16[60,16,128]{2,1,0:T(8,128)(2,1)S(1)} %pad_maximum_fusion), channel_id=1, source_target_pairs={{0,1},{1,0},{2,3},{3,2},{4,5},{5,4},{6,7},{7,6},{8,9},{9,8},{10,11... | collective-permute-start | bytes 737288 | tf_op jit(solution)/shard_map/ppermute | solution.py:304
  12.3 5.5 %collective-permute-start.4 = (bf16[4,16,128]{2,1,0:T(8,128)(2,1)S(1)}, bf16[4,16,128]{2,1,0:T(8,128)(2,1)S(1)}, u32[]{:S(2)}, u32[]{:S(2)}) collective-permute-start(bf16[4,16,128]{2,1,0:T(8,128)(2,1)S(1)} %constant_dynamic-update-slice_fusion.2.rest_0_), channel_id=1, source_target_pairs={{0,2},{2,0},{4,6},{6,4},{8,10},{10,8},{12,14},{14,12},{16,18},{18,... | collective-permute-start | bytes 49160 | tf_op jit(solution)/shard_map/ppermute | solution.py:306
  13.2 4.7 %collective-permute-start.5 = (bf16[4,16,128]{2,1,0:T(8,128)(2,1)S(1)}, bf16[4,16,128]{2,1,0:T(8,128)(2,1)S(1)}, u32[]{:S(2)}, u32[]{:S(2)}) collective-permute-start(bf16[4,16,128]{2,1,0:T(8,128)(2,1)S(1)} %constant_dynamic-update-slice_fusion.2.rest_0_), channel_id=1, source_target_pairs={{0,6},{2,4},{4,2},{6,0},{8,14},{10,12},{12,10},{14,8},{16,22},{18,... | collective-permute-start | bytes 49160 | tf_op jit(solution)/shard_map/ppermute | solution.py:306
  14.2 3.7 %collective-permute-start.6 = (bf16[4,16,128]{2,1,0:T(8,128)(2,1)S(1)}, bf16[4,16,128]{2,1,0:T(8,128)(2,1)S(1)}, u32[]{:S(2)}, u32[]{:S(2)}) collective-permute-start(bf16[4,16,128]{2,1,0:T(8,128)(2,1)S(1)} %constant_dynamic-update-slice_fusion.2.rest_0_), channel_id=1, source_target_pairs={{0,4},{2,6},{4,0},{6,2},{8,12},{10,14},{12,8},{14,10},{16,20},{18,... | collective-permute-start | bytes 49160 | tf_op jit(solution)/shard_map/ppermute | solution.py:306
  18.0 1.3 %collective-permute-start.8 = (bf16[8,16,256]{2,1,0:T(8,128)(2,1)S(1)}, bf16[8,16,256]{2,1,0:T(8,128)(2,1)S(1)}, u32[]{:S(2)}, u32[]{:S(2)}) collective-permute-start(bf16[8,16,256]{2,1,0:T(8,128)(2,1)S(1)} %get-tuple-element.46), channel_id=1, source_target_pairs={{0,1},{1,0},{2,3},{3,2},{4,5},{5,4},{6,7},{7,6},{8,9},{9,8},{10,11... | collective-permute-start | bytes 196616 | tf_op jit(solution)/shard_map/ppermute | solution.py:310
